TPU v7x, 32 devices: a whole 2x2x4 slice. The times are simulated.
32 devices in a mesh: section: 2 (over x), dp: 4 (over y, core), expert: 4 (over z).
Axes of the slice: x: 2, y: 2, z: 4, core: 2. Of those that a mesh axis runs over, the one named last changes fastest.
Arguments:
- inputs: bfloat16 [2, 4, 1024, 1024], P(None, 'dp', 'expert'), may hold values from -6 to 6
- cotangent: bfloat16 [2, 4, 1024, 1024], P(None, 'dp', 'expert'), may hold values from -6 to 6
- gain_attn: float32 [2, 1024], P('section'), may hold values from 0.5 to 1.5
- w_query: bfloat16 [2, 1024, 1024], P('section'), may hold values from -0.1875 to 0.1875
- w_key: bfloat16 [2, 1024, 512], P('section'), may hold values from -0.1875 to 0.1875
- w_value: bfloat16 [2, 1024, 512], P('section'), may hold values from -0.1875 to 0.1875
- w_out: bfloat16 [2, 1024, 1024], P('section'), may hold values from -0.75 to 0.75
- gain_moe: float32 [2, 1024], P('section'), may hold values from 0.5 to 1.5
- w_router: bfloat16 [2, 1024, 32], P('section'), may hold values from -0.09375 to 0.09375
- w_gate: bfloat16 [2, 32, 1024, 512], P('section', 'expert'), may hold values from -0.1875 to 0.1875
- w_up: bfloat16 [2, 32, 1024, 512], P('section', 'expert'), may hold values from -0.1875 to 0.1875
- w_down: bfloat16 [2, 32, 512, 1024], P('section', 'expert'), may hold values from -0.75 to 0.75
- doc_lengths: int32 [2, 4, 4], P(None, 'dp'), may hold values from 0 to 1024, as said below
- routes: int32 [2, 2, 4, 1024, 8], P('section', None, 'dp', 'expert'), may hold values from 0 to 31, all different within a row
Outputs:
- layer_outputs: bfloat16 [2, 2, 4, 1024, 1024], P('section', None, 'dp', 'expert')
- input_grads: bfloat16 [2, 2, 4, 1024, 1024], P('section', None, 'dp', 'expert')
- grad_gain_attn: float32 [2, 1024], P('section', ('dp', 'expert'))
- grad_query: float32 [2, 1024, 1024], P('section', ('dp', 'expert'))
- grad_key: float32 [2, 1024, 512], P('section', ('dp', 'expert'))
- grad_value: float32 [2, 1024, 512], P('section', ('dp', 'expert'))
- grad_out: float32 [2, 1024, 1024], P('section', ('dp', 'expert'))
- grad_gain_moe: float32 [2, 1024], P('section', ('dp', 'expert'))
- grad_router: float32 [2, 1024, 32], P('section', ('dp', 'expert'))
- grad_gate: float32 [2, 32, 1024, 512], P('section', 'expert', 'dp')
- grad_up: float32 [2, 32, 1024, 512], P('section', 'expert', 'dp')
- grad_down: float32 [2, 32, 512, 1024], P('section', 'expert', 'dp')
Inputs may be any that keep to these rules, and one draw needn't show every extreme that they name: `doc_lengths`: each sequence's lengths sum to 1024 or less; in every group of 4 sequences each sequence has one micro-batch in which a single document fills all 1024 positions, the other lengths being 0. `routes`: each token names 8 different experts.
All inputs are finite; a program needn't handle non-finite values.
Results may differ from a plain program's by a relative error of at most 0.023.
Values may be sent and summed in bfloat16 or wider, within the bound.
No kernel may reach another device: no remote copies, remote signals or barrier semaphores. Data moves between devices by JAX's collectives and lax.ppermute only.
A program may use at most 384 MiB of HBM per device.

v0:
```python
import jax
import jax.numpy as jnp
from jax import lax
from jax.sharding import PartitionSpec as P

HEADS = 16
KV_HEADS = 8
HEAD_DIM = 64
EXPERTS = 32
TOPK = 8
WINDOW = 512
NDOC = 4


epsilon = 1e-06
highest = lax.Precision.HIGHEST


def shifted(value, axis, steps):
    count = lax.axis_size(axis)
    initial, last = (max(0, -steps), min(count, count - steps))
    return lax.ppermute(value, axis, [(source, source + steps) for source in range(initial, last)])


def as_sent(shard):
    return jax.tree.map(lambda a: a.astype(jnp.bfloat16) if a.dtype == jnp.float32 else a, shard)


def rms_scale(values):
    return lax.rsqrt(jnp.mean(values * values, axis=-1, keepdims=True) + epsilon)


def rope_tables(positions):
    half_dim = HEAD_DIM // 2
    inverse = 10000.0 ** (-(jnp.arange(half_dim, dtype=jnp.float32) * (2.0 / HEAD_DIM)))
    angles = positions.astype(jnp.float32)[:, None] * inverse[None, :]
    return (jnp.cos(angles), jnp.sin(angles))


def rotate(vectors, cosine, sine):
    half_dim = HEAD_DIM // 2
    first = vectors[..., :half_dim]
    second = vectors[..., half_dim:]
    cosine = cosine[:, None, :]
    sine = sine[:, None, :]
    return jnp.concatenate(
        [first * cosine - second * sine, second * cosine + first * sine], axis=-1
    )


def unrotate(vectors, cosine, sine):
    half_dim = HEAD_DIM // 2
    first = vectors[..., :half_dim]
    second = vectors[..., half_dim:]
    cosine = cosine[:, None, :]
    sine = sine[:, None, :]
    return jnp.concatenate(
        [first * cosine + second * sine, second * cosine - first * sine], axis=-1
    )


def doc_ids(lengths, positions):
    endings = jnp.cumsum(lengths)
    return jnp.sum((positions[:, None] >= endings[None, :]).astype(jnp.int32), axis=1)


def slot_table(chosen, usable, capacity):
    experts_iota = jnp.arange(EXPERTS, dtype=jnp.int32)
    onehot = ((chosen[:, :, None] == experts_iota[None, None, :]) & usable[:, None, None]).astype(
        jnp.int32
    )
    flat_hot = onehot.reshape(-1, EXPERTS)
    ranking = jnp.cumsum(flat_hot, axis=0) - 1
    placed = jnp.sum(ranking * flat_hot, axis=1).reshape(chosen.shape)
    retained = usable[:, None] & (placed < capacity)
    slot_index = jnp.where(retained, chosen * capacity + placed, EXPERTS * capacity)
    return (slot_index, retained)


def layer_forward(hidden_in, weights, lengths, chosen, offset, ranks):
    gain_attn, w_query, w_key, w_value, w_out, gain_moe, w_router, w_gate, w_up, w_down = weights
    row_count, model_width = hidden_in.shape
    group_size = HEADS // KV_HEADS
    kv_width = KV_HEADS * HEAD_DIM
    capacity = row_count * TOPK // EXPERTS
    local_experts = EXPERTS // ranks
    positions = offset + jnp.arange(row_count, dtype=jnp.int32)
    documents = doc_ids(lengths, positions)
    cosine, sine = rope_tables(positions)
    scale_attn = rms_scale(hidden_in)
    normed = (hidden_in * scale_attn * gain_attn).astype(jnp.bfloat16)
    query = rotate(
        jnp.dot(normed, w_query, preferred_element_type=jnp.float32).reshape(
            row_count, HEADS, HEAD_DIM
        ),
        cosine,
        sine,
    ).astype(jnp.bfloat16)
    key_flat = (
        rotate(
            jnp.dot(normed, w_key, preferred_element_type=jnp.float32).reshape(
                row_count, KV_HEADS, HEAD_DIM
            ),
            cosine,
            sine,
        )
        .astype(jnp.bfloat16)
        .reshape(row_count, kv_width)
    )
    value_flat = jnp.dot(normed, w_value, preferred_element_type=jnp.float32).astype(jnp.bfloat16)
    reach = min((WINDOW - 1) // row_count + 1, ranks - 1)
    key_parts = [key_flat]
    value_parts = [value_flat]
    for lag_step in range(1, reach + 1):
        key_prev, value_prev = shifted((key_flat, value_flat), "expert", lag_step)
        key_parts.insert(0, key_prev)
        value_parts.insert(0, value_prev)
    key_rows = jnp.concatenate(key_parts, axis=0).reshape(-1, KV_HEADS, HEAD_DIM)
    value_rows = jnp.concatenate(value_parts, axis=0).reshape(-1, KV_HEADS, HEAD_DIM)
    key_places = offset - reach * row_count + jnp.arange((reach + 1) * row_count, dtype=jnp.int32)
    key_docs = doc_ids(lengths, key_places)
    distance = positions[:, None] - key_places[None, :]
    allowed = (
        (distance >= 0)
        & (distance < WINDOW)
        & (key_places[None, :] >= 0)
        & (documents[:, None] == key_docs[None, :])
    )
    grouped = query.reshape(row_count, KV_HEADS, group_size, HEAD_DIM)
    scores = jnp.einsum(
        "qhgd,khd->hgqk", grouped, key_rows, preferred_element_type=jnp.float32
    ) * HEAD_DIM ** (-0.5)
    scores = jnp.where(allowed[None, None], scores, -1e30)
    peak = jnp.max(scores, axis=-1, keepdims=True)
    expo = jnp.exp(scores - peak)
    totals = jnp.sum(expo, axis=-1, keepdims=True)
    probs = expo / totals
    log_total = peak + jnp.log(totals)
    mixed = jnp.einsum(
        "hgqk,khd->qhgd", probs.astype(jnp.bfloat16), value_rows, preferred_element_type=jnp.float32
    )
    mixed = mixed.reshape(row_count, model_width).astype(jnp.bfloat16)
    middle = hidden_in + jnp.dot(mixed, w_out, preferred_element_type=jnp.float32)
    scale_moe = rms_scale(middle)
    routed_in = (middle * scale_moe * gain_moe).astype(jnp.bfloat16)
    logits = jnp.dot(routed_in, w_router, preferred_element_type=jnp.float32)
    gates = jax.nn.softmax(jnp.take_along_axis(logits, chosen, axis=1), axis=-1)
    slot_index, retained = slot_table(chosen, documents < NDOC, capacity)
    buffer = jnp.zeros((EXPERTS * capacity + 1, model_width), jnp.bfloat16)
    buffer = buffer.at[slot_index.reshape(-1)].add(jnp.repeat(routed_in, TOPK, axis=0))[
        : EXPERTS * capacity
    ]
    buffer = buffer.reshape(ranks, local_experts, capacity, model_width)
    arrived = lax.all_to_all(buffer, "expert", split_axis=0, concat_axis=2, tiled=True)[0]
    gate_pre = jnp.einsum("ecd,edf->ecf", arrived, w_gate, preferred_element_type=jnp.float32)
    up_pre = jnp.einsum("ecd,edf->ecf", arrived, w_up, preferred_element_type=jnp.float32)
    activated = (jax.nn.silu(gate_pre) * up_pre).astype(jnp.bfloat16)
    produced = jnp.einsum(
        "ecf,efd->ecd", activated, w_down, preferred_element_type=jnp.float32
    ).astype(jnp.bfloat16)
    returned = lax.all_to_all(produced[None], "expert", split_axis=2, concat_axis=0, tiled=True)
    table = jnp.concatenate(
        [
            returned.reshape(EXPERTS * capacity, model_width),
            jnp.zeros((1, model_width), jnp.bfloat16),
        ],
        axis=0,
    )
    fetched = table[slot_index]
    weighting = gates * retained
    result = middle + jnp.sum(weighting[:, :, None] * fetched, axis=1)
    kept = (
        hidden_in,
        scale_attn,
        normed,
        cosine,
        sine,
        query,
        key_rows,
        value_rows,
        allowed,
        log_total,
        mixed,
        middle,
        scale_moe,
        routed_in,
        gates,
        slot_index,
        retained,
        chosen,
        arrived,
        gate_pre,
        up_pre,
        activated,
        fetched,
    )
    return (result, kept)


def layer_backward(grad_in, kept, weights, ranks):
    gain_attn, w_query, w_key, w_value, w_out, gain_moe, w_router, w_gate, w_up, w_down = weights
    (
        hidden_in,
        scale_attn,
        normed,
        cosine,
        sine,
        query,
        key_rows,
        value_rows,
        allowed,
        log_total,
        mixed,
        middle,
        scale_moe,
        routed_in,
        gates,
        slot_index,
        retained,
        chosen,
        arrived,
        gate_pre,
        up_pre,
        activated,
        fetched,
    ) = kept
    row_count, model_width = hidden_in.shape
    group_size = HEADS // KV_HEADS
    kv_width = KV_HEADS * HEAD_DIM
    capacity = row_count * TOPK // EXPERTS
    local_experts = EXPERTS // ranks
    weighting = gates * retained
    d_gates = jnp.sum(grad_in[:, None, :] * fetched, axis=2) * retained
    pair_grads = (weighting[:, :, None] * grad_in[:, None, :]).reshape(-1, model_width)
    d_table = jnp.zeros((EXPERTS * capacity + 1, model_width), jnp.float32)
    d_table = (
        d_table.at[slot_index.reshape(-1)]
        .add(pair_grads)[: EXPERTS * capacity]
        .astype(jnp.bfloat16)
    )
    d_produced = lax.all_to_all(
        d_table.reshape(ranks, local_experts, capacity, model_width),
        "expert",
        split_axis=0,
        concat_axis=2,
        tiled=True,
    )[0]
    d_activated = jnp.einsum("ecd,efd->ecf", d_produced, w_down, preferred_element_type=jnp.float32)
    grad_down = jnp.einsum(
        "ecf,ecd->efd", activated, d_produced, preferred_element_type=jnp.float32
    )
    sigma = jax.nn.sigmoid(gate_pre)
    d_gate_pre = (d_activated * up_pre * sigma * (1.0 + gate_pre * (1.0 - sigma))).astype(
        jnp.bfloat16
    )
    d_up_pre = (d_activated * gate_pre * sigma).astype(jnp.bfloat16)
    grad_gate = jnp.einsum("ecd,ecf->edf", arrived, d_gate_pre, preferred_element_type=jnp.float32)
    grad_up = jnp.einsum("ecd,ecf->edf", arrived, d_up_pre, preferred_element_type=jnp.float32)
    d_rows = jnp.einsum("ecf,edf->ecd", d_gate_pre, w_gate, preferred_element_type=jnp.float32)
    d_rows = (
        d_rows + jnp.einsum("ecf,edf->ecd", d_up_pre, w_up, preferred_element_type=jnp.float32)
    ).astype(jnp.bfloat16)
    d_back = lax.all_to_all(d_rows[None], "expert", split_axis=2, concat_axis=0, tiled=True)
    d_back = jnp.concatenate(
        [
            d_back.reshape(EXPERTS * capacity, model_width),
            jnp.zeros((1, model_width), jnp.bfloat16),
        ],
        axis=0,
    )
    d_routed = jnp.sum(d_back[slot_index].astype(jnp.float32), axis=1)
    d_picked = gates * (d_gates - jnp.sum(gates * d_gates, axis=1, keepdims=True))
    experts_iota = jnp.arange(EXPERTS, dtype=jnp.int32)
    d_logits = jnp.sum(
        d_picked[:, :, None] * (chosen[:, :, None] == experts_iota[None, None, :]), axis=1
    )
    router_wide = w_router.astype(jnp.float32)
    d_routed = d_routed + jnp.dot(d_logits, router_wide.T, precision=highest)
    grad_router = jnp.dot(routed_in.astype(jnp.float32).T, d_logits, precision=highest)
    normal_moe = middle * scale_moe
    grad_gain_moe = jnp.sum(d_routed * normal_moe, axis=0)
    d_norm_moe = d_routed * gain_moe
    d_middle = grad_in + scale_moe * (
        d_norm_moe - normal_moe * jnp.mean(d_norm_moe * normal_moe, axis=1, keepdims=True)
    )
    d_branch = d_middle.astype(jnp.bfloat16)
    grad_out = jnp.einsum("td,te->de", mixed, d_branch, preferred_element_type=jnp.float32)
    d_mixed = jnp.einsum("te,de->td", d_branch, w_out, preferred_element_type=jnp.float32).astype(
        jnp.bfloat16
    )
    d_mixed = d_mixed.reshape(row_count, KV_HEADS, group_size, HEAD_DIM)
    grouped = query.reshape(row_count, KV_HEADS, group_size, HEAD_DIM)
    scale = HEAD_DIM ** (-0.5)
    scores = (
        jnp.einsum("qhgd,khd->hgqk", grouped, key_rows, preferred_element_type=jnp.float32) * scale
    )
    scores = jnp.where(allowed[None, None], scores, -1e30)
    probs = jnp.exp(scores - log_total)
    d_values = jnp.einsum(
        "hgqk,qhgd->khd", probs.astype(jnp.bfloat16), d_mixed, preferred_element_type=jnp.float32
    )
    d_probs = jnp.einsum("qhgd,khd->hgqk", d_mixed, value_rows, preferred_element_type=jnp.float32)
    d_scores = (probs * (d_probs - jnp.sum(probs * d_probs, axis=-1, keepdims=True))).astype(
        jnp.bfloat16
    ) * scale
    d_query = jnp.einsum(
        "hgqk,khd->qhgd", d_scores, key_rows, preferred_element_type=jnp.float32
    ).reshape(row_count, HEADS, HEAD_DIM)
    d_keys = jnp.einsum(
        "hgqk,qhgd->khd", d_scores, grouped, preferred_element_type=jnp.float32
    ).reshape(-1, kv_width)
    d_values = d_values.reshape(-1, kv_width)
    reach = d_keys.shape[0] // row_count - 1
    d_key_own = d_keys[reach * row_count :]
    d_value_own = d_values[reach * row_count :]
    for lag_step in range(1, reach + 1):
        begin = (reach - lag_step) * row_count
        key_home, value_home = (
            shifted(
                d_keys[begin : begin + row_count].astype(jnp.bfloat16), "expert", -lag_step
            ).astype(jnp.float32),
            shifted(
                d_values[begin : begin + row_count].astype(jnp.bfloat16), "expert", -lag_step
            ).astype(jnp.float32),
        )
        d_key_own = d_key_own + key_home
        d_value_own = d_value_own + value_home
    d_query_pre = (
        unrotate(d_query, cosine, sine).reshape(row_count, model_width).astype(jnp.bfloat16)
    )
    d_key_pre = (
        unrotate(d_key_own.reshape(row_count, KV_HEADS, HEAD_DIM), cosine, sine)
        .reshape(row_count, kv_width)
        .astype(jnp.bfloat16)
    )
    d_value_pre = d_value_own.astype(jnp.bfloat16)
    grad_query = jnp.einsum("td,te->de", normed, d_query_pre, preferred_element_type=jnp.float32)
    grad_key = jnp.einsum("td,te->de", normed, d_key_pre, preferred_element_type=jnp.float32)
    grad_value = jnp.einsum("td,te->de", normed, d_value_pre, preferred_element_type=jnp.float32)
    d_normed = jnp.einsum("te,de->td", d_query_pre, w_query, preferred_element_type=jnp.float32)
    d_normed = d_normed + jnp.einsum(
        "te,de->td", d_key_pre, w_key, preferred_element_type=jnp.float32
    )
    d_normed = d_normed + jnp.einsum(
        "te,de->td", d_value_pre, w_value, preferred_element_type=jnp.float32
    )
    normal_attn = hidden_in * scale_attn
    grad_gain_attn = jnp.sum(d_normed * normal_attn, axis=0)
    d_norm_attn = d_normed * gain_attn
    d_hidden = d_middle + scale_attn * (
        d_norm_attn - normal_attn * jnp.mean(d_norm_attn * normal_attn, axis=1, keepdims=True)
    )
    dense = (grad_gain_attn, grad_query, grad_key, grad_value, grad_out, grad_gain_moe, grad_router)
    expert_side = (grad_gate, grad_up, grad_down)
    return (d_hidden, dense, expert_side)


def per_device(
    inputs,
    cotangent,
    gain_attn,
    w_query,
    w_key,
    w_value,
    w_out,
    gain_moe,
    w_router,
    w_gate,
    w_up,
    w_down,
    doc_lengths,
    routes,
):
    micro_count = inputs.shape[0]
    row_count = inputs.shape[2]
    model_width = inputs.shape[3]
    ranks = lax.axis_size("expert")
    last_section = lax.axis_size("section") - 1
    section_index = lax.axis_index("section")
    offset = lax.axis_index("expert") * row_count
    weights = (
        gain_attn[0],
        w_query[0],
        w_key[0],
        w_value[0],
        w_out[0],
        gain_moe[0],
        w_router[0],
        w_gate[0],
        w_up[0],
        w_down[0],
    )
    tick_count = micro_count + last_section
    received = jnp.zeros((row_count, model_width), jnp.bfloat16)
    outputs = jnp.zeros((micro_count, row_count, model_width), jnp.bfloat16)
    kept_ticks = []
    for tick_step in range(tick_count):
        batch_index = tick_step - section_index
        active = (batch_index >= 0) & (batch_index < micro_count)
        safe_index = jnp.clip(batch_index, 0, micro_count - 1)
        first_input = lax.dynamic_index_in_dim(inputs[:, 0], safe_index, 0, False)
        current = jnp.where(section_index == 0, first_input, received).astype(jnp.float32)
        lengths = lax.dynamic_index_in_dim(doc_lengths[:, 0], safe_index, 0, False)
        chosen = lax.dynamic_index_in_dim(routes[0, :, 0], safe_index, 0, False)
        result, kept = layer_forward(current, weights, lengths, chosen, offset, ranks)
        sent = result.astype(jnp.bfloat16)
        outputs = jnp.where(
            active, lax.dynamic_update_index_in_dim(outputs, sent, safe_index, 0), outputs
        )
        kept_ticks.append(kept)
        if tick_step + 1 < tick_count:
            received = shifted(sent, "section", 1)
    kept_all = jax.tree.map(lambda *pieces: jnp.stack(pieces), *kept_ticks)
    back_in = jnp.zeros((row_count, model_width), jnp.bfloat16)
    input_grads = jnp.zeros((micro_count, row_count, model_width), jnp.bfloat16)
    dense_total = None
    expert_total = None
    for tick_step in range(tick_count):
        batch_index = micro_count - 1 - tick_step + (last_section - section_index)
        active = (batch_index >= 0) & (batch_index < micro_count)
        safe_index = jnp.clip(batch_index, 0, micro_count - 1)
        kept = jax.tree.map(
            lambda stacked: lax.dynamic_index_in_dim(stacked, safe_index + section_index, 0, False),
            kept_all,
        )
        top_grad = lax.dynamic_index_in_dim(cotangent[:, 0], safe_index, 0, False)
        incoming = jnp.where(section_index == last_section, top_grad, back_in).astype(jnp.float32)
        d_hidden, dense, expert_side = layer_backward(incoming, kept, weights, ranks)
        factor = active.astype(jnp.float32)
        sent_back = d_hidden.astype(jnp.bfloat16)
        input_grads = jnp.where(
            active,
            lax.dynamic_update_index_in_dim(input_grads, sent_back, safe_index, 0),
            input_grads,
        )
        if tick_step == 0:
            dense_total = tuple((g * factor for g in dense))
            expert_total = tuple((g * factor for g in expert_side))
        else:
            dense_total = tuple((a + factor * b for a, b in zip(dense_total, dense)))
            expert_total = tuple((a + factor * b for a, b in zip(expert_total, expert_side)))
        if tick_step + 1 < tick_count:
            back_in = shifted(sent_back, "section", -1)
    dense_total = lax.psum_scatter(dense_total, ("dp", "expert"), scatter_dimension=0, tiled=True)
    expert_total = jax.tree.map(
        lambda part: part.astype(jnp.float32),
        lax.psum_scatter(as_sent(expert_total), "dp", scatter_dimension=1, tiled=True),
    )
    return (
        outputs[None, :, None],
        input_grads[None, :, None],
        dense_total[0][None],
        dense_total[1][None],
        dense_total[2][None],
        dense_total[3][None],
        dense_total[4][None],
        dense_total[5][None],
        dense_total[6][None],
        expert_total[0][None],
        expert_total[1][None],
        expert_total[2][None],
    )


def solution(mesh):
    placed = (
        P(None, "dp", "expert", None),
        P(None, "dp", "expert", None),
        P("section", None),
        P("section", None, None),
        P("section", None, None),
        P("section", None, None),
        P("section", None, None),
        P("section", None),
        P("section", None, None),
        P("section", "expert", None, None),
        P("section", "expert", None, None),
        P("section", "expert", None, None),
        P(None, "dp", None),
        P("section", None, "dp", "expert", None),
    )
    return jax.shard_map(
        per_device,
        mesh=mesh,
        in_specs=placed,
        out_specs=(
            P("section", None, "dp", "expert", None),
            P("section", None, "dp", "expert", None),
            P("section", ("dp", "expert")),
            P("section", ("dp", "expert"), None),
            P("section", ("dp", "expert"), None),
            P("section", ("dp", "expert"), None),
            P("section", ("dp", "expert"), None),
            P("section", ("dp", "expert")),
            P("section", ("dp", "expert"), None),
            P("section", "expert", "dp", None),
            P("section", "expert", "dp", None),
            P("section", "expert", "dp", None),
        ),
        check_vma=False,
    )
```

profile of v0, /device:TPU:0, one launch (start us, length us, event | category | flops | bytes accessed | tf_op | source)
XLA Modules:
  0.0 2496.3 jit_solution(1770356350808113210)
XLA Ops:
  89.3 30.7 %scatter_custom_fusion = bf16[2049,1024]{1,0:T(8,128)(2,1)} fusion(s32[2048]{0:T(1024)S(1)} %bitcast.1630, bf16[]{:T(256)} %constant.331.clone.1, bf16[256,1024]{1,0:T(8,128)(2,1)} %multiply_convert_fusion.6), kind=kCustom, calls=%fused_computation.199 | custom fusion | flops 2097152 | bytes 4720642 | tf_op jit(solution)/shard_map/scatter-add | solution.py:150
  122.2 95.7 %all_to_all.189 = bf16[4,8,64,1024]{3,2,1,0:T(8,128)(2,1)S(1)} all-to-all(bf16[4,8,64,1024]{3,2,1,0:T(8,128)(2,1)S(1)} %bitcast.1458), channel_id=1, replica_groups=mesh['section'=2,'dp'=4,'expert'=4] {'expert'}, dimensions={0} | all-to-all | bytes 8388608 | tf_op jit(solution)/shard_map/all_to_all | solution.py:154
  252.9 16.8 gather_fusion.6
  272.5 66.7 %all-to-all-done.1 = bf16[1,8,256,1024]{3,1,0,2:T(8,128)(2,1)} async-done(((bf16[1,8,256,1024]{3,1,0,2:T(8,128)(2,1)}), bf16[1,8,256,1024]{3,1,0,2:T(8,128)(2,1)}, u32[]{:S(2)}, u32[]{:S(2)}) %all-to-all-start.1) | async-done | bytes 4194336 | tf_op jit(solution)/shard_map/all_to_all | solution.py:161
  346.2 13.7 gather_fusion
  414.9 20.9 scatter_custom_fusion.1
  438.0 106.0 %all_to_all.190 = bf16[4,8,64,1024]{3,2,1,0:T(8,128)(2,1)S(1)} all-to-all(bf16[4,8,64,1024]{3,2,1,0:T(8,128)(2,1)S(1)} %bitcast.1459), channel_id=1, replica_groups=mesh['section'=2,'dp'=4,'expert'=4] {'expert'}, dimensions={0} | all-to-all | bytes 8388608 | tf_op jit(solution)/shard_map/all_to_all | solution.py:154
  585.5 17.7 reduce-window.61
  619.9 16.8 gather_fusion.7
  639.5 25.5 %all-to-all-done.3 = bf16[1,8,256,1024]{3,1,0,2:T(8,128)(2,1)} async-done(((bf16[1,8,256,1024]{3,1,0,2:T(8,128)(2,1)}), bf16[1,8,256,1024]{3,1,0,2:T(8,128)(2,1)}, u32[]{:S(2)}, u32[]{:S(2)}) %all-to-all-start.3) | async-done | bytes 4194336 | tf_op jit(solution)/shard_map/all_to_all | solution.py:161
  672.0 13.7 gather_fusion.1
  745.8 20.9 scatter_custom_fusion.2
  771.4 15.9 all-to-all-start.4
  800.0 16.8 gather_fusion.8
  819.0 22.3 scatter_custom_fusion.3
  847.5 30.2 %all-to-all-done.4 = bf16[4,8,64,1024]{3,2,1,0:T(8,128)(2,1)} async-done(((bf16[4,8,64,1024]{3,2,1,0:T(8,128)(2,1)}), bf16[4,8,64,1024]{3,2,1,0:T(8,128)(2,1)}, u32[]{:S(2)}, u32[]{:S(2)}) %all-to-all-start.4) | async-done | bytes 4194336 | tf_op jit(solution)/shard_map/all_to_all | solution.py:154
  911.0 64.2 %all-to-all-done.6 = bf16[4,8,64,1024]{3,2,1,0:T(8,128)(2,1)} async-done(((bf16[4,8,64,1024]{3,2,1,0:T(8,128)(2,1)}), bf16[4,8,64,1024]{3,2,1,0:T(8,128)(2,1)}, u32[]{:S(2)}, u32[]{:S(2)}) %all-to-all-start.6) | async-done | bytes 4194336 | tf_op jit(solution)/shard_map/all_to_all | solution.py:241
  1008.5 12.7 fusion.123
  1048.6 24.2 all-to-all-done.5
  1113.7 56.7 %all-to-all-done.7 = bf16[1,8,256,1024]{3,1,0,2:T(8,128)(2,1)} async-done(((bf16[1,8,256,1024]{3,1,0,2:T(8,128)(2,1)}), bf16[1,8,256,1024]{3,1,0,2:T(8,128)(2,1)}, u32[]{:S(2)}, u32[]{:S(2)}) %all-to-all-start.7) | async-done | bytes 4194336 | tf_op jit(solution)/shard_map/all_to_all | solution.py:263
  1177.3 14.0 gather_fusion.3
  1199.5 13.7 gather_fusion.2
  1240.2 20.7 fusion.159
  1260.8 21.2 fusion.533
  1328.3 13.1 collective-permute-done.18
  1343.7 22.3 scatter_custom_fusion.4
  1370.2 100.3 %all_to_all.191 = bf16[4,8,64,1024]{3,2,1,0:T(8,128)(2,1)S(1)} all-to-all(bf16[4,8,64,1024]{3,2,1,0:T(8,128)(2,1)S(1)} %bitcast.1472), channel_id=1, replica_groups=mesh['section'=2,'dp'=4,'expert'=4] {'expert'}, dimensions={0} | all-to-all | bytes 8388608 | tf_op jit(solution)/shard_map/all_to_all | solution.py:241
  1472.9 12.6 fusion.114
  1532.6 77.6 %all-to-all-done.9 = bf16[1,8,256,1024]{3,1,0,2:T(8,128)(2,1)} async-done(((bf16[1,8,256,1024]{3,1,0,2:T(8,128)(2,1)}), bf16[1,8,256,1024]{3,1,0,2:T(8,128)(2,1)}, u32[]{:S(2)}, u32[]{:S(2)}) %all-to-all-start.9) | async-done | bytes 4194336 | tf_op jit(solution)/shard_map/all_to_all | solution.py:263
  1617.2 13.8 gather_fusion.4
  1651.0 20.4 fusion.162
  1671.4 21.6 fusion.535
  1735.8 13.7 collective-permute-done.23
  1750.7 22.1 scatter_custom_fusion.5
  1824.4 57.2 %all-to-all-done.10 = bf16[4,8,64,1024]{3,2,1,0:T(8,128)(2,1)} async-done(((bf16[4,8,64,1024]{3,2,1,0:T(8,128)(2,1)}), bf16[4,8,64,1024]{3,2,1,0:T(8,128)(2,1)}, u32[]{:S(2)}, u32[]{:S(2)}) %all-to-all-start.10) | async-done | bytes 4194336 | tf_op jit(solution)/shard_map/all_to_all | solution.py:241
  1886.5 12.7 fusion.105
  1899.3 18.1 add_convert_fusion.2
  1917.5 14.2 fusion.96
  1942.8 18.4 add_convert_fusion.1
  1982.8 19.1 add_convert_fusion
  2049.4 80.6 %all-to-all-done.11 = bf16[1,8,256,1024]{3,1,0,2:T(8,128)(2,1)} async-done(((bf16[1,8,256,1024]{3,1,0,2:T(8,128)(2,1)}), bf16[1,8,256,1024]{3,1,0,2:T(8,128)(2,1)}, u32[]{:S(2)}, u32[]{:S(2)}) %all-to-all-start.11) | async-done | bytes 4194336 | tf_op jit(solution)/shard_map/all_to_all | solution.py:263
  2136.9 14.0 gather_fusion.5
  2167.6 21.2 fusion.537
  2221.3 14.5 collective-permute-done.27
  2245.6 19.7 fusion.165
  2299.0 35.2 %all-reduce.8 = (f32[1024]{0:T(1024)S(1)}, f32[1024]{0:T(1024)S(1)}) all-reduce(f32[1024]{0:T(1024)S(1)} %multiply_add_fusion.11, f32[1024]{0:T(1024)S(1)} %multiply_add_fusion.10), channel_id=2, replica_groups=mesh['section'=2,'dp'=4,'expert'=4] {'dp','expert'}, use_global_device_ids=true, to_apply=%region_69.71.clone | all-reduce | flops 2048 | bytes 16384
  2350.8 61.7 %reduce-scatter.11.cloned.1.call-done = f32[64,1024]{1,0:T(8,128)} async-done(((f32[1024,1024]{1,0:T(8,128)}), f32[64,1024]{1,0:T(8,128)}) %reduce-scatter.11.cloned.1.call-update) | async-done | bytes 262160 | tf_op jit(solution)/shard_map/reduce_scatter | solution.py:444
  2412.6 76.7 %reduce-scatter.17.cloned.1.call-done = f32[64,1024]{1,0:T(8,128)} async-done(((f32[1024,1024]{1,0:T(8,128)}), f32[64,1024]{1,0:T(8,128)}) %reduce-scatter.17.cloned.1.call-update) | async-done | bytes 262160 | tf_op jit(solution)/shard_map/reduce_scatter | solution.py:444
  (1070 shorter events, 938.1 us)
Async XLA Ops:
  11.3 63.0 %collective-permute-start.1 = (bf16[256,512]{1,0:T(8,128)(2,1)}, bf16[256,512]{1,0:T(8,128)(2,1)}, u32[]{:S(2)}, u32[]{:S(2)}) collective-permute-start(bf16[256,512]{1,0:T(8,128)(2,1)} %convolution_convert_fusion.2), channel_id=1, source_target_pairs={{0,1},{1,2},{2,3},{4,5},{5,6},{6,7},{8,9},{9,10},{10,11},{12,13},{... | collective-permute-start | bytes 786440 | tf_op jit(solution)/shard_map/ppermute | solution.py:22
  17.0 57.2 %collective-permute-start = (bf16[256,512]{1,0:T(8,128)(2,1)}, bf16[256,512]{1,0:T(8,128)(2,1)}, u32[]{:S(2)}, u32[]{:S(2)}) collective-permute-start(bf16[256,512]{1,0:T(8,128)(2,1)} %convolution_convert_fusion.2), channel_id=1, source_target_pairs={{0,2},{1,3},{4,6},{5,7},{8,10},{9,11},{12,14},{13,15},{16,18},{17,... | collective-permute-start | bytes 786440 | tf_op jit(solution)/shard_map/ppermute | solution.py:22
  25.8 697.1 %copy-start.75 = (f32[256,32]{0,1:T(8,128)}, f32[256,32]{0,1:T(8,128)S(1)}, u32[]{:S(2)}) copy-start(f32[256,32]{0,1:T(8,128)S(1)} %get-tuple-element.214) | copy-start | bytes 98308
  25.8 697.1 %copy-start.78 = (f32[256,32]{0,1:T(8,128)}, f32[256,32]{0,1:T(8,128)S(1)}, u32[]{:S(2)}) copy-start(f32[256,32]{0,1:T(8,128)S(1)} %get-tuple-element.215) | copy-start | bytes 98308
  26.7 51.0 %collective-permute-start.3 = (bf16[256,512]{0,1:T(8,128)(2,1)}, bf16[256,512]{0,1:T(8,128)(2,1)}, u32[]{:S(2)}, u32[]{:S(2)}) collective-permute-start(bf16[256,512]{0,1:T(8,128)(2,1)} %bitcast.13), channel_id=1, source_target_pairs={{0,1},{1,2},{2,3},{4,5},{5,6},{6,7},{8,9},{9,10},{10,11},{12,13},{... | collective-permute-start | bytes 786440 | tf_op jit(solution)/shard_map/ppermute | solution.py:22
  28.7 49.0 %collective-permute-start.2 = (bf16[256,512]{0,1:T(8,128)(2,1)}, bf16[256,512]{0,1:T(8,128)(2,1)}, u32[]{:S(2)}, u32[]{:S(2)}) collective-permute-start(bf16[256,512]{0,1:T(8,128)(2,1)} %bitcast.13), channel_id=1, source_target_pairs={{0,2},{1,3},{4,6},{5,7},{8,10},{9,11},{12,14},{13,15},{16,18},{17,... | collective-permute-start | bytes 786440 | tf_op jit(solution)/shard_map/ppermute | solution.py:22
  36.1 578.2 %copy-start.70 = (s32[1,1,1,256,8]{4,3,2,1,0:T(8,128)}, s32[1,1,1,256,8]{4,3,2,1,0:T(8,128)S(1)}, u32[]{:S(2)}) copy-start(s32[1,1,1,256,8]{4,3,2,1,0:T(8,128)S(1)} %copy.440) | copy-start | bytes 24580
  241.6 97.7 %all-to-all-start.1 = ((bf16[1,8,256,1024]{3,1,0,2:T(8,128)(2,1)}), bf16[1,8,256,1024]{3,1,0,2:T(8,128)(2,1)}, u32[]{:S(2)}, u32[]{:S(2)}) async-start(bf16[1,8,256,1024]{3,1,0,2:T(8,128)(2,1)} %copy.313), calls=%async_computation.1 | async-start | bytes 8388608 | tf_op jit(solution)/shard_map/all_to_all | solution.py:161
  365.2 14.0 collective-permute-start.4
  381.2 12.4 collective-permute-start.6
  382.5 12.3 collective-permute-start.5
  388.5 12.0 collective-permute-start.8
  390.5 13.0 collective-permute-start.7
  568.0 97.0 %all-to-all-start.3 = ((bf16[1,8,256,1024]{3,1,0,2:T(8,128)(2,1)}), bf16[1,8,256,1024]{3,1,0,2:T(8,128)(2,1)}, u32[]{:S(2)}, u32[]{:S(2)}) async-start(bf16[1,8,256,1024]{3,1,0,2:T(8,128)(2,1)} %copy.323), calls=%async_computation.3 | async-start | bytes 8388608 | tf_op jit(solution)/shard_map/all_to_all | solution.py:161
  692.8 15.1 collective-permute-start.9
  711.9 11.2 collective-permute-start.11
  713.2 12.3 collective-permute-start.10
  718.6 12.7 collective-permute-start.13
  720.8 13.5 collective-permute-start.12
  771.4 106.2 %all-to-all-start.4 = ((bf16[4,8,64,1024]{3,2,1,0:T(8,128)(2,1)}), bf16[4,8,64,1024]{3,2,1,0:T(8,128)(2,1)}, u32[]{:S(2)}, u32[]{:S(2)}) async-start(bf16[4,8,64,1024]{3,2,1,0:T(8,128)(2,1)} %bitcast.1462), calls=%async_computation.4 | async-start | bytes 8388608 | tf_op jit(solution)/shard_map/all_to_all | solution.py:154
  877.6 97.6 %all-to-all-start.6 = ((bf16[4,8,64,1024]{3,2,1,0:T(8,128)(2,1)}), bf16[4,8,64,1024]{3,2,1,0:T(8,128)(2,1)}, u32[]{:S(2)}, u32[]{:S(2)}) async-start(bf16[4,8,64,1024]{3,2,1,0:T(8,128)(2,1)} %bitcast.1464), calls=%async_computation.6 | async-start | bytes 8388608 | tf_op jit(solution)/shard_map/all_to_all | solution.py:241
  975.3 97.5 %all-to-all-start.5 = ((bf16[1,8,256,1024]{3,1,0,2:T(8,128)(2,1)}), bf16[1,8,256,1024]{3,1,0,2:T(8,128)(2,1)}, u32[]{:S(2)}, u32[]{:S(2)}) async-start(bf16[1,8,256,1024]{3,1,0,2:T(8,128)(2,1)} %copy.333), calls=%async_computation.5 | async-start | bytes 8388608 | tf_op jit(solution)/shard_map/all_to_all | solution.py:161
  1072.8 97.6 %all-to-all-start.7 = ((bf16[1,8,256,1024]{3,1,0,2:T(8,128)(2,1)}), bf16[1,8,256,1024]{3,1,0,2:T(8,128)(2,1)}, u32[]{:S(2)}, u32[]{:S(2)}) async-start(bf16[1,8,256,1024]{3,1,0,2:T(8,128)(2,1)} %copy.348), calls=%async_computation.7 | async-start | bytes 8388608 | tf_op jit(solution)/shard_map/all_to_all | solution.py:263
  1289.9 15.3 collective-permute-start.15
  1291.2 16.7 collective-permute-start.14
  1292.6 27.2 %collective-permute-start.17 = (bf16[256,512]{0,1:T(8,128)(2,1)S(1)}, bf16[256,512]{0,1:T(8,128)(2,1)S(1)}, u32[]{:S(2)}, u32[]{:S(2)}) collective-permute-start(bf16[256,512]{0,1:T(8,128)(2,1)S(1)} %bitcast.1571), channel_id=1, source_target_pairs={{2,0},{3,1},{6,4},{7,5},{10,8},{11,9},{14,12},{15,13},{18,16},{19,... | collective-permute-start | bytes 786440 | tf_op jit(solution)/shard_map/ppermute | solution.py:22
  1294.1 25.8 %collective-permute-start.16 = (bf16[256,512]{0,1:T(8,128)(2,1)S(1)}, bf16[256,512]{0,1:T(8,128)(2,1)S(1)}, u32[]{:S(2)}, u32[]{:S(2)}) collective-permute-start(bf16[256,512]{0,1:T(8,128)(2,1)S(1)} %bitcast.1569), channel_id=1, source_target_pairs={{1,0},{2,1},{3,2},{5,4},{6,5},{7,6},{9,8},{10,9},{11,10},{13,12},{... | collective-permute-start | bytes 786440 | tf_op jit(solution)/shard_map/ppermute | solution.py:22
  1325.2 16.2 collective-permute-start.18
  1512.7 97.6 %all-to-all-start.9 = ((bf16[1,8,256,1024]{3,1,0,2:T(8,128)(2,1)}), bf16[1,8,256,1024]{3,1,0,2:T(8,128)(2,1)}, u32[]{:S(2)}, u32[]{:S(2)}) async-start(bf16[1,8,256,1024]{3,1,0,2:T(8,128)(2,1)} %copy.367), calls=%async_computation.9 | async-start | bytes 8388608 | tf_op jit(solution)/shard_map/all_to_all | solution.py:263
  1701.0 15.1 collective-permute-start.20
  1702.3 16.7 collective-permute-start.19
  1703.7 27.1 %collective-permute-start.22 = (bf16[256,512]{0,1:T(8,128)(2,1)S(1)}, bf16[256,512]{0,1:T(8,128)(2,1)S(1)}, u32[]{:S(2)}, u32[]{:S(2)}) collective-permute-start(bf16[256,512]{0,1:T(8,128)(2,1)S(1)} %bitcast.1572), channel_id=1, source_target_pairs={{2,0},{3,1},{6,4},{7,5},{10,8},{11,9},{14,12},{15,13},{18,16},{19,... | collective-permute-start | bytes 786440 | tf_op jit(solution)/shard_map/ppermute | solution.py:22
  1705.0 25.8 %collective-permute-start.21 = (bf16[256,512]{0,1:T(8,128)(2,1)S(1)}, bf16[256,512]{0,1:T(8,128)(2,1)S(1)}, u32[]{:S(2)}, u32[]{:S(2)}) collective-permute-start(bf16[256,512]{0,1:T(8,128)(2,1)S(1)} %bitcast.1570), channel_id=1, source_target_pairs={{1,0},{2,1},{3,2},{5,4},{6,5},{7,6},{9,8},{10,9},{11,10},{13,12},{... | collective-permute-start | bytes 786440 | tf_op jit(solution)/shard_map/ppermute | solution.py:22
  1733.7 15.7 collective-permute-start.23
  1779.1 102.5 %all-to-all-start.10 = ((bf16[4,8,64,1024]{3,2,1,0:T(8,128)(2,1)}), bf16[4,8,64,1024]{3,2,1,0:T(8,128)(2,1)}, u32[]{:S(2)}, u32[]{:S(2)}) async-start(bf16[4,8,64,1024]{3,2,1,0:T(8,128)(2,1)} %bitcast.1463), calls=%async_computation.10 | async-start | bytes 8388608 | tf_op jit(solution)/shard_map/all_to_all | solution.py:241
  1786.7 503.8 %reduce-scatter.25.cloned.1.call-start = ((), (), s32[]{:S(2)}) async-start(), calls=%async_computation.27 | async-start | bytes 557056
  1824.4 513.9 %reduce-scatter.19.cloned.1.call-start = ((), (), s32[]{:S(2)}) async-start(), calls=%async_computation.24 | async-start | bytes 10485760 | tf_op jit(solution)/shard_map/reduce_scatter | solution.py:447
  1917.4 425.0 %reduce-scatter.21.cloned.1.call-start = ((), (), s32[]{:S(2)}) async-start(), calls=%async_computation.25 | async-start | bytes 10485760 | tf_op jit(solution)/shard_map/reduce_scatter | solution.py:447
  1961.2 385.4 %reduce-scatter.23.cloned.1.call-start = ((), (), s32[]{:S(2)}) async-start(), calls=%async_computation.26 | async-start | bytes 10485760 | tf_op jit(solution)/shard_map/reduce_scatter | solution.py:447
  2031.7 98.3 %all-to-all-start.11 = ((bf16[1,8,256,1024]{3,1,0,2:T(8,128)(2,1)}), bf16[1,8,256,1024]{3,1,0,2:T(8,128)(2,1)}, u32[]{:S(2)}, u32[]{:S(2)}) async-start(bf16[1,8,256,1024]{3,1,0,2:T(8,128)(2,1)} %copy.380), calls=%async_computation.11 | async-start | bytes 8388608 | tf_op jit(solution)/shard_map/all_to_all | solution.py:263
  2036.7 314.1 %reduce-scatter.13.cloned.1.call-start = ((), (), s32[]{:S(2)}) async-start(), calls=%async_computation.21 | async-start | bytes 2228224 | tf_op jit(solution)/shard_map/reduce_scatter | solution.py:444
  2190.0 13.6 collective-permute-start.25
  2191.3 14.7 collective-permute-start.24
  2210.0 140.9 %reduce-scatter.15.cloned.1.call-start = ((), (), s32[]{:S(2)}) async-start(), calls=%async_computation.22 | async-start | bytes 2228224 | tf_op jit(solution)/shard_map/reduce_scatter | solution.py:444
  2218.2 17.7 collective-permute-start.27
  2219.5 16.4 collective-permute-start.26
  2237.9 174.7 %reduce-scatter.11.cloned.1.call-start = ((), (), s32[]{:S(2)}) async-start(), calls=%async_computation.20 | async-start | bytes 4456448 | tf_op jit(solution)/shard_map/reduce_scatter | solution.py:444
  2273.1 216.2 %reduce-scatter.17.cloned.1.call-start = ((), (), s32[]{:S(2)}) async-start(), calls=%async_computation.23 | async-start | bytes 4456448 | tf_op jit(solution)/shard_map/reduce_scatter | solution.py:444
  (274 other events, 4113.3 us)
Sparse Core Ops, SparseCore 0:
  1824.5 75.4 reduce-scatter.24
  1917.5 71.8 reduce-scatter.18
  1992.1 71.6 reduce-scatter.20
  2066.4 71.6 reduce-scatter.22
  2210.1 61.4 reduce-scatter.12
  2276.2 60.5 reduce-scatter.14
  2341.2 71.2 reduce-scatter.10
  2417.5 71.7 reduce-scatter.16
where the time goes:
time: 2500 us
  waiting for transfers between devices  753 us (30%)
  matrix products  548 us (22%)
  other arithmetic  367 us (15%)
  local copies, waits for them, and re-layouts  352 us (14%)
  blocking collectives  337 us (13%)
  starting transfers between devices  119 us (5%)
    all_to_all x3, waiting for transfers between devices, layer_backward(): lax.all_to_all(d_rows[None], 'expert', split_axis=2, concat_axis=0, tiled...  215 us
    all_to_all x2, blocking collectives, layer_forward(): lax.all_to_all(buffer, 'expert', split_axis=0, concat_axis=2, tiled=True)[0]  202 us
    reduce_scatter x4, waiting for transfers between devices, per_device(): lax.psum_scatter(dense_total, ('dp', 'expert'), scatter_dimension=0, tile...  138 us
    ppermute x28, waiting for transfers between devices, shifted(): lax.ppermute(value, axis, [(source, source + steps) for source in range(i...  131 us
    all_to_all x2, waiting for transfers between devices, layer_backward(): lax.all_to_all(d_table.reshape(ranks, local_experts, capacity, model_widt...  121 us
    all_to_all x3, waiting for transfers between devices, layer_forward(): lax.all_to_all(produced[None], 'expert', split_axis=2, concat_axis=0, til...  116 us
    all_to_all x1, blocking collectives, layer_backward(): lax.all_to_all(d_table.reshape(ranks, local_experts, capacity, model_widt...  100 us
    scatter-add x3, other arithmetic, layer_forward(): buffer.at[slot_index.reshape(-1)].add(jnp.repeat(routed_in, TOPK, axis=0))  72.5 us
  transfers between devices with their start and end apart: 45, of which 30 were waited for; matrix products, arithmetic and copies ran while one was open for 29% of the time, Pallas kernels for 0%

commit v1 on v0

v1 whole, which is shorter than its diff:
```python
import functools

import jax
import jax.numpy as jnp
from jax import lax
from jax.experimental import pallas as pl
from jax.experimental.pallas import tpu as pltpu
from jax.sharding import PartitionSpec as P

HEADS = 16
KV_HEADS = 8
HEAD_DIM = 64
EXPERTS = 32
TOPK = 8
WINDOW = 512
NDOC = 4
EPSILON = 1e-06
MASKED = -1e30
LANES = 128
VMEM_BYTES = 56 * 1024 * 1024
bf16 = jnp.bfloat16
f32 = jnp.float32


def shifted(value, axis, steps, sources=None):
    count = lax.axis_size(axis)
    initial, last = (max(0, -steps), min(count, count - steps))
    names = range(initial, last) if sources is None else sources
    return lax.ppermute(value, axis, [(source, source + steps) for source in names])


def swapped(value, axis, bit):
    count = lax.axis_size(axis)
    return lax.ppermute(value, axis, [(source, source ^ bit) for source in range(count)])


def line_gather(block):
    ups, downs = [], []
    up, down = block, block
    for _ in range(lax.axis_size("expert") - 1):
        up = shifted(up, "expert", 1)
        down = shifted(down, "expert", -1)
        ups.append(up)
        downs.append(down)
    return ups, downs


def line_reduce(parts):
    ranks = lax.axis_size("expert")
    me = lax.axis_index("expert")

    def pick(index):
        return lax.dynamic_index_in_dim(parts, jnp.clip(index, 0, ranks - 1), 0, False)

    up = down = None
    for step in range(1, ranks):
        up_part = pick(me + ranks - step)
        down_part = pick(me - ranks + step)
        up = up_part if up is None else (up.astype(f32) + up_part.astype(f32)).astype(bf16)
        down = down_part if down is None else (down.astype(f32) + down_part.astype(f32)).astype(bf16)
        up = shifted(up, "expert", 1, range(0, step))
        down = shifted(down, "expert", -1, range(ranks - step, ranks))
    return pick(me).astype(f32) + up.astype(f32) + down.astype(f32)


def dp_bits():
    bits, bit = [], 1
    while bit < lax.axis_size("dp"):
        bits.append(bit)
        bit *= 2
    return bits


def fetch_pieces(piece):
    pieces = {0: swapped(piece, "section", 1)}
    for bit in reversed(dp_bits()):
        for k in list(pieces):
            pieces[k | bit] = swapped(pieces[k], "dp", bit)
    return [pieces[k] for k in range(len(pieces))]


def dp_reduce(keep, send):
    for bit in dp_bits():
        total = (keep.astype(f32) + swapped(send, "dp", bit).astype(f32)).astype(bf16)
        if total.shape[0] > 1:
            keep, send = total[0::2], total[1::2]
    return total[0]


def to_owner(value, layer):
    return lax.ppermute(value, "section", [(1 - layer, layer)])


def call(kernel, out_shape, in_specs, out_specs, scratch, grid=None, flops=0, bytes_accessed=0, name=None):
    extra = {} if grid is None else {"grid": grid}
    return pl.pallas_call(
        kernel,
        out_shape=out_shape,
        in_specs=in_specs,
        out_specs=out_specs,
        scratch_shapes=scratch,
        compiler_params=pltpu.CompilerParams(vmem_limit_bytes=VMEM_BYTES),
        cost_estimate=pl.CostEstimate(flops=flops, bytes_accessed=bytes_accessed, transcendentals=0),
        name=name,
        **extra,
    )


SMEM = pl.BlockSpec(memory_space=pltpu.SMEM)
VMEM = pl.BlockSpec(memory_space=pltpu.VMEM)
ANY = pl.BlockSpec(memory_space=pl.ANY)


def struct(shape, dtype):
    return jax.ShapeDtypeStruct(shape, dtype)


def dot(left, right, left_dim=1, right_dim=0):
    return lax.dot_general(left, right, (((left_dim,), (right_dim,)), ((), ())), preferred_element_type=f32)


def upper_lanes(shape):
    return lax.broadcasted_iota(jnp.int32, shape, 1) % LANES >= HEAD_DIM


def half_swap(tile):
    lane = lax.broadcasted_iota(jnp.int32, tile.shape, 1)
    half = HEAD_DIM // 2
    return jnp.where(
        lane % HEAD_DIM < half, pltpu.roll(tile, LANES - half, 1), pltpu.roll(tile, half, 1)
    )


def load_dense(info, owns, pieces, first, width, target, sem):
    rows = target.shape[0] // len(pieces)

    @pl.when(info[0] == 1)
    def _():
        start = 0
        for own in owns:
            size = own.shape[1]
            pltpu.make_async_copy(own, target.at[:, pl.ds(start, size)], sem).start()
            start += size

    @pl.when(info[0] == 0)
    def _():
        for k, piece in enumerate(pieces):
            place = pl.multiple_of((info[1] ^ k) * rows, rows)
            pltpu.make_async_copy(
                piece.at[:, pl.ds(first, width)], target.at[pl.ds(place, rows), :], sem
            ).start()


def wait_dense(target, sem):
    pltpu.make_async_copy(target, target, sem).wait()


def load_experts(info, owns, chunks, expert, slot, buffers, sems):
    gate_buf, up_buf, down_buf = buffers
    per_chunk = chunks[0][0].shape[0]
    pieces = len(chunks[0])
    wide = gate_buf.shape[1] // pieces
    narrow = down_buf.shape[1] // pieces
    half = down_buf.shape[2] // 2

    @pl.when(info[0] == 1)
    def _():
        for own, buf, index in zip(owns, buffers, range(3)):
            pltpu.make_async_copy(own.at[expert], buf.at[slot], sems.at[slot, index]).start()

    for c, chunk in enumerate(chunks):

        @pl.when((info[0] == 0) & (expert // per_chunk == c))
        def _():
            local = expert - c * per_chunk
            for k, piece in enumerate(chunk):
                owner = info[1] ^ k
                row = pl.multiple_of(owner * wide, wide)
                low = pl.multiple_of(owner * narrow, narrow)
                pltpu.make_async_copy(
                    piece.at[local, pl.ds(0, wide)], gate_buf.at[slot, pl.ds(row, wide)], sems.at[slot, 0]
                ).start()
                pltpu.make_async_copy(
                    piece.at[local, pl.ds(wide, wide)], up_buf.at[slot, pl.ds(row, wide)], sems.at[slot, 1]
                ).start()
                for side in range(2):
                    pltpu.make_async_copy(
                        piece.at[local, pl.ds(2 * wide + side * narrow, narrow)],
                        down_buf.at[slot, pl.ds(low, narrow), pl.ds(side * half, half)],
                        sems.at[slot, 2],
                    ).start()


def wait_experts(slot, index, buffers, sems):
    pltpu.make_async_copy(buffers[index].at[slot], buffers[index].at[slot], sems.at[slot, index]).wait()


def load_line(info, own, ups, downs, target, sem):
    ranks = target.shape[0]
    me = info[2]
    pltpu.make_async_copy(own, target.at[me], sem).start()
    for s in range(1, ranks):

        @pl.when(me >= s)
        def _():
            pltpu.make_async_copy(ups[s - 1], target.at[me - s], sem).start()

        @pl.when(me < s)
        def _():
            pltpu.make_async_copy(downs[ranks - s - 1], target.at[me - s + ranks], sem).start()


def wait_line(target, sem):
    pltpu.make_async_copy(target, target, sem).wait()


def write_pieces(info, value, keep, send, place):
    pieces = 2 * keep.shape[0]
    rows = value.shape[0] // pieces
    for p in range(pieces):
        k = info[1] ^ p
        part = value[p * rows : (p + 1) * rows].astype(keep.dtype)

        @pl.when(k % 2 == 0)
        def _():
            keep[(k // 2,) + place] = part

        @pl.when(k % 2 == 1)
        def _():
            send[(k // 2,) + place] = part


def rms(values):
    return lax.rsqrt(jnp.mean(values * values, axis=-1, keepdims=True) + EPSILON)


def mask_bias(info, query_docs, key_docs, bias):
    rows, keys = bias.shape
    row = lax.broadcasted_iota(jnp.int32, (rows, keys), 0)
    col = lax.broadcasted_iota(jnp.int32, (rows, keys), 1)
    distance = row + (keys - rows) - col
    allowed = (distance >= 0) & (distance < WINDOW) & (query_docs[...] == key_docs[...])
    bias[...] = jnp.where(allowed, 0.0, MASKED)


def load_keys(own, earlier, target, sem):
    rows = own.shape[0]
    reach = len(earlier)
    pltpu.make_async_copy(own, target.at[pl.ds(reach * rows, rows)], sem).start()
    for s, part in enumerate(earlier):
        pltpu.make_async_copy(part, target.at[pl.ds((reach - 1 - s) * rows, rows)], sem).start()


def doubled(pair, which):
    wide = pair.astype(f32)
    turned = pltpu.roll(wide, HEAD_DIM, 1)
    upper = upper_lanes(wide.shape)
    picked = jnp.where(upper, turned, wide) if which == 0 else jnp.where(upper, wide, turned)
    return picked.astype(bf16)


def one_head(tile, which, upper):
    return jnp.where(upper, tile, 0.0) if which == 1 else jnp.where(upper, 0.0, tile)


def project_kernel(pieces, info, x, gain, cosine, sine, w_query, w_key, w_value, *rest):
    parts = rest[:pieces]
    query, keyval, weights, sem = rest[pieces:]
    width = weights.shape[1]
    load_dense(info, (w_query, w_key, w_value), parts, 0, width, weights, sem)
    hidden = x[...].astype(f32)
    normed = (hidden * rms(hidden) * gain[...]).astype(bf16)
    wait_dense(weights, sem)
    q_width, k_width = w_query.shape[1], w_key.shape[1]
    cos, sin = cosine[...], sine[...]
    step = 2 * LANES
    for begin in range(0, width, step):
        product = dot(normed, weights[:, begin : begin + step])
        for inner in range(0, step, LANES):
            tile = product[:, inner : inner + LANES]
            place = begin + inner
            if place < q_width + k_width:
                tile = tile * cos + half_swap(tile) * sin
            if place < q_width:
                query[:, place : place + LANES] = tile.astype(bf16)
            else:
                place -= q_width
                keyval[:, place : place + LANES] = tile.astype(bf16)


def attend_kernel(pieces, reach, info, query, own_kv, *rest):
    earlier = rest[:reach]
    query_docs, key_docs, x, gain, w_out = rest[reach : reach + 5]
    parts = rest[reach + 5 : reach + 5 + pieces]
    mixed, log_total, middle, routed = rest[reach + 5 + pieces : reach + 9 + pieces]
    keyval, bias, weights, kv_sem, w_sem = rest[reach + 9 + pieces :]
    load_keys(own_kv, earlier, keyval, kv_sem)
    first = 2 * x.shape[1]
    load_dense(info, (w_out,), parts, first, x.shape[1], weights, w_sem)
    mask_bias(info, query_docs, key_docs, bias)
    log_total[...] = jnp.zeros_like(log_total)
    pltpu.make_async_copy(keyval, keyval, kv_sem).wait()
    kv_width = KV_HEADS * HEAD_DIM
    rows = query.shape[0]
    upper = upper_lanes((rows, LANES))
    lane = lax.broadcasted_iota(jnp.int32, (rows, LANES), 1)

    @pl.loop(0, KV_HEADS // 2)
    def _(pair):
        k_pair = keyval[:, pl.ds(pl.multiple_of(pair * LANES, LANES), LANES)]
        v_pair = keyval[:, pl.ds(pl.multiple_of(kv_width + pair * LANES, LANES), LANES)]
        for head in range(2):
            keys, values = doubled(k_pair, head), doubled(v_pair, head)
            place = pl.multiple_of((pair * 2 + head) * LANES, LANES)
            tile = query[:, pl.ds(place, LANES)].astype(f32) * HEAD_DIM ** (-0.5)
            results = []
            for g in range(2):
                scores = dot(one_head(tile, g, upper).astype(bf16), keys, 1, 1) + bias[...]
                peak = jnp.max(scores, axis=1, keepdims=True)
                expo = jnp.exp(scores - peak)
                total = jnp.sum(expo, axis=1, keepdims=True)
                results.append(dot(expo.astype(bf16), values) * (1.0 / total))
                index = (pair * 2 + head) * 2 + g
                log_total[...] = jnp.where(lane == index, peak + jnp.log(total), log_total[...])
            mixed[:, pl.ds(place, LANES)] = jnp.where(upper, results[1], results[0]).astype(bf16)

    wait_dense(weights, w_sem)
    between = x[...].astype(f32) + dot(mixed[...], weights[...])
    middle[...] = between
    routed[...] = (between * rms(between) * gain[...]).astype(bf16)


def attend_back_kernel(pieces, reach, info, d_routed, grad, middle, gain, mixed, query, log_total, own_kv, *rest):
    earlier = rest[:reach]
    query_docs, key_docs, cosine, sine, w_out = rest[reach : reach + 5]
    rest = rest[reach + 5 :]
    parts = rest[:pieces]
    rest = rest[pieces:]
    d_middle, d_query, d_own = rest[:3]
    d_earlier = rest[3 : 3 + reach]
    keep, send, grad_gain = rest[3 + reach : 6 + reach]
    keyval, bias, weights, d_mixed, d_kv, kv_sem, w_sem = rest[6 + reach :]
    load_keys(own_kv, earlier, keyval, kv_sem)
    first = 2 * middle.shape[1]
    load_dense(info, (w_out,), parts, first, middle.shape[1], weights, w_sem)
    mask_bias(info, query_docs, key_docs, bias)
    between = middle[...]
    scale = rms(between)
    normal = between * scale
    routed = d_routed[...]
    grad_gain[...] = jnp.sum(routed * normal, axis=0, keepdims=True)
    d_norm = routed * gain[...]
    total = grad[...].astype(f32) + scale * (
        d_norm - normal * jnp.mean(d_norm * normal, axis=1, keepdims=True)
    )
    d_middle[...] = total
    branch = total.astype(bf16)
    wait_dense(weights, w_sem)
    d_mixed[...] = dot(branch, weights[...], 1, 1).astype(bf16)
    write_pieces(info, dot(mixed[...], branch, 0, 0), keep, send, ())
    pltpu.make_async_copy(keyval, keyval, kv_sem).wait()
    kv_width = KV_HEADS * HEAD_DIM
    rows = query.shape[0]
    upper = upper_lanes((rows, LANES))
    lane = lax.broadcasted_iota(jnp.int32, (rows, LANES), 1)
    cos, sin = cosine[...], sine[...]

    @pl.loop(0, KV_HEADS // 2)
    def _(pair):
        k_pair = keyval[:, pl.ds(pl.multiple_of(pair * LANES, LANES), LANES)]
        v_pair = keyval[:, pl.ds(pl.multiple_of(kv_width + pair * LANES, LANES), LANES)]
        for head in range(2):
            keys, values = doubled(k_pair, head), doubled(v_pair, head)
            place = pl.multiple_of((pair * 2 + head) * LANES, LANES)
            tile = query[:, pl.ds(place, LANES)].astype(f32) * HEAD_DIM ** (-0.5)
            d_tile = d_mixed[:, pl.ds(place, LANES)].astype(f32)
            inner = d_tile * mixed[:, pl.ds(place, LANES)].astype(f32)
            dq, dk, dv = [], None, None
            for g in range(2):
                index = (pair * 2 + head) * 2 + g
                log_column = jnp.sum(jnp.where(lane == index, log_total[...], 0.0), axis=1, keepdims=True)
                weight = jnp.sum(one_head(inner, g, upper), axis=1, keepdims=True)
                own_query = one_head(tile, g, upper).astype(bf16)
                own_grad = one_head(d_tile, g, upper).astype(bf16)
                scores = dot(own_query, keys, 1, 1) + bias[...]
                probs = jnp.exp(scores - log_column)
                d_probs = dot(own_grad, values, 1, 1)
                d_scores = (probs * (d_probs - weight)).astype(bf16)
                dq.append(dot(d_scores, keys))
                k_term = dot(own_query, d_scores, 0, 0)
                v_term = dot(own_grad, probs.astype(bf16), 0, 0)
                dk = k_term if dk is None else dk + k_term
                dv = v_term if dv is None else dv + v_term
            whole = jnp.where(upper, dq[1], dq[0]) * HEAD_DIM ** (-0.5)
            whole = whole * cos - half_swap(whole) * sin
            d_query[:, pl.ds(place, LANES)] = whole.astype(bf16)
            k_row = pl.multiple_of((pair * 2 + head) * HEAD_DIM, HEAD_DIM)
            v_row = pl.multiple_of(kv_width + (pair * 2 + head) * HEAD_DIM, HEAD_DIM)
            d_kv[pl.ds(k_row, HEAD_DIM), :] = dk[:HEAD_DIM] + dk[HEAD_DIM:]
            d_kv[pl.ds(v_row, HEAD_DIM), :] = dv[:HEAD_DIM] + dv[HEAD_DIM:]

    for block in range(reach + 1):
        turned = d_kv[:, block * rows : (block + 1) * rows].T
        if block == reach:
            d_own[...] = turned
        else:
            d_earlier[reach - 1 - block][...] = turned.astype(bf16)


def query_back_kernel(pieces, info, x, gain, d_query, w_query, *rest):
    parts = rest[:pieces]
    d_normed, keep, send, weights, sem = rest[pieces:]
    load_dense(info, (w_query,), parts, 0, weights.shape[1], weights, sem)
    hidden = x[...].astype(f32)
    normed = (hidden * rms(hidden) * gain[...]).astype(bf16)
    write_pieces(info, dot(normed, d_query[...], 0, 0), keep, send, ())
    wait_dense(weights, sem)
    d_normed[...] = dot(d_query[...], weights[...], 1, 1)


def keyval_back_kernel(pieces, info, x, gain, d_own, d_others, d_normed, d_middle, cosine, sine, w_key, w_value, *rest):
    parts = rest[:pieces]
    d_x, keep, send, grad_gain, weights, d_pre, sem = rest[pieces:]
    load_dense(info, (w_key, w_value), parts, x.shape[1], weights.shape[1], weights, sem)
    hidden = x[...].astype(f32)
    scale = rms(hidden)
    normal = hidden * scale
    normed = (normal * gain[...]).astype(bf16)
    cos, sin = cosine[...], sine[...]
    width = w_key.shape[1]
    for place in range(0, 2 * width, LANES):
        tile = d_own[:, place : place + LANES] + d_others[:, place : place + LANES].astype(f32)
        if place < width:
            tile = tile * cos - half_swap(tile) * sin
        d_pre[:, place : place + LANES] = tile.astype(bf16)
    wait_dense(weights, sem)
    total = d_normed[...] + dot(d_pre[...], weights[...], 1, 1)
    grad_gain[...] = jnp.sum(total * normal, axis=0, keepdims=True)
    d_norm = total * gain[...]
    d_x[...] = (
        d_middle[...]
        + scale * (d_norm - normal * jnp.mean(d_norm * normal, axis=1, keepdims=True))
    ).astype(bf16)
    write_pieces(info, dot(normed, d_pre[...], 0, 0), keep, send, ())


def slot_rows(info, table, local, experts_here):
    row = lax.broadcasted_iota(jnp.int32, table.shape, 0)
    picked = jnp.where(row == info[2] * experts_here + local, table, 0.0)
    return jnp.sum(picked, axis=0, keepdims=True)


def slot_hits(codes, capacity):
    slot = lax.broadcasted_iota(jnp.int32, (capacity, codes.shape[1]), 0).astype(f32)
    return slot == codes


def experts_kernel(pieces, ranks, chunk_count, info, own, *rest):
    ups, downs = rest[: ranks - 1], rest[ranks - 1 : 2 * ranks - 2]
    rest = rest[2 * ranks - 2 :]
    routes, usable, router, w_gate, w_up, w_down = rest[:6]
    rest = rest[6:]
    chunks = [rest[c * pieces : (c + 1) * pieces] for c in range(chunk_count)]
    rest = rest[chunk_count * pieces :]
    sums, everyone, rows, gates, codes, gate_out, up_out = rest[:7]
    hits, results, gate_buf, up_buf, down_buf, sems, line_sem = rest[7:]
    expert, count = pl.program_id(0), pl.num_programs(0)
    buffers = (gate_buf, up_buf, down_buf)
    owns = (w_gate, w_up, w_down)
    experts_here = w_gate.shape[0]
    tokens = own.shape[0]
    capacity = tokens * TOPK // EXPERTS
    slot = expert % 2

    @pl.when(expert == 0)
    def _():
        load_line(info, own, ups, downs, everyone, line_sem)
        load_experts(info, owns, chunks, 0, 0, buffers, sems)
        earlier = lax.broadcasted_iota(jnp.int32, (tokens, tokens), 0)
        later = lax.broadcasted_iota(jnp.int32, (tokens, tokens), 1)
        triangle = jnp.where(earlier < later, 1.0, 0.0).astype(bf16)
        number = lax.broadcasted_iota(jnp.int32, (EXPERTS, tokens), 0)
        wait_line(everyone, line_sem)
        for block in range(ranks):
            span = slice(block * tokens, (block + 1) * tokens)
            named = routes[0:1, span] == number
            for k in range(1, TOPK):
                named = named | (routes[k : k + 1, span] == number)
            logits = jnp.where(named, dot(router[...], everyone[block], 1, 1), MASKED)
            expo = jnp.where(named, jnp.exp(logits - jnp.max(logits, axis=0, keepdims=True)), 0.0)
            weight = expo / jnp.sum(expo, axis=0, keepdims=True)
            held = named & (usable[:, span] > 0)
            rank = dot(jnp.where(held, 1.0, 0.0).astype(bf16), triangle)
            code = jnp.where(held & (rank < capacity), rank, -1.0)
            gates[block] = weight
            codes[block] = code
            for e in range(experts_here):
                hit = slot_hits(slot_rows(info, code, e, experts_here), capacity)
                hits[block, e * capacity : (e + 1) * capacity, :] = jnp.where(hit, 1.0, 0.0).astype(bf16)
            rows[block] = dot(hits[block], everyone[block]).astype(bf16)

    @pl.when(expert + 1 < count)
    def _():
        load_experts(info, owns, chunks, expert + 1, 1 - slot, buffers, sems)

    place = pl.multiple_of(expert * capacity, capacity)
    mine = jnp.concatenate([rows[block, pl.ds(place, capacity), :] for block in range(ranks)], axis=0)
    wait_experts(slot, 0, buffers, sems)
    gate_pre = dot(mine, gate_buf[slot])
    wait_experts(slot, 1, buffers, sems)
    up_pre = dot(mine, up_buf[slot])
    gate_out[0] = gate_pre.astype(bf16)
    up_out[0] = up_pre.astype(bf16)
    activated = (gate_pre * jax.nn.sigmoid(gate_pre) * up_pre).astype(bf16)
    wait_experts(slot, 2, buffers, sems)
    produced = dot(activated, down_buf[slot]).astype(bf16)
    for block in range(ranks):
        results[block, pl.ds(place, capacity), :] = produced[block * capacity : (block + 1) * capacity]

    @pl.when(expert + 1 == count)
    def _():
        for block in range(ranks):
            weighted = []
            for e in range(experts_here):
                weight = slot_rows(info, gates[block], e, experts_here)
                hit = hits[block, e * capacity : (e + 1) * capacity, :].astype(f32)
                weighted.append((hit * weight).astype(bf16))
            sums[block] = dot(jnp.concatenate(weighted, axis=0), results[block], 0, 0).astype(bf16)


def experts_back_kernel(pieces, ranks, chunk_count, info, own, *rest):
    ups, downs = rest[: ranks - 1], rest[ranks - 1 : 2 * ranks - 2]
    rest = rest[2 * ranks - 2 :]
    everyone, gates, codes, router, gate_pre, up_pre, w_gate, w_up, w_down = rest[:9]
    rest = rest[9:]
    chunks = [rest[c * pieces : (c + 1) * pieces] for c in range(chunk_count)]
    rest = rest[chunk_count * pieces :]
    sums, grad_router, grad_rows, gate_out, up_out, active_out = rest[:6]
    incoming, hits, columns, d_gates, d_rows, gate_buf, up_buf, down_buf, sems, line_sem = rest[6:]
    expert, count = pl.program_id(0), pl.num_programs(0)
    buffers = (gate_buf, up_buf, down_buf)
    owns = (w_gate, w_up, w_down)
    experts_here = w_gate.shape[0]
    tokens = own.shape[0]
    capacity = tokens * TOPK // EXPERTS
    slot = expert % 2

    @pl.when(expert == 0)
    def _():
        load_line(info, own, ups, downs, incoming, line_sem)
        load_experts(info, owns, chunks, 0, 0, buffers, sems)
        for block in range(ranks):
            for e in range(experts_here):
                hit = slot_hits(slot_rows(info, codes[block], e, experts_here), capacity)
                span = slice(e * capacity, (e + 1) * capacity)
                hits[block, span, :] = jnp.where(hit, 1.0, 0.0).astype(bf16)
                weight = slot_rows(info, gates[block], e, experts_here)
                column = jnp.sum(jnp.where(hit, weight, 0.0), axis=1, keepdims=True)
                columns[block, span, :] = jnp.broadcast_to(column, (capacity, LANES))
        wait_line(incoming, line_sem)
        for block in range(ranks):
            grad_rows[block] = dot(hits[block], incoming[block]).astype(bf16)

    @pl.when(expert + 1 < count)
    def _():
        load_experts(info, owns, chunks, expert + 1, 1 - slot, buffers, sems)

    place = pl.multiple_of(expert * capacity, capacity)
    mine = jnp.concatenate([grad_rows[block, pl.ds(place, capacity), :] for block in range(ranks)], axis=0)
    weight = jnp.concatenate(
        [columns[block, pl.ds(place, capacity), :] for block in range(ranks)], axis=0
    )[:, :1]
    gate = gate_pre[0].astype(f32)
    up = up_pre[0].astype(f32)
    sigma = jax.nn.sigmoid(gate)
    silu = gate * sigma
    activated = silu * up
    wait_experts(slot, 2, buffers, sems)
    unweighted = dot(mine, down_buf[slot], 1, 1)
    d_weight = jnp.sum(unweighted * activated, axis=1, keepdims=True)
    for block in range(ranks):
        hit = hits[block, pl.ds(place, capacity), :].astype(f32)
        spread = hit * d_weight[block * capacity : (block + 1) * capacity]
        d_gates[block, pl.ds(expert, 1), :] = jnp.sum(spread, axis=0, keepdims=True)
    d_active = unweighted * weight
    active_out[0] = (activated * weight).astype(bf16)
    d_gate = (d_active * up * sigma * (1.0 + gate * (1.0 - sigma))).astype(bf16)
    d_up = (d_active * silu).astype(bf16)
    gate_out[0] = d_gate
    up_out[0] = d_up
    wait_experts(slot, 0, buffers, sems)
    wait_experts(slot, 1, buffers, sems)
    produced = (dot(d_gate, gate_buf[slot], 1, 1) + dot(d_up, up_buf[slot], 1, 1)).astype(bf16)
    for block in range(ranks):
        d_rows[block, pl.ds(place, capacity), :] = produced[block * capacity : (block + 1) * capacity]

    @pl.when(expert + 1 == count)
    def _():
        number = lax.broadcasted_iota(jnp.int32, (EXPERTS, tokens), 0)
        router_total = jnp.zeros(grad_router.shape, f32)
        for block in range(ranks):
            weight = gates[block]
            own_grads = jnp.zeros((EXPERTS, tokens), f32)
            for e in range(experts_here):
                here = number == info[2] * experts_here + e
                own_grads = jnp.where(here, d_gates[block, e : e + 1, :], own_grads)
            inner = jnp.sum(weight * own_grads, axis=0, keepdims=True)
            d_logits = (weight * (own_grads - inner)).astype(bf16)
            router_total = router_total + dot(d_logits, everyone[block])
            back = dot(hits[block], d_rows[block], 0, 0) + dot(d_logits, router[...], 0, 0)
            sums[block] = back.astype(bf16)
        grad_router[...] = router_total


def expert_grads_kernel(info, rows, grad_rows, d_gate, d_up, activated, keep, send):
    capacity, width = rows.shape[1], rows.shape[2]
    mine = rows[...].reshape(rows.shape[0] * capacity, width)
    incoming = grad_rows[...].reshape(rows.shape[0] * capacity, width)
    pieces = 2 * keep.shape[0]
    wide = width // pieces
    narrow = activated.shape[2] // pieces
    half = width // 2
    write_pieces(info, dot(mine, d_gate[0], 0, 0), keep, send, (0, slice(0, wide)))
    write_pieces(info, dot(mine, d_up[0], 0, 0), keep, send, (0, slice(wide, 2 * wide)))
    down = dot(activated[0], incoming, 0, 0)
    for side in range(2):
        begin = 2 * wide + side * narrow
        write_pieces(
            info, down[:, side * half : (side + 1) * half], keep, send, (0, slice(begin, begin + narrow))
        )


def layer_forward(x, weights, tables, info, routes):
    (gain_attn, gain_moe, router, owns, dense_parts, expert_parts) = weights
    w_query, w_key, w_value, w_out, w_gate, w_up, w_down = owns
    cosine, sine, query_docs, key_docs, usable, reach = tables
    rows, width = x.shape
    ranks = lax.axis_size("expert")
    pieces = lax.axis_size("dp")
    kv_width = 2 * KV_HEADS * HEAD_DIM
    keys = (reach + 1) * rows
    query, keyval = call(
        functools.partial(project_kernel, pieces),
        (struct((rows, width), bf16), struct((rows, kv_width), bf16)),
        [SMEM] + [VMEM] * 4 + [ANY] * (3 + pieces),
        (VMEM, VMEM),
        [pltpu.VMEM((width, width + kv_width), bf16), pltpu.SemaphoreType.DMA],
        flops=2 * rows * width * (width + kv_width),
        bytes_accessed=2 * width * (width + kv_width),
        name="project",
    )(info, x, gain_attn, cosine, sine, w_query, w_key, w_value, *dense_parts)
    earlier, moving = [], keyval
    for _ in range(reach):
        moving = shifted(moving, "expert", 1)
        earlier.append(moving)
    mixed, log_total, middle, routed = call(
        functools.partial(attend_kernel, pieces, reach),
        (
            struct((rows, width), bf16),
            struct((rows, LANES), f32),
            struct((rows, width), f32),
            struct((rows, width), bf16),
        ),
        [SMEM, VMEM] + [ANY] * (1 + reach) + [VMEM] * 4 + [ANY] * (1 + pieces),
        (VMEM,) * 4,
        [
            pltpu.VMEM((keys, kv_width), bf16),
            pltpu.VMEM((rows, keys), f32),
            pltpu.VMEM((width, width), bf16),
            pltpu.SemaphoreType.DMA,
            pltpu.SemaphoreType.DMA,
        ],
        flops=16 * rows * keys * width,
        bytes_accessed=2 * width * width,
        name="attend",
    )(info, query, keyval, *earlier, query_docs, key_docs, x, gain_moe, w_out, *dense_parts)
    ups, downs = line_gather(routed)
    experts_here, _, hidden = w_gate.shape
    capacity = rows * TOPK // EXPERTS
    slots = experts_here * capacity
    sums, everyone, expert_rows, gates, codes, gate_pre, up_pre = call(
        functools.partial(experts_kernel, pieces, ranks, len(expert_parts)),
        (
            struct((ranks, rows, width), bf16),
            struct((ranks, rows, width), bf16),
            struct((ranks, slots, width), bf16),
            struct((ranks, EXPERTS, rows), f32),
            struct((ranks, EXPERTS, rows), f32),
            struct((experts_here, ranks * capacity, hidden), bf16),
            struct((experts_here, ranks * capacity, hidden), bf16),
        ),
        [SMEM] + [ANY] * (2 * ranks - 1) + [VMEM] * 3 + [ANY] * (3 + pieces * len(expert_parts)),
        (VMEM,) * 5
        + (pl.BlockSpec((1, ranks * capacity, hidden), lambda e: (e, 0, 0)),) * 2,
        [
            pltpu.VMEM((ranks, slots, rows), bf16),
            pltpu.VMEM((ranks, slots, width), bf16),
            pltpu.VMEM((2, width, hidden), bf16),
            pltpu.VMEM((2, width, hidden), bf16),
            pltpu.VMEM((2, hidden, width), bf16),
            pltpu.SemaphoreType.DMA((2, 3)),
            pltpu.SemaphoreType.DMA,
        ],
        grid=(experts_here,),
        flops=6 * experts_here * ranks * capacity * width * hidden,
        bytes_accessed=6 * experts_here * width * hidden,
        name="experts",
    )(
        info, routed, *ups, *downs, routes, usable, router, w_gate, w_up, w_down,
        *[piece for chunk in expert_parts for piece in chunk],
    )
    result = (middle + line_reduce(sums)).astype(bf16)
    kept = (x, query, keyval, earlier, mixed, log_total, middle, everyone, expert_rows, gates, codes, gate_pre, up_pre)
    return result, kept


def layer_backward(grad, grad_line, kept, weights, tables, info):
    (gain_attn, gain_moe, router, owns, dense_parts, expert_parts) = weights
    w_query, w_key, w_value, w_out, w_gate, w_up, w_down = owns
    cosine, sine, query_docs, key_docs, usable, reach = tables
    (x, query, keyval, earlier, mixed, log_total, middle, everyone, expert_rows, gates, codes, gate_pre, up_pre) = kept
    rows, width = x.shape
    ranks = lax.axis_size("expert")
    pieces = lax.axis_size("dp")
    kv_width = 2 * KV_HEADS * HEAD_DIM
    keys = (reach + 1) * rows
    experts_here, _, hidden = w_gate.shape
    capacity = rows * TOPK // EXPERTS
    slots = experts_here * capacity
    ups, downs = grad_line
    per_expert = pl.BlockSpec((1, ranks * capacity, hidden), lambda e: (e, 0, 0))
    sums, grad_router, grad_rows, d_gate, d_up, activated = call(
        functools.partial(experts_back_kernel, pieces, ranks, len(expert_parts)),
        (
            struct((ranks, rows, width), bf16),
            struct((EXPERTS, width), f32),
            struct((ranks, slots, width), bf16),
        )
        + (struct((experts_here, ranks * capacity, hidden), bf16),) * 3,
        [SMEM] + [ANY] * (2 * ranks - 1) + [VMEM] * 4 + [per_expert] * 2
        + [ANY] * (3 + pieces * len(expert_parts)),
        (VMEM,) * 3 + (per_expert,) * 3,
        [
            pltpu.VMEM((ranks, rows, width), bf16),
            pltpu.VMEM((ranks, slots, rows), bf16),
            pltpu.VMEM((ranks, slots, LANES), f32),
            pltpu.VMEM((ranks, max(8, experts_here), rows), f32),
            pltpu.VMEM((ranks, slots, width), bf16),
            pltpu.VMEM((2, width, hidden), bf16),
            pltpu.VMEM((2, width, hidden), bf16),
            pltpu.VMEM((2, hidden, width), bf16),
            pltpu.SemaphoreType.DMA((2, 3)),
            pltpu.SemaphoreType.DMA,
        ],
        grid=(experts_here,),
        flops=6 * experts_here * ranks * capacity * width * hidden,
        bytes_accessed=6 * experts_here * width * hidden,
        name="experts_back",
    )(
        info, grad, *ups, *downs, everyone, gates, codes, router, gate_pre, up_pre, w_gate, w_up, w_down,
        *[piece for chunk in expert_parts for piece in chunk],
    )
    chunk_count = len(expert_parts)
    per_chunk = experts_here // chunk_count
    wide, narrow = width // pieces, hidden // pieces
    piece_rows = 2 * wide + 2 * narrow
    expert_sums = []
    for c in range(chunk_count):
        place = functools.partial(lambda c, e: (c * per_chunk + e, 0, 0), c)
        row_place = functools.partial(lambda c, e: (0, c * per_chunk + e, 0), c)
        keep, send = call(
            expert_grads_kernel,
            (struct((pieces // 2, per_chunk, piece_rows, hidden), bf16),) * 2,
            [SMEM]
            + [pl.BlockSpec((ranks, capacity, width), row_place)] * 2
            + [pl.BlockSpec((1, ranks * capacity, hidden), place)] * 3,
            (pl.BlockSpec((pieces // 2, 1, piece_rows, hidden), lambda e: (0, e, 0, 0)),) * 2,
            [],
            grid=(per_chunk,),
            flops=6 * per_chunk * ranks * capacity * width * hidden,
            bytes_accessed=6 * per_chunk * width * hidden,
            name="expert_grads",
        )(info, expert_rows, grad_rows, d_gate, d_up, activated)
        expert_sums.append(dp_reduce(keep, send))
    d_routed = line_reduce(sums)
    outs = call(
        functools.partial(attend_back_kernel, pieces, reach),
        (
            struct((rows, width), f32),
            struct((rows, width), bf16),
            struct((rows, kv_width), f32),
        )
        + (struct((rows, kv_width), bf16),) * reach
        + (struct((pieces // 2, width // pieces, width), bf16),) * 2
        + (struct((1, width), f32),),
        [SMEM] + [VMEM] * 7 + [ANY] * (1 + reach) + [VMEM] * 4 + [ANY] * (1 + pieces),
        (VMEM,) * (6 + reach),
        [
            pltpu.VMEM((keys, kv_width), bf16),
            pltpu.VMEM((rows, keys), f32),
            pltpu.VMEM((width, width), bf16),
            pltpu.VMEM((rows, width), bf16),
            pltpu.VMEM((kv_width, keys), f32),
            pltpu.SemaphoreType.DMA,
            pltpu.SemaphoreType.DMA,
        ],
        flops=40 * rows * keys * width,
        bytes_accessed=2 * width * width,
        name="attend_back",
    )(
        info, d_routed, grad, middle, gain_moe, mixed, query, log_total, keyval, *earlier,
        query_docs, key_docs, cosine, sine, w_out, *dense_parts,
    )
    d_middle, d_query, d_own = outs[:3]
    d_earlier = outs[3 : 3 + reach]
    out_keep, out_send, grad_gain_moe = outs[3 + reach :]
    moving = d_earlier[reach - 1]
    for s in reversed(range(reach)):
        moving = shifted(moving, "expert", -1)
        if s > 0:
            moving = (moving.astype(f32) + d_earlier[s - 1].astype(f32)).astype(bf16)
    piece_struct = struct((pieces // 2, width // pieces, width), bf16)
    d_normed, query_keep, query_send = call(
        functools.partial(query_back_kernel, pieces),
        (struct((rows, width), f32), piece_struct, piece_struct),
        [SMEM] + [VMEM] * 3 + [ANY] * (1 + pieces),
        (VMEM,) * 3,
        [pltpu.VMEM((width, width), bf16), pltpu.SemaphoreType.DMA],
        flops=4 * rows * width * width,
        bytes_accessed=4 * width * width,
        name="query_back",
    )(info, x, gain_attn, d_query, w_query, *dense_parts)
    d_x, kv_keep, kv_send, grad_gain_attn = call(
        functools.partial(keyval_back_kernel, pieces),
        (struct((rows, width), bf16), piece_struct, piece_struct, struct((1, width), f32)),
        [SMEM] + [VMEM] * 8 + [ANY] * (2 + pieces),
        (VMEM,) * 4,
        [
            pltpu.VMEM((width, kv_width), bf16),
            pltpu.VMEM((rows, kv_width), bf16),
            pltpu.SemaphoreType.DMA,
        ],
        flops=4 * rows * width * kv_width,
        bytes_accessed=4 * width * kv_width,
        name="keyval_back",
    )(
        info, x, gain_attn, d_own, moving, d_normed, d_middle, cosine, sine, w_key, w_value, *dense_parts,
    )
    dense_sums = []
    for keep, send in ((out_keep, out_send), (query_keep, query_send), (kv_keep, kv_send)):
        mine = dp_reduce(keep, send)
        dense_sums.append(line_reduce(mine.reshape(ranks, -1, width)))
    small = jnp.concatenate([grad_router, grad_gain_moe, grad_gain_attn], axis=0).T
    small = lax.psum_scatter(small, ("dp", "expert"), scatter_dimension=0, tiled=True)
    return d_x, expert_sums, dense_sums, small


def doc_ids(lengths, positions):
    endings = jnp.cumsum(lengths)
    return jnp.sum((positions[:, None] >= endings[None, :]).astype(jnp.int32), axis=1)


def per_device(
    inputs, cotangent, gain_attn, w_query, w_key, w_value, w_out, gain_moe, w_router, w_gate, w_up, w_down,
    doc_lengths, routes,
):
    rows, width = inputs.shape[2:]
    ranks = lax.axis_size("expert")
    pieces = lax.axis_size("dp")
    section = lax.axis_index("section")
    place = lax.axis_index("dp")
    line = lax.axis_index("expert")
    experts_here, _, hidden = w_gate.shape[1:]
    first = section == 0

    def mine(values):
        return lax.dynamic_index_in_dim(values, section, 0, False)

    def other(values):
        return lax.dynamic_index_in_dim(values, 1 - section, 0, False)

    x = mine(inputs[:, 0])
    top = mine(cotangent[:, 0])
    lengths = mine(doc_lengths[:, 0])

    wide, narrow = width // pieces, hidden // pieces

    def rows_of(matrix, axis, size):
        return lax.dynamic_slice_in_dim(matrix, place * size, size, axis)

    dense_piece = jnp.concatenate(
        [rows_of(w[0], 0, wide) for w in (w_query, w_key, w_value, w_out)], axis=1
    )
    dense_parts = fetch_pieces(dense_piece)
    small = jnp.concatenate([w_router[0].T.astype(f32), gain_attn, gain_moe], axis=0)
    other_small = swapped(small, "section", 1)
    chunk_count = 4 if experts_here % 4 == 0 else 1
    per_chunk = experts_here // chunk_count
    expert_parts = []
    for c in range(chunk_count):
        span = slice(c * per_chunk, (c + 1) * per_chunk)
        down = rows_of(w_down[0, span], 1, narrow)
        piece = jnp.concatenate(
            [
                rows_of(w_gate[0, span], 1, wide),
                rows_of(w_up[0, span], 1, wide),
                down[:, :, : width // 2],
                down[:, :, width // 2 :],
            ],
            axis=1,
        )
        expert_parts.append(fetch_pieces(piece))

    owns = (w_query[0], w_key[0], w_value[0], w_out[0], w_gate[0], w_up[0], w_down[0])
    here = routes[0, :, 0]
    my_routes = mine(here)
    other_routes = swapped(other(here), "section", 1)
    both = jnp.stack([jnp.where(first, my_routes, other_routes), jnp.where(first, other_routes, my_routes)])
    both = lax.all_gather(both, "expert", axis=1, tiled=True).transpose(0, 2, 1)
    layers, infos = [], []
    for layer in range(2):
        held = section == layer
        table = jnp.where(held, small, other_small)
        layers.append((table[EXPERTS : EXPERTS + 1], table[EXPERTS + 1 :], table[:EXPERTS].astype(bf16), owns, dense_parts, expert_parts))
        infos.append(jnp.stack([held.astype(jnp.int32), place, line]).astype(jnp.int32))

    offset = line * rows
    reach = min((WINDOW - 1) // rows + 1, ranks - 1)
    positions = offset + jnp.arange(rows, dtype=jnp.int32)
    key_places = offset - reach * rows + jnp.arange((reach + 1) * rows, dtype=jnp.int32)
    query_docs = doc_ids(lengths, positions)[:, None]
    key_docs = jnp.where(key_places >= 0, doc_ids(lengths, key_places), -1)[None, :]
    usable = (doc_ids(lengths, jnp.arange(ranks * rows, dtype=jnp.int32)) < NDOC).astype(jnp.int32)[None, :]
    half = HEAD_DIM // 2
    inverse = 10000.0 ** (-(jnp.arange(half, dtype=f32) * (2.0 / HEAD_DIM)))
    angles = positions.astype(f32)[:, None] * inverse[None, :]
    cosine = jnp.tile(jnp.cos(angles), (1, 4))
    sine = jnp.sin(angles)
    sine = jnp.concatenate([-sine, sine, -sine, sine], axis=1)
    tables = (cosine, sine, query_docs, key_docs, usable, reach)

    top_line = line_gather(top)
    between, kept_first = layer_forward(x, layers[0], tables, infos[0], both[0])
    final, kept_second = layer_forward(between, layers[1], tables, infos[1], both[1])
    d_between, experts_second, dense_second, small_second = layer_backward(
        top, top_line, kept_second, layers[1], tables, infos[1]
    )
    d_first, experts_first, dense_first, small_first = layer_backward(
        d_between, line_gather(d_between), kept_first, layers[0], tables, infos[0]
    )

    def by_section(of_first, of_second):
        held = jnp.where(first, of_first, of_second)
        got = swapped(jnp.where(first, of_second, of_first), "section", 1)
        return jnp.stack([jnp.where(first, held, got), jnp.where(first, got, held)])

    def total(of_first, of_second):
        got = to_owner(of_first, 0), to_owner(of_second, 1)
        return jnp.where(
            first, of_first.astype(f32) + got[0].astype(f32), of_second.astype(f32) + got[1].astype(f32)
        )

    outputs = by_section(between, final)
    input_grads = by_section(d_first, d_between)
    chunks = [total(a, b) for a, b in zip(experts_first, experts_second)]
    grad_gate = jnp.concatenate([c[:, :wide] for c in chunks], axis=0)
    grad_up = jnp.concatenate([c[:, wide : 2 * wide] for c in chunks], axis=0)
    grad_down = jnp.concatenate(
        [
            jnp.concatenate([c[:, 2 * wide : 2 * wide + narrow], c[:, 2 * wide + narrow :]], axis=2)
            for c in chunks
        ],
        axis=0,
    )
    grad_out, grad_query, grad_keyval = [
        total(a.astype(bf16), b.astype(bf16)) for a, b in zip(dense_first, dense_second)
    ]
    vectors = total(small_first, small_second)
    kv_half = KV_HEADS * HEAD_DIM
    return (
        outputs[None, :, None],
        input_grads[None, :, None],
        vectors[:, EXPERTS + 1][None],
        grad_query[None],
        grad_keyval[:, :kv_half][None],
        grad_keyval[:, kv_half:][None],
        grad_out[None],
        vectors[:, EXPERTS][None],
        vectors[:, :EXPERTS][None],
        grad_gate[None],
        grad_up[None],
        grad_down[None],
    )


def solution(mesh):
    placed = (
        P(None, "dp", "expert", None),
        P(None, "dp", "expert", None),
        P("section", None),
        P("section", None, None),
        P("section", None, None),
        P("section", None, None),
        P("section", None, None),
        P("section", None),
        P("section", None, None),
        P("section", "expert", None, None),
        P("section", "expert", None, None),
        P("section", "expert", None, None),
        P(None, "dp", None),
        P("section", None, "dp", "expert", None),
    )
    return jax.shard_map(
        per_device,
        mesh=mesh,
        in_specs=placed,
        out_specs=(
            P("section", None, "dp", "expert", None),
            P("section", None, "dp", "expert", None),
            P("section", ("dp", "expert")),
            P("section", ("dp", "expert"), None),
            P("section", ("dp", "expert"), None),
            P("section", ("dp", "expert"), None),
            P("section", ("dp", "expert"), None),
            P("section", ("dp", "expert")),
            P("section", ("dp", "expert"), None),
            P("section", "expert", "dp", None),
            P("section", "expert", "dp", None),
            P("section", "expert", "dp", None),
        ),
        check_vma=False,
    )
```

time: 2500 us -> 1400 us (0.56)
  matrix products: 548 us -> 0 us
  blocking collectives: 337 us -> 19.6 us
  local copies, waits for them, and re-layouts: 352 us -> 56.4 us
  other arithmetic: 367 us -> 111 us
  Pallas kernels: 0 us -> 246 us
  starting transfers between devices: 119 us -> 313 us
  waiting for transfers between devices: 753 us -> 623 us
    dot_general x93 -> x0, matrix products: 548 us -> none  [the longest x3 63.9 us: layer_backward(): jnp.einsum('hgqk,qhgd->khd', d_scores, grouped, preferred_element_type=jn...]
    all_to_all x9 -> x0, waiting for transfers between devices: 483 us -> none  [the longest x3 215 us: layer_backward(): lax.all_to_all(d_rows[None], 'expert', split_axis=2, concat_axis=0, tiled...]
    ppermute x28 -> x160, waiting for transfers between devices: 131 us -> 520 us  [the longest x52 271 us: swapped(): lax.ppermute(value, axis, [(source, source ^ bit) for source in range(cou...]
    all_to_all x3 -> x0, blocking collectives: 302 us -> none  [the longest x2 202 us: layer_forward(): lax.all_to_all(buffer, 'expert', split_axis=0, concat_axis=2, tiled=True)[0]]
    ppermute x28 -> x160, starting transfers between devices: 58.7 us -> 313 us  [the longest x92 240 us: shifted(): lax.ppermute(value, axis, [(source, source + steps) for source in names])]
    pallas_call x0 -> x22, Pallas kernels: none -> 246 us  [the longest x8 56.4 us: layer_backward(): call(expert_grads_kernel, (struct((pieces // 2, per_chunk, piece_rows, hi...]
    scatter-add x6 -> x0, other arithmetic: 139 us -> none  [the longest x3 72.5 us: layer_forward(): buffer.at[slot_index.reshape(-1)].add(jnp.repeat(routed_in, TOPK, axis=0))]
    reduce_scatter x7 -> x0, waiting for transfers between devices: 138 us -> none  [the longest x4 138 us: per_device(): lax.psum_scatter(dense_total, ('dp', 'expert'), scatter_dimension=0, tile...]
  transfers between devices with their start and end apart: 45 -> 162, of which waited for: 30 -> 58; matrix products, arithmetic and copies ran while one was open for 29% -> 10% of each run, Pallas kernels for 0% -> 13%
where the time goes in v1:
time: 1400 us; the launch traced here: 1390 us
  waiting for transfers between devices  623 us (44%)
  starting transfers between devices  313 us (22%)
  Pallas kernels  246 us (18%)
  other arithmetic  111 us (8%)
  local copies, waits for them, and re-layouts  56.4 us (4%)
  blocking collectives  19.6 us (1%)
  between operations  17.6 us (1%)
    ppermute x52, waiting for transfers between devices, swapped(): lax.ppermute(value, axis, [(source, source ^ bit) for source in range(cou...  271 us
    ppermute x92, starting transfers between devices, shifted(): lax.ppermute(value, axis, [(source, source + steps) for source in names])  240 us
    ppermute x92, waiting for transfers between devices, shifted(): lax.ppermute(value, axis, [(source, source + steps) for source in names])  142 us
    ppermute x16, waiting for transfers between devices, to_owner(): return lax.ppermute(value, 'section', [(1 - layer, layer)])  107 us
    unnamed x4, waiting for transfers between devices  103 us
    pallas_call x8, Pallas kernels, layer_backward(): call(expert_grads_kernel, (struct((pieces // 2, per_chunk, piece_rows, hi...  56.4 us
    pallas_call x2, Pallas kernels, layer_backward(): call(functools.partial(experts_back_kernel, pieces, ranks, len(expert_par...  52.8 us
    pallas_call x2, Pallas kernels, layer_forward(): call(functools.partial(experts_kernel, pieces, ranks, len(expert_parts)),...  45.7 us
  transfers between devices with their start and end apart: 162, of which 58 were waited for; matrix products, arithmetic and copies ran while one was open for 10% of the time, Pallas kernels for 13%

profile of v1, /device:TPU:0, one launch (start us, length us, event | category | flops | bytes accessed | tf_op | source)
XLA Modules:
  0.0 1387.8 jit_solution(14048861815948830998)
XLA Ops:
  33.8 21.8 %collective-permute-done.1.rest_0_.rest_7_ = bf16[256,3072]{1,0:T(8,128)(2,1)S(1)} collective-permute-done((bf16[256,3072]{1,0:T(8,128)(2,1)}, bf16[256,3072]{1,0:T(8,128)(2,1)S(1)}, u32[]{:S(2)}, u32[]{:S(2)}) %collective-permute-start.1) | collective-permute-done | bytes 1572896 | tf_op jit(solution)/shard_map/ppermute | solution.py:34
  65.9 23.4 %collective-permute-done.3.rest_2_.rest_9_ = bf16[256,3072]{1,0:T(8,128)(2,1)} collective-permute-done((bf16[256,3072]{1,0:T(8,128)(2,1)S(1)}, bf16[256,3072]{1,0:T(8,128)(2,1)}, u32[]{:S(2)}, u32[]{:S(2)}) %collective-permute-start.3) | collective-permute-done | bytes 1572896 | tf_op jit(solution)/shard_map/ppermute | solution.py:34
  94.3 28.9 %collective-permute-done.22.rest_20_.rest_23_ = bf16[2,768,512]{2,1,0:T(8,128)(2,1)} collective-permute-done((bf16[2,768,512]{2,1,0:T(8,128)(2,1)}, bf16[2,768,512]{2,1,0:T(8,128)(2,1)}, u32[]{:S(2)}, u32[]{:S(2)}) %collective-permute-start.22) | collective-permute-done | bytes 1572896 | tf_op jit(solution)/shard_map/ppermute | solution.py:34
  125.2 31.7 %collective-permute-done.18.rest_16_.rest_19_ = bf16[2,768,512]{2,1,0:T(8,128)(2,1)} collective-permute-done((bf16[2,768,512]{2,1,0:T(8,128)(2,1)}, bf16[2,768,512]{2,1,0:T(8,128)(2,1)}, u32[]{:S(2)}, u32[]{:S(2)}) %collective-permute-start.18) | collective-permute-done | bytes 1572896 | tf_op jit(solution)/shard_map/ppermute | solution.py:34
  167.6 21.5 %collective-permute-done.26.rest_24_.rest_27_ = bf16[2,768,512]{2,1,0:T(8,128)(2,1)} collective-permute-done((bf16[2,768,512]{2,1,0:T(8,128)(2,1)}, bf16[2,768,512]{2,1,0:T(8,128)(2,1)}, u32[]{:S(2)}, u32[]{:S(2)}) %collective-permute-start.26) | collective-permute-done | bytes 1572896 | tf_op jit(solution)/shard_map/ppermute | solution.py:34
  192.8 10.0 collective-permute-done.5.rest_0_
  209.5 6.4 collective-permute-done.6.rest_1_
  217.6 12.8 attend.2
  230.4 14.4 %collective-permute-done.20.rest_18_.rest_21_ = bf16[2,768,512]{2,1,0:T(8,128)(2,1)} collective-permute-done((bf16[2,768,512]{2,1,0:T(8,128)(2,1)}, bf16[2,768,512]{2,1,0:T(8,128)(2,1)}, u32[]{:S(2)}, u32[]{:S(2)}) %collective-permute-start.20) | collective-permute-done | bytes 1572896 | tf_op jit(solution)/shard_map/ppermute | solution.py:34
  250.7 23.9 %collective-permute-done.28.rest_26_.rest_29_ = bf16[2,768,512]{2,1,0:T(8,128)(2,1)} collective-permute-done((bf16[2,768,512]{2,1,0:T(8,128)(2,1)}, bf16[2,768,512]{2,1,0:T(8,128)(2,1)}, u32[]{:S(2)}, u32[]{:S(2)}) %collective-permute-start.28) | collective-permute-done | bytes 1572896 | tf_op jit(solution)/shard_map/ppermute | solution.py:34
  282.6 8.8 collective-permute-done.11.rest_4_
  297.3 19.6 %all_gather.3 = s32[2,1024,8]{1,2,0:T(8,128)S(1)} all-gather(s32[2,256,8]{1,2,0:T(8,128)S(1)} %pad_add_fusion), channel_id=1, replica_groups=mesh['section'=2,'dp'=4,'expert'=4] {'expert'}, dimensions={1}, use_global_device_ids=true | all-gather | bytes 81920 | tf_op jit(solution)/shard_map/all_gather | solution.py:919
  320.1 22.3 %experts.2 = (bf16[4,256,1024]{2,1,0:T(8,128)(2,1)}, bf16[4,256,1024]{2,1,0:T(8,128)(2,1)}, bf16[4,512,1024]{2,1,0:T(8,128)(2,1)}, f32[4,32,256]{2,1,0:T(8,128)}...) custom-call(s32[3]{0:T(128)} %add_add_fusion.info, ...), custom_call_target="tpu_custom_call" | custom-call | flops 6442450944 | bytes 25165824 | tf_op jit(solution)/shard_map/experts/pallas_call | solution.py:681
  350.6 5.8 collective-permute-done.30
  373.5 9.1 collective-permute-start.32
  403.1 10.1 collective-permute-done.36.rest_0_
  417.5 6.6 collective-permute-done.37.rest_1_
  425.0 12.7 attend.3
  498.2 23.4 %experts.3 = (bf16[4,256,1024]{2,1,0:T(8,128)(2,1)}, bf16[4,256,1024]{2,1,0:T(8,128)(2,1)}, bf16[4,512,1024]{2,1,0:T(8,128)(2,1)}, f32[4,32,256]{2,1,0:T(8,128)}...) custom-call(s32[3]{0:T(128)} %add_add_fusion.1.info, ...), custom_call_target="tpu_custom_call" | custom-call | flops 6442450944 | bytes 25165824 | tf_op jit(solution)/shard_map/experts/pallas_call | solution.py:681
  522.6 26.4 %experts_back.2 = (bf16[4,256,1024]{2,1,0:T(8,128)(2,1)}, f32[32,1024]{1,0:T(8,128)}, bf16[4,512,1024]{2,1,0:T(8,128)(2,1)}, bf16[8,256,512]{2,1,0:T(8,128)(2,1)...) custom-call(s32[3]{0:T(128)} %add_add_fusion.1.info, bf16[256,1024]{1,0:T(8,128)(2,1)} %copy-done.31, ...), custom_call_target="tpu_custom_call" | custom-call | flops 6442450944 | bytes 25165824 | tf_op jit(solution)/shard_map/experts_back/pallas_call | solution.py:732
  557.7 9.5 collective-permute-done.57
  572.7 5.7 collective-permute-done.44
  602.5 7.2 collective-permute-done.62
  610.9 15.9 %attend_back.2 = (f32[256,1024]{1,0:T(8,128)}, bf16[256,1024]{1,0:T(8,128)(2,1)}, f32[256,1024]{1,0:T(8,128)}, bf16[256,1024]{1,0:T(8,128)(2,1)}, bf16[256,1024]...) custom-call(s32[3]{0:T(128)} %add_add_fusion.1.info, ...), custom_call_target="tpu_custom_call" | custom-call | flops 8053063680 | bytes 2097152 | tf_op jit(solution)/shard_map/attend_back/pallas_call | solution.py:786
  628.1 7.1 expert_grads.15
  637.6 7.1 expert_grads.13
  646.9 7.0 expert_grads.11
  654.2 7.1 expert_grads.9
  670.1 7.5 keyval_back.2
  683.0 53.6 %reduce-scatter.9.cloned.1.call-done = f32[64,34]{1,0:T(8,128)} async-done(((f32[1024,34]{1,0:T(8,128)}), f32[64,34]{1,0:T(8,128)}) %reduce-scatter.9.cloned.1.call-update) | async-done | bytes 8720
  775.3 9.9 collective-permute-done.93
  801.0 6.6 collective-permute-done.94
  819.5 26.4 %experts_back.3 = (bf16[4,256,1024]{2,1,0:T(8,128)(2,1)}, f32[32,1024]{1,0:T(8,128)}, bf16[4,512,1024]{2,1,0:T(8,128)(2,1)}, bf16[8,256,512]{2,1,0:T(8,128)(2,1)...) custom-call(s32[3]{0:T(128)} %add_add_fusion.info, bf16[256,1024]{1,0:T(8,128)(2,1)} %get-tuple-element.120.own.grad, ...), custom_call_target="tpu_custom_call" | custom-call | flops 6442450944 | bytes 25165824 | tf_op jit(solution)/shard_map/experts_back/pallas_call | solution.py:732
  877.6 7.0 expert_grads.14
  897.7 7.0 expert_grads.12
  914.0 15.7 %attend_back.3 = (f32[256,1024]{1,0:T(8,128)}, bf16[256,1024]{1,0:T(8,128)(2,1)}, f32[256,1024]{1,0:T(8,128)}, bf16[256,1024]{1,0:T(8,128)(2,1)}, bf16[256,1024]...) custom-call(s32[3]{0:T(128)} %add_add_fusion.info, ...), custom_call_target="tpu_custom_call" | custom-call | flops 8053063680 | bytes 2097152 | tf_op jit(solution)/shard_map/attend_back/pallas_call | solution.py:786
  932.2 7.0 expert_grads.10
  939.2 7.1 expert_grads.8
  953.8 22.3 %collective-permute-done.146 = bf16[1,2,768,512]{3,2,1,0:T(8,128)(2,1)} collective-permute-done((bf16[1,2,768,512]{3,2,1,0:T(8,128)(2,1)}, bf16[1,2,768,512]{3,2,1,0:T(8,128)(2,1)}, u32[]{:S(2)}, u32[]{:S(2)}) %collective-permute-start.146) | collective-permute-done | bytes 1572896 | tf_op jit(solution)/shard_map/ppermute | solution.py:34
  983.6 16.5 %collective-permute-done.140 = bf16[1,2,768,512]{3,2,1,0:T(8,128)(2,1)} collective-permute-done((bf16[1,2,768,512]{3,2,1,0:T(8,128)(2,1)}, bf16[1,2,768,512]{3,2,1,0:T(8,128)(2,1)}, u32[]{:S(2)}, u32[]{:S(2)}) %collective-permute-start.140) | collective-permute-done | bytes 1572896 | tf_op jit(solution)/shard_map/ppermute | solution.py:34
  1007.0 7.1 keyval_back.3
  1023.7 49.2 %reduce-scatter.7.cloned.1.call-done = f32[64,34]{1,0:T(8,128)} async-done(((f32[1024,34]{1,0:T(8,128)}), f32[64,34]{1,0:T(8,128)}) %reduce-scatter.7.cloned.1.call-update) | async-done | bytes 8720
  1144.3 39.2 %collective-permute-done.101 = bf16[1,256,1024]{2,1,0:T(8,128)(2,1)S(1)} collective-permute-done((bf16[1,256,1024]{2,1,0:T(8,128)(2,1)S(1)}, bf16[1,256,1024]{2,1,0:T(8,128)(2,1)S(1)}, u32[]{:S(2)}, u32[]{:S(2)}) %collective-permute-start.101) | collective-permute-done | bytes 524320 | tf_op jit(solution)/shard_map/ppermute | solution.py:34
  1230.8 19.7 %collective-permute-done.137 = bf16[1,2,768,512]{3,2,1,0:T(8,128)(2,1)S(1)} collective-permute-done((bf16[1,2,768,512]{3,2,1,0:T(8,128)(2,1)S(1)}, bf16[1,2,768,512]{3,2,1,0:T(8,128)(2,1)S(1)}, u32[]{:S(2)}, u32[]{:S(2)}) %collective-permute-start.137) | collective-permute-done | bytes 1572896 | tf_op jit(solution)/shard_map/ppermute | solution.py:34
  1253.4 42.9 %collective-permute-done.108 = bf16[64,1024]{1,0:T(8,128)(2,1)S(1)} collective-permute-done((bf16[64,1024]{1,0:T(8,128)(2,1)S(1)}, bf16[64,1024]{1,0:T(8,128)(2,1)S(1)}, u32[]{:S(2)}, u32[]{:S(2)}) %collective-permute-start.108) | collective-permute-done | bytes 131104 | tf_op jit(solution)/shard_map/ppermute | solution.py:91
  1309.9 22.7 %collective-permute-done.147 = bf16[2,768,512]{2,1,0:T(8,128)(2,1)} collective-permute-done((bf16[2,768,512]{2,1,0:T(8,128)(2,1)S(1)}, bf16[2,768,512]{2,1,0:T(8,128)(2,1)}, u32[]{:S(2)}, u32[]{:S(2)}) %collective-permute-start.147) | collective-permute-done | bytes 1572896 | tf_op jit(solution)/shard_map/ppermute | solution.py:91
  1332.6 26.7 %collective-permute-done.141 = bf16[2,768,512]{2,1,0:T(8,128)(2,1)} collective-permute-done((bf16[2,768,512]{2,1,0:T(8,128)(2,1)S(1)}, bf16[2,768,512]{2,1,0:T(8,128)(2,1)}, u32[]{:S(2)}, u32[]{:S(2)}) %collective-permute-start.141) | collective-permute-done | bytes 1572896 | tf_op jit(solution)/shard_map/ppermute | solution.py:91
  1359.3 8.7 collective-permute-done.138
  (660 shorter events, 561.4 us)
Async XLA Ops:
  7.2 729.5 %reduce-scatter.9.cloned.1.call-start = ((), (), s32[]{:S(2)}) async-start(), calls=%async_computation.3 | async-start | bytes 557056
  8.0 56.1 %collective-permute-start.13 = (s32[256,8]{0,1:T(8,128)S(1)}, s32[256,8]{0,1:T(8,128)S(1)}, u32[]{:S(2)}, u32[]{:S(2)}) collective-permute-start(s32[256,8]{0,1:T(8,128)S(1)} %fusion.70), channel_id=1, source_target_pairs={{0,16},{16,0},{1,17},{17,1},{2,18},{18,2},{3,19},{19,3},{4,20},{20... | collective-permute-start | bytes 24584 | tf_op jit(solution)/shard_map/ppermute | solution.py:34
  12.5 53.2 %collective-permute-start = (f32[34,1024]{1,0:T(8,128)S(1)}, f32[34,1024]{1,0:T(8,128)}, u32[]{:S(2)}, u32[]{:S(2)}) collective-permute-start(f32[34,1024]{1,0:T(8,128)S(1)} %pad_maximum_fusion.5), channel_id=1, source_target_pairs={{0,16},{16,0},{1,17},{17,1},{2,18},{18,2},{3,19},{19,3},{4,20},{20... | collective-permute-start | bytes 417800 | tf_op jit(solution)/shard_map/ppermute | solution.py:34
  33.7 56.9 %collective-permute-start.14 = (bf16[2,768,512]{2,1,0:T(8,128)(2,1)S(1)}, bf16[2,768,512]{2,1,0:T(8,128)(2,1)}, u32[]{:S(2)}, u32[]{:S(2)}) collective-permute-start(bf16[2,768,512]{2,1,0:T(8,128)(2,1)S(1)} %pad_maximum_fusion.1), channel_id=1, source_target_pairs={{0,16},{16,0},{1,17},{17,1},{2,18},{18,2},{3,19},{19,3},{4,20},{20... | collective-permute-start | bytes 4718600 | tf_op jit(solution)/shard_map/ppermute | solution.py:34
  60.2 63.0 %collective-permute-start.22 = (bf16[2,768,512]{2,1,0:T(8,128)(2,1)}, bf16[2,768,512]{2,1,0:T(8,128)(2,1)}, u32[]{:S(2)}, u32[]{:S(2)}) collective-permute-start(bf16[2,768,512]{2,1,0:T(8,128)(2,1)} %pad_maximum_fusion.3), channel_id=1, source_target_pairs={{0,16},{16,0},{1,17},{17,1},{2,18},{18,2},{3,19},{19,3},{4,20},{20... | collective-permute-start | bytes 4718600 | tf_op jit(solution)/shard_map/ppermute | solution.py:34
  64.1 92.7 %collective-permute-start.18 = (bf16[2,768,512]{2,1,0:T(8,128)(2,1)}, bf16[2,768,512]{2,1,0:T(8,128)(2,1)}, u32[]{:S(2)}, u32[]{:S(2)}) collective-permute-start(bf16[2,768,512]{2,1,0:T(8,128)(2,1)} %pad_maximum_fusion.2), channel_id=1, source_target_pairs={{0,16},{16,0},{1,17},{17,1},{2,18},{18,2},{3,19},{19,3},{4,20},{20... | collective-permute-start | bytes 4718600 | tf_op jit(solution)/shard_map/ppermute | solution.py:34
  65.8 92.6 %collective-permute-start.2 = (bf16[256,3072]{1,0:T(8,128)(2,1)S(1)}, bf16[256,3072]{1,0:T(8,128)(2,1)}, u32[]{:S(2)}, u32[]{:S(2)}) collective-permute-start(bf16[256,3072]{1,0:T(8,128)(2,1)S(1)} %collective-permute-done.1.rest_0_.rest_7_), channel_id=1, source_target_pairs={{0,4},{4,0},{8,12},{12,8},{1,5},{5,1},{9,13},{13,9},{2,6},{6,2},{1... | collective-permute-start | bytes 4718600 | tf_op jit(solution)/shard_map/ppermute | solution.py:34
  89.2 71.2 %collective-permute-start.4 = (bf16[256,3072]{1,0:T(8,128)(2,1)}, bf16[256,3072]{1,0:T(8,128)(2,1)}, u32[]{:S(2)}, u32[]{:S(2)}) collective-permute-start(bf16[256,3072]{1,0:T(8,128)(2,1)} %collective-permute-done.3.rest_2_.rest_9_), channel_id=1, source_target_pairs={{0,4},{4,0},{8,12},{12,8},{1,5},{5,1},{9,13},{13,9},{2,6},{6,2},{1... | collective-permute-start | bytes 4718600 | tf_op jit(solution)/shard_map/ppermute | solution.py:34
  90.6 98.5 %collective-permute-start.26 = (bf16[2,768,512]{2,1,0:T(8,128)(2,1)}, bf16[2,768,512]{2,1,0:T(8,128)(2,1)}, u32[]{:S(2)}, u32[]{:S(2)}) collective-permute-start(bf16[2,768,512]{2,1,0:T(8,128)(2,1)} %pad_maximum_fusion.4), channel_id=1, source_target_pairs={{0,16},{16,0},{1,17},{17,1},{2,18},{18,2},{3,19},{19,3},{4,20},{20... | collective-permute-start | bytes 4718600 | tf_op jit(solution)/shard_map/ppermute | solution.py:34
  123.2 84.0 %collective-permute-start.16 = (bf16[2,768,512]{2,1,0:T(8,128)(2,1)}, bf16[2,768,512]{2,1,0:T(8,128)(2,1)}, u32[]{:S(2)}, u32[]{:S(2)}) collective-permute-start(bf16[2,768,512]{2,1,0:T(8,128)(2,1)} %collective-permute-done.14.rest_12_.rest_15_), channel_id=1, source_target_pairs={{0,8},{4,12},{8,0},{12,4},{1,9},{5,13},{9,1},{13,5},{2,10},{6,14},... | collective-permute-start | bytes 4718600 | tf_op jit(solution)/shard_map/ppermute | solution.py:34
  156.9 51.9 %collective-permute-start.15 = (bf16[2,768,512]{2,1,0:T(8,128)(2,1)}, bf16[2,768,512]{2,1,0:T(8,128)(2,1)}, u32[]{:S(2)}, u32[]{:S(2)}) collective-permute-start(bf16[2,768,512]{2,1,0:T(8,128)(2,1)} %collective-permute-done.14.rest_12_.rest_15_), channel_id=1, source_target_pairs={{0,4},{4,0},{8,12},{12,8},{1,5},{5,1},{9,13},{13,9},{2,6},{6,2},{1... | collective-permute-start | bytes 4718600 | tf_op jit(solution)/shard_map/ppermute | solution.py:34
  158.4 50.4 %collective-permute-start.24 = (bf16[2,768,512]{2,1,0:T(8,128)(2,1)}, bf16[2,768,512]{2,1,0:T(8,128)(2,1)S(1)}, u32[]{:S(2)}, u32[]{:S(2)}) collective-permute-start(bf16[2,768,512]{2,1,0:T(8,128)(2,1)} %collective-permute-done.22.rest_20_.rest_23_), channel_id=1, source_target_pairs={{0,8},{4,12},{8,0},{12,4},{1,9},{5,13},{9,1},{13,5},{2,10},{6,14},... | collective-permute-start | bytes 4718600 | tf_op jit(solution)/shard_map/ppermute | solution.py:34
  160.4 48.9 %collective-permute-start.23 = (bf16[2,768,512]{2,1,0:T(8,128)(2,1)}, bf16[2,768,512]{2,1,0:T(8,128)(2,1)}, u32[]{:S(2)}, u32[]{:S(2)}) collective-permute-start(bf16[2,768,512]{2,1,0:T(8,128)(2,1)} %collective-permute-done.22.rest_20_.rest_23_), channel_id=1, source_target_pairs={{0,4},{4,0},{8,12},{12,8},{1,5},{5,1},{9,13},{13,9},{2,6},{6,2},{1... | collective-permute-start | bytes 4718600 | tf_op jit(solution)/shard_map/ppermute | solution.py:34
  208.7 65.9 %collective-permute-start.28 = (bf16[2,768,512]{2,1,0:T(8,128)(2,1)}, bf16[2,768,512]{2,1,0:T(8,128)(2,1)}, u32[]{:S(2)}, u32[]{:S(2)}) collective-permute-start(bf16[2,768,512]{2,1,0:T(8,128)(2,1)} %collective-permute-done.26.rest_24_.rest_27_), channel_id=1, source_target_pairs={{0,8},{4,12},{8,0},{12,4},{1,9},{5,13},{9,1},{13,5},{2,10},{6,14},... | collective-permute-start | bytes 4718600 | tf_op jit(solution)/shard_map/ppermute | solution.py:34
  209.3 65.4 %collective-permute-start.27 = (bf16[2,768,512]{2,1,0:T(8,128)(2,1)}, bf16[2,768,512]{2,1,0:T(8,128)(2,1)}, u32[]{:S(2)}, u32[]{:S(2)}) collective-permute-start(bf16[2,768,512]{2,1,0:T(8,128)(2,1)} %collective-permute-done.26.rest_24_.rest_27_), channel_id=1, source_target_pairs={{0,4},{4,0},{8,12},{12,8},{1,5},{5,1},{9,13},{13,9},{2,6},{6,2},{1... | collective-permute-start | bytes 4718600 | tf_op jit(solution)/shard_map/ppermute | solution.py:34
  215.8 59.3 %collective-permute-start.17 = (bf16[2,768,512]{2,1,0:T(8,128)(2,1)}, bf16[2,768,512]{2,1,0:T(8,128)(2,1)}, u32[]{:S(2)}, u32[]{:S(2)}) collective-permute-start(bf16[2,768,512]{2,1,0:T(8,128)(2,1)} %collective-permute-done.16.rest_14_.rest_17_), channel_id=1, source_target_pairs={{0,4},{4,0},{8,12},{12,8},{1,5},{5,1},{9,13},{13,9},{2,6},{6,2},{1... | collective-permute-start | bytes 4718600 | tf_op jit(solution)/shard_map/ppermute | solution.py:34
  274.7 44.4 %collective-permute-start.25 = (bf16[2,768,512]{2,1,0:T(8,128)(2,1)S(1)}, bf16[2,768,512]{2,1,0:T(8,128)(2,1)}, u32[]{:S(2)}, u32[]{:S(2)}) collective-permute-start(bf16[2,768,512]{2,1,0:T(8,128)(2,1)S(1)} %collective-permute-done.24.rest_22_.rest_25_), channel_id=1, source_target_pairs={{0,4},{4,0},{8,12},{12,8},{1,5},{5,1},{9,13},{13,9},{2,6},{6,2},{1... | collective-permute-start | bytes 4718600 | tf_op jit(solution)/shard_map/ppermute | solution.py:34
  635.3 102.8 %collective-permute-start.157 = (bf16[2,2,768,512]{3,2,1,0:T(8,128)(2,1)}, bf16[2,2,768,512]{3,2,1,0:T(8,128)(2,1)}, u32[]{:S(2)}, u32[]{:S(2)}) collective-permute-start(bf16[2,2,768,512]{3,2,1,0:T(8,128)(2,1)} %get-tuple-element.179), channel_id=1, source_target_pairs={{0,4},{4,0},{8,12},{12,8},{1,5},{5,1},{9,13},{13,9},{2,6},{6,2},{1... | collective-permute-start | bytes 9437192 | tf_op jit(solution)/shard_map/ppermute | solution.py:34
  644.7 100.9 %collective-permute-start.151 = (bf16[2,2,768,512]{3,2,1,0:T(8,128)(2,1)}, bf16[2,2,768,512]{3,2,1,0:T(8,128)(2,1)}, u32[]{:S(2)}, u32[]{:S(2)}) collective-permute-start(bf16[2,2,768,512]{3,2,1,0:T(8,128)(2,1)} %get-tuple-element.175), channel_id=1, source_target_pairs={{0,4},{4,0},{8,12},{12,8},{1,5},{5,1},{9,13},{13,9},{2,6},{6,2},{1... | collective-permute-start | bytes 9437192 | tf_op jit(solution)/shard_map/ppermute | solution.py:34
  653.9 96.3 %collective-permute-start.145 = (bf16[2,2,768,512]{3,2,1,0:T(8,128)(2,1)}, bf16[2,2,768,512]{3,2,1,0:T(8,128)(2,1)}, u32[]{:S(2)}, u32[]{:S(2)}) collective-permute-start(bf16[2,2,768,512]{3,2,1,0:T(8,128)(2,1)} %get-tuple-element.171), channel_id=1, source_target_pairs={{0,4},{4,0},{8,12},{12,8},{1,5},{5,1},{9,13},{13,9},{2,6},{6,2},{1... | collective-permute-start | bytes 9437192 | tf_op jit(solution)/shard_map/ppermute | solution.py:34
  662.2 91.9 %collective-permute-start.139 = (bf16[2,2,768,512]{3,2,1,0:T(8,128)(2,1)}, bf16[2,2,768,512]{3,2,1,0:T(8,128)(2,1)}, u32[]{:S(2)}, u32[]{:S(2)}) collective-permute-start(bf16[2,2,768,512]{3,2,1,0:T(8,128)(2,1)} %get-tuple-element.167), channel_id=1, source_target_pairs={{0,4},{4,0},{8,12},{12,8},{1,5},{5,1},{9,13},{13,9},{2,6},{6,2},{1... | collective-permute-start | bytes 9437192 | tf_op jit(solution)/shard_map/ppermute | solution.py:34
  679.4 393.6 %reduce-scatter.7.cloned.1.call-start = ((), (), s32[]{:S(2)}) async-start(), calls=%async_computation.2 | async-start | bytes 557056
  679.5 86.3 %collective-permute-start.68 = (bf16[256,1024]{1,0:T(8,128)(2,1)}, bf16[256,1024]{1,0:T(8,128)(2,1)S(1)}, u32[]{:S(2)}, u32[]{:S(2)}) collective-permute-start(bf16[256,1024]{1,0:T(8,128)(2,1)} %get-tuple-element.120.own.grad), channel_id=1, source_target_pairs={{1,0},{2,1},{3,2},{5,4},{6,5},{7,6},{9,8},{10,9},{11,10},{13,12},{... | collective-permute-start | bytes 1572872 | tf_op jit(solution)/shard_map/ppermute | solution.py:29
  750.2 100.6 %collective-permute-start.109 = (bf16[2,256,1024]{2,1,0:T(8,128)(2,1)}, bf16[2,256,1024]{2,1,0:T(8,128)(2,1)}, u32[]{:S(2)}, u32[]{:S(2)}) collective-permute-start(bf16[2,256,1024]{2,1,0:T(8,128)(2,1)} %get-tuple-element.149), channel_id=1, source_target_pairs={{0,4},{4,0},{8,12},{12,8},{1,5},{5,1},{9,13},{13,9},{2,6},{6,2},{1... | collective-permute-start | bytes 3145736 | tf_op jit(solution)/shard_map/ppermute | solution.py:34
  807.6 46.3 %collective-permute-start.131 = (bf16[64,1024]{1,0:T(8,128)(2,1)}, bf16[64,1024]{1,0:T(8,128)(2,1)S(1)}, u32[]{:S(2)}, u32[]{:S(2)}) collective-permute-start(bf16[64,1024]{1,0:T(8,128)(2,1)} %get-tuple-element.304), channel_id=1, source_target_pairs={{0,1},{1,2},{2,3},{4,5},{5,6},{6,7},{8,9},{9,10},{10,11},{12,13},{... | collective-permute-start | bytes 393224 | tf_op jit(solution)/shard_map/ppermute | solution.py:29
  858.0 90.4 %collective-permute-start.158 = (bf16[1,2,768,512]{3,2,1,0:T(8,128)(2,1)}, bf16[1,2,768,512]{3,2,1,0:T(8,128)(2,1)}, u32[]{:S(2)}, u32[]{:S(2)}) collective-permute-start(bf16[1,2,768,512]{3,2,1,0:T(8,128)(2,1)} %slice.389), channel_id=1, source_target_pairs={{0,8},{4,12},{8,0},{12,4},{1,9},{5,13},{9,1},{13,5},{2,10},{6,14},... | collective-permute-start | bytes 4718600 | tf_op jit(solution)/shard_map/ppermute | solution.py:34
  904.7 48.6 %collective-permute-start.152 = (bf16[1,2,768,512]{3,2,1,0:T(8,128)(2,1)}, bf16[1,2,768,512]{3,2,1,0:T(8,128)(2,1)}, u32[]{:S(2)}, u32[]{:S(2)}) collective-permute-start(bf16[1,2,768,512]{3,2,1,0:T(8,128)(2,1)} %slice.384), channel_id=1, source_target_pairs={{0,8},{4,12},{8,0},{12,4},{1,9},{5,13},{9,1},{13,5},{2,10},{6,14},... | collective-permute-start | bytes 4718600 | tf_op jit(solution)/shard_map/ppermute | solution.py:34
  905.9 70.2 %collective-permute-start.146 = (bf16[1,2,768,512]{3,2,1,0:T(8,128)(2,1)}, bf16[1,2,768,512]{3,2,1,0:T(8,128)(2,1)}, u32[]{:S(2)}, u32[]{:S(2)}) collective-permute-start(bf16[1,2,768,512]{3,2,1,0:T(8,128)(2,1)} %slice.379), channel_id=1, source_target_pairs={{0,8},{4,12},{8,0},{12,4},{1,9},{5,13},{9,1},{13,5},{2,10},{6,14},... | collective-permute-start | bytes 4718600 | tf_op jit(solution)/shard_map/ppermute | solution.py:34
  929.7 70.5 %collective-permute-start.140 = (bf16[1,2,768,512]{3,2,1,0:T(8,128)(2,1)}, bf16[1,2,768,512]{3,2,1,0:T(8,128)(2,1)}, u32[]{:S(2)}, u32[]{:S(2)}) collective-permute-start(bf16[1,2,768,512]{3,2,1,0:T(8,128)(2,1)} %slice.374), channel_id=1, source_target_pairs={{0,8},{4,12},{8,0},{12,4},{1,9},{5,13},{9,1},{13,5},{2,10},{6,14},... | collective-permute-start | bytes 4718600 | tf_op jit(solution)/shard_map/ppermute | solution.py:34
  947.3 136.5 %collective-permute-start.154 = (bf16[2,2,768,512]{3,2,1,0:T(8,128)(2,1)}, bf16[2,2,768,512]{3,2,1,0:T(8,128)(2,1)}, u32[]{:S(2)}, u32[]{:S(2)}) collective-permute-start(bf16[2,2,768,512]{3,2,1,0:T(8,128)(2,1)} %get-tuple-element.177), channel_id=1, source_target_pairs={{0,4},{4,0},{8,12},{12,8},{1,5},{5,1},{9,13},{13,9},{2,6},{6,2},{1... | collective-permute-start | bytes 9437192 | tf_op jit(solution)/shard_map/ppermute | solution.py:34
  948.4 51.7 %collective-permute-start.78 = (bf16[256,1024]{1,0:T(8,128)(2,1)}, bf16[256,1024]{1,0:T(8,128)(2,1)S(1)}, u32[]{:S(2)}, u32[]{:S(2)}) collective-permute-start(bf16[256,1024]{1,0:T(8,128)(2,1)} %add_convert_fusion.28), channel_id=1, source_target_pairs={{1,0},{2,1},{3,2},{5,4},{6,5},{7,6},{9,8},{10,9},{11,10},{13,12},{... | collective-permute-start | bytes 1572872 | tf_op jit(solution)/shard_map/ppermute | solution.py:29
  953.3 133.6 %collective-permute-start.148 = (bf16[2,2,768,512]{3,2,1,0:T(8,128)(2,1)}, bf16[2,2,768,512]{3,2,1,0:T(8,128)(2,1)}, u32[]{:S(2)}, u32[]{:S(2)}) collective-permute-start(bf16[2,2,768,512]{3,2,1,0:T(8,128)(2,1)} %get-tuple-element.173), channel_id=1, source_target_pairs={{0,4},{4,0},{8,12},{12,8},{1,5},{5,1},{9,13},{13,9},{2,6},{6,2},{1... | collective-permute-start | bytes 9437192 | tf_op jit(solution)/shard_map/ppermute | solution.py:34
  1000.2 89.9 %collective-permute-start.142 = (bf16[2,2,768,512]{3,2,1,0:T(8,128)(2,1)}, bf16[2,2,768,512]{3,2,1,0:T(8,128)(2,1)}, u32[]{:S(2)}, u32[]{:S(2)}) collective-permute-start(bf16[2,2,768,512]{3,2,1,0:T(8,128)(2,1)} %get-tuple-element.169), channel_id=1, source_target_pairs={{0,4},{4,0},{8,12},{12,8},{1,5},{5,1},{9,13},{13,9},{2,6},{6,2},{1... | collective-permute-start | bytes 9437192 | tf_op jit(solution)/shard_map/ppermute | solution.py:34
  1006.7 87.0 %collective-permute-start.136 = (bf16[2,2,768,512]{3,2,1,0:T(8,128)(2,1)}, bf16[2,2,768,512]{3,2,1,0:T(8,128)(2,1)}, u32[]{:S(2)}, u32[]{:S(2)}) collective-permute-start(bf16[2,2,768,512]{3,2,1,0:T(8,128)(2,1)} %get-tuple-element.160), channel_id=1, source_target_pairs={{0,4},{4,0},{8,12},{12,8},{1,5},{5,1},{9,13},{13,9},{2,6},{6,2},{1... | collective-permute-start | bytes 9437192 | tf_op jit(solution)/shard_map/ppermute | solution.py:34
  1017.7 56.7 %collective-permute-start.81 = (f32[64,34]{0,1:T(8,128)}, f32[64,34]{0,1:T(8,128)}, u32[]{:S(2)}, u32[]{:S(2)}) collective-permute-start(f32[64,34]{0,1:T(8,128)} %copy.84), channel_id=1, source_target_pairs={{0,16},{1,17},{2,18},{3,19},{4,20},{5,21},{6,22},{7,23},{8,24},{9,... | collective-permute-start | bytes 26120 | tf_op jit(solution)/shard_map/ppermute | solution.py:91
  1093.7 116.8 %collective-permute-start.155 = (bf16[1,2,768,512]{3,2,1,0:T(8,128)(2,1)S(1)}, bf16[1,2,768,512]{3,2,1,0:T(8,128)(2,1)S(1)}, u32[]{:S(2)}, u32[]{:S(2)}) collective-permute-start(bf16[1,2,768,512]{3,2,1,0:T(8,128)(2,1)S(1)} %slice.387), channel_id=1, source_target_pairs={{0,8},{4,12},{8,0},{12,4},{1,9},{5,13},{9,1},{13,5},{2,10},{6,14},... | collective-permute-start | bytes 4718600 | tf_op jit(solution)/shard_map/ppermute | solution.py:34
  1098.6 120.5 %collective-permute-start.149 = (bf16[1,2,768,512]{3,2,1,0:T(8,128)(2,1)S(1)}, bf16[1,2,768,512]{3,2,1,0:T(8,128)(2,1)S(1)}, u32[]{:S(2)}, u32[]{:S(2)}) collective-permute-start(bf16[1,2,768,512]{3,2,1,0:T(8,128)(2,1)S(1)} %slice.382), channel_id=1, source_target_pairs={{0,8},{4,12},{8,0},{12,4},{1,9},{5,13},{9,1},{13,5},{2,10},{6,14},... | collective-permute-start | bytes 4718600 | tf_op jit(solution)/shard_map/ppermute | solution.py:34
  1126.7 56.8 %collective-permute-start.101 = (bf16[1,256,1024]{2,1,0:T(8,128)(2,1)S(1)}, bf16[1,256,1024]{2,1,0:T(8,128)(2,1)S(1)}, u32[]{:S(2)}, u32[]{:S(2)}) collective-permute-start(bf16[1,256,1024]{2,1,0:T(8,128)(2,1)S(1)} %slice.360), channel_id=1, source_target_pairs={{0,8},{4,12},{8,0},{12,4},{1,9},{5,13},{9,1},{13,5},{2,10},{6,14},... | collective-permute-start | bytes 1572872 | tf_op jit(solution)/shard_map/ppermute | solution.py:34
  1135.0 93.2 %collective-permute-start.143 = (bf16[1,2,768,512]{3,2,1,0:T(8,128)(2,1)S(1)}, bf16[1,2,768,512]{3,2,1,0:T(8,128)(2,1)S(1)}, u32[]{:S(2)}, u32[]{:S(2)}) collective-permute-start(bf16[1,2,768,512]{3,2,1,0:T(8,128)(2,1)S(1)} %slice.377), channel_id=1, source_target_pairs={{0,8},{4,12},{8,0},{12,4},{1,9},{5,13},{9,1},{13,5},{2,10},{6,14},... | collective-permute-start | bytes 4718600 | tf_op jit(solution)/shard_map/ppermute | solution.py:34
  1140.3 44.7 %collective-permute-start.86 = (bf16[64,1024]{1,0:T(8,128)(2,1)S(1)}, bf16[64,1024]{1,0:T(8,128)(2,1)S(1)}, u32[]{:S(2)}, u32[]{:S(2)}) collective-permute-start(bf16[64,1024]{1,0:T(8,128)(2,1)S(1)} %get-tuple-element.322), channel_id=1, source_target_pairs={{0,1},{1,2},{2,3},{4,5},{5,6},{6,7},{8,9},{9,10},{10,11},{12,13},{... | collective-permute-start | bytes 393224 | tf_op jit(solution)/shard_map/ppermute | solution.py:29
  1221.0 78.7 %collective-permute-start.159 = (bf16[2,768,512]{2,1,0:T(8,128)(2,1)S(1)}, bf16[2,768,512]{2,1,0:T(8,128)(2,1)S(1)}, u32[]{:S(2)}, u32[]{:S(2)}) collective-permute-start(bf16[2,768,512]{2,1,0:T(8,128)(2,1)S(1)} %copy-done.13), channel_id=1, source_target_pairs={{0,16},{1,17},{2,18},{3,19},{4,20},{5,21},{6,22},{7,23},{8,24},{9,... | collective-permute-start | bytes 4718600 | tf_op jit(solution)/shard_map/ppermute | solution.py:91
  1225.4 76.8 %collective-permute-start.153 = (bf16[2,768,512]{2,1,0:T(8,128)(2,1)S(1)}, bf16[2,768,512]{2,1,0:T(8,128)(2,1)S(1)}, u32[]{:S(2)}, u32[]{:S(2)}) collective-permute-start(bf16[2,768,512]{2,1,0:T(8,128)(2,1)S(1)} %copy-done.16), channel_id=1, source_target_pairs={{0,16},{1,17},{2,18},{3,19},{4,20},{5,21},{6,22},{7,23},{8,24},{9,... | collective-permute-start | bytes 4718600 | tf_op jit(solution)/shard_map/ppermute | solution.py:91
  1226.9 76.6 %collective-permute-start.156 = (bf16[2,768,512]{2,1,0:T(8,128)(2,1)S(1)}, bf16[2,768,512]{2,1,0:T(8,128)(2,1)S(1)}, u32[]{:S(2)}, u32[]{:S(2)}) collective-permute-start(bf16[2,768,512]{2,1,0:T(8,128)(2,1)S(1)} %fusion.6), channel_id=1, source_target_pairs={{16,0},{17,1},{18,2},{19,3},{20,4},{21,5},{22,6},{23,7},{24,8},{25... | collective-permute-start | bytes 4718600 | tf_op jit(solution)/shard_map/ppermute | solution.py:91
  1228.2 76.7 %collective-permute-start.150 = (bf16[2,768,512]{2,1,0:T(8,128)(2,1)S(1)}, bf16[2,768,512]{2,1,0:T(8,128)(2,1)}, u32[]{:S(2)}, u32[]{:S(2)}) collective-permute-start(bf16[2,768,512]{2,1,0:T(8,128)(2,1)S(1)} %fusion.4), channel_id=1, source_target_pairs={{16,0},{17,1},{18,2},{19,3},{20,4},{21,5},{22,6},{23,7},{24,8},{25... | collective-permute-start | bytes 4718600 | tf_op jit(solution)/shard_map/ppermute | solution.py:91
  1250.5 45.8 %collective-permute-start.108 = (bf16[64,1024]{1,0:T(8,128)(2,1)S(1)}, bf16[64,1024]{1,0:T(8,128)(2,1)S(1)}, u32[]{:S(2)}, u32[]{:S(2)}) collective-permute-start(bf16[64,1024]{1,0:T(8,128)(2,1)S(1)} %fusion.55), channel_id=1, source_target_pairs={{16,0},{17,1},{18,2},{19,3},{20,4},{21,5},{22,6},{23,7},{24,8},{25... | collective-permute-start | bytes 393224 | tf_op jit(solution)/shard_map/ppermute | solution.py:91
  1299.7 59.6 %collective-permute-start.141 = (bf16[2,768,512]{2,1,0:T(8,128)(2,1)S(1)}, bf16[2,768,512]{2,1,0:T(8,128)(2,1)}, u32[]{:S(2)}, u32[]{:S(2)}) collective-permute-start(bf16[2,768,512]{2,1,0:T(8,128)(2,1)S(1)} %copy-done.15), channel_id=1, source_target_pairs={{0,16},{1,17},{2,18},{3,19},{4,20},{5,21},{6,22},{7,23},{8,24},{9,... | collective-permute-start | bytes 4718600 | tf_op jit(solution)/shard_map/ppermute | solution.py:91
  1302.2 57.1 %collective-permute-start.144 = (bf16[2,768,512]{2,1,0:T(8,128)(2,1)S(1)}, bf16[2,768,512]{2,1,0:T(8,128)(2,1)}, u32[]{:S(2)}, u32[]{:S(2)}) collective-permute-start(bf16[2,768,512]{2,1,0:T(8,128)(2,1)S(1)} %fusion.2), channel_id=1, source_target_pairs={{16,0},{17,1},{18,2},{19,3},{20,4},{21,5},{22,6},{23,7},{24,8},{25... | collective-permute-start | bytes 4718600 | tf_op jit(solution)/shard_map/ppermute | solution.py:91
  1303.5 64.5 %collective-permute-start.138 = (bf16[2,768,512]{2,1,0:T(8,128)(2,1)}, bf16[2,768,512]{2,1,0:T(8,128)(2,1)}, u32[]{:S(2)}, u32[]{:S(2)}) collective-permute-start(bf16[2,768,512]{2,1,0:T(8,128)(2,1)} %fusion), channel_id=1, source_target_pairs={{16,0},{17,1},{18,2},{19,3},{20,4},{21,5},{22,6},{23,7},{24,8},{25... | collective-permute-start | bytes 4718600 | tf_op jit(solution)/shard_map/ppermute | solution.py:91
  (206 other events, 3967.5 us)
Sparse Core Ops, SparseCore 0:
  679.5 57.0 reduce-scatter.8
  1016.0 56.8 reduce-scatter.6

commit v2 on v1

--- a/solution.py
+++ b/solution.py
@@ -34,6 +34,10 @@
     return lax.ppermute(value, axis, [(source, source ^ bit) for source in range(count)])
 
 
+def tie(*values):
+    return lax.optimization_barrier(values)
+
+
 def line_gather(block):
     ups, downs = [], []
     up, down = block, block
@@ -45,7 +49,7 @@
     return ups, downs
 
 
-def line_reduce(parts):
+def line_reduce(parts, ties={}, marks=None):
     ranks = lax.axis_size("expert")
     me = lax.axis_index("expert")
 
@@ -58,45 +62,54 @@
         down_part = pick(me - ranks + step)
         up = up_part if up is None else (up.astype(f32) + up_part.astype(f32)).astype(bf16)
         down = down_part if down is None else (down.astype(f32) + down_part.astype(f32)).astype(bf16)
+        if step in ties:
+            up, down, *ties[step] = tie(up, down, *ties[step])
         up = shifted(up, "expert", 1, range(0, step))
         down = shifted(down, "expert", -1, range(ranks - step, ranks))
+        if marks is not None:
+            marks.append([up, down])
     return pick(me).astype(f32) + up.astype(f32) + down.astype(f32)
 
 
-def dp_bits():
-    bits, bit = [], 1
-    while bit < lax.axis_size("dp"):
+def dp_size():
+    return lax.axis_size("far") * lax.axis_size("near")
+
+
+def dp_swapped(value, bit):
+    return swapped(value, "near", 1) if bit == 1 else swapped(value, "far", bit // 2)
+
+
+def fetch_bits():
+    bits, bit = [], dp_size() // 2
+    while bit >= 1:
         bits.append(bit)
-        bit *= 2
+        bit //= 2
     return bits
 
 
-def fetch_pieces(piece):
-    pieces = {0: swapped(piece, "section", 1)}
-    for bit in reversed(dp_bits()):
+def spread_pieces(piece, before=None):
+    pieces = {0: piece}
+    for bit in fetch_bits():
         for k in list(pieces):
-            pieces[k | bit] = swapped(pieces[k], "dp", bit)
+            if before is not None and k == max(pieces):
+                pieces[k] = before(pieces[k], bit)
+            pieces[k | bit] = dp_swapped(pieces[k], bit)
     return [pieces[k] for k in range(len(pieces))]
 
 
-def dp_reduce(keep, send):
-    for bit in dp_bits():
-        total = (keep.astype(f32) + swapped(send, "dp", bit).astype(f32)).astype(bf16)
-        if total.shape[0] > 1:
-            keep, send = total[0::2], total[1::2]
-    return total[0]
-
-
-def to_owner(value, layer):
-    return lax.ppermute(value, "section", [(1 - layer, layer)])
-
-
-def call(kernel, out_shape, in_specs, out_specs, scratch, grid=None, flops=0, bytes_accessed=0, name=None):
+def near_sum(keep, send):
+    return (keep.astype(f32) + swapped(send, "near", 1).astype(f32)).astype(bf16)
+
+
+def call(
+    kernel, out_shape, in_specs, out_specs, scratch, grid=None, flops=0, bytes_accessed=0, name=None, waits=()
+):
     extra = {} if grid is None else {"grid": grid}
-    return pl.pallas_call(
-        kernel,
+    begin, end = len(in_specs), len(in_specs) + len(waits)
+    run = pl.pallas_call(
+        lambda *refs: kernel(*refs[:begin], *refs[end:]),
         out_shape=out_shape,
-        in_specs=in_specs,
+        in_specs=[*in_specs, *[ANY] * len(waits)],
         out_specs=out_specs,
         scratch_shapes=scratch,
         compiler_params=pltpu.CompilerParams(vmem_limit_bytes=VMEM_BYTES),
@@ -104,6 +117,7 @@
         name=name,
         **extra,
     )
+    return lambda *args: run(*args, *waits)
 
 
 SMEM = pl.BlockSpec(memory_space=pltpu.SMEM)
@@ -157,7 +171,6 @@
 
 def load_experts(info, owns, chunks, expert, slot, buffers, sems):
     gate_buf, up_buf, down_buf = buffers
-    per_chunk = chunks[0][0].shape[0]
     pieces = len(chunks[0])
     wide = gate_buf.shape[1] // pieces
     narrow = down_buf.shape[1] // pieces
@@ -168,11 +181,13 @@
         for own, buf, index in zip(owns, buffers, range(3)):
             pltpu.make_async_copy(own.at[expert], buf.at[slot], sems.at[slot, index]).start()
 
-    for c, chunk in enumerate(chunks):
-
-        @pl.when((info[0] == 0) & (expert // per_chunk == c))
+    begin = 0
+    for chunk in chunks:
+        first, begin = begin, begin + chunk[0].shape[0]
+
+        @pl.when((info[0] == 0) & (expert >= first) & (expert < begin))
         def _():
-            local = expert - c * per_chunk
+            local = expert - first
             for k, piece in enumerate(chunk):
                 owner = info[1] ^ k
                 row = pl.multiple_of(owner * wide, wide)
@@ -198,16 +213,17 @@
 def load_line(info, own, ups, downs, target, sem):
     ranks = target.shape[0]
     me = info[2]
-    pltpu.make_async_copy(own, target.at[me], sem).start()
+    columns = pl.ds(0, target.shape[2])
+    pltpu.make_async_copy(own.at[:, columns], target.at[me], sem).start()
     for s in range(1, ranks):
 
         @pl.when(me >= s)
         def _():
-            pltpu.make_async_copy(ups[s - 1], target.at[me - s], sem).start()
+            pltpu.make_async_copy(ups[s - 1].at[:, columns], target.at[me - s], sem).start()
 
         @pl.when(me < s)
         def _():
-            pltpu.make_async_copy(downs[ranks - s - 1], target.at[me - s + ranks], sem).start()
+            pltpu.make_async_copy(downs[ranks - s - 1].at[:, columns], target.at[me - s + ranks], sem).start()
 
 
 def wait_line(target, sem):
@@ -218,16 +234,16 @@
     pieces = 2 * keep.shape[0]
     rows = value.shape[0] // pieces
     for p in range(pieces):
-        k = info[1] ^ p
         part = value[p * rows : (p + 1) * rows].astype(keep.dtype)
-
-        @pl.when(k % 2 == 0)
+        same = info[1] % 2 == p % 2
+
+        @pl.when(same)
         def _():
-            keep[(k // 2,) + place] = part
-
-        @pl.when(k % 2 == 1)
+            keep[(p // 2,) + place] = part
+
+        @pl.when(jnp.logical_not(same))
         def _():
-            send[(k // 2,) + place] = part
+            send[(p // 2,) + place] = part
 
 
 def rms(values):
@@ -261,6 +277,71 @@
 
 def one_head(tile, which, upper):
     return jnp.where(upper, tile, 0.0) if which == 1 else jnp.where(upper, 0.0, tile)
+
+
+def pack_dense_kernel(info, *refs):
+    begin = 0
+    for matrix in refs[:-1]:
+        width = matrix.shape[1]
+        refs[-1][:, begin : begin + width] = matrix[...]
+        begin += width
+
+
+def pack_experts_kernel(info, gate, up, down, out):
+    wide, narrow = gate.shape[1], down.shape[1]
+    half = out.shape[2]
+    out[0, :wide] = gate[0]
+    out[0, wide : 2 * wide] = up[0]
+    out[0, 2 * wide : 2 * wide + narrow] = down[0, :, :half]
+    out[0, 2 * wide + narrow :] = down[0, :, half:]
+
+
+def packed(kernel, out_shape, grid, in_specs, out_specs, name):
+    size = 4 * functools.reduce(lambda a, b: a * b, out_shape.shape)
+    return pl.pallas_call(
+        kernel,
+        out_shape=out_shape,
+        grid_spec=pltpu.PrefetchScalarGridSpec(
+            num_scalar_prefetch=1, grid=grid, in_specs=in_specs, out_specs=out_specs
+        ),
+        cost_estimate=pl.CostEstimate(flops=0, bytes_accessed=size, transcendentals=0),
+        name=name,
+    )
+
+
+def pack_dense(info, matrices, pieces):
+    rows = matrices[0].shape[0] // pieces
+    total = sum(matrix.shape[1] for matrix in matrices)
+    return packed(
+        pack_dense_kernel,
+        struct((rows, total), bf16),
+        (1,),
+        [pl.BlockSpec((rows, matrix.shape[1]), lambda i, info: (info[1], 0)) for matrix in matrices],
+        pl.BlockSpec((rows, total), lambda i, info: (0, 0)),
+        "pack_dense",
+    )(info, *matrices)
+
+
+def pack_experts(info, matrices, pieces, first, count):
+    gate, up, down = matrices
+    wide, narrow = gate.shape[1] // pieces, down.shape[1] // pieces
+    hidden, width = gate.shape[2], down.shape[2]
+
+    def own(e, info):
+        return (first + e, info[1], 0)
+
+    return packed(
+        pack_experts_kernel,
+        struct((count, 2 * wide + 2 * narrow, hidden), bf16),
+        (count,),
+        [
+            pl.BlockSpec((1, wide, hidden), own),
+            pl.BlockSpec((1, wide, hidden), own),
+            pl.BlockSpec((1, narrow, width), own),
+        ],
+        pl.BlockSpec((1, 2 * wide + 2 * narrow, hidden), lambda e, info: (e, 0, 0)),
+        "pack_experts",
+    )(info, gate, up, down)
 
 
 def project_kernel(pieces, info, x, gain, cosine, sine, w_query, w_key, w_value, *rest):
@@ -418,9 +499,12 @@
     d_normed[...] = dot(d_query[...], weights[...], 1, 1)
 
 
-def keyval_back_kernel(pieces, info, x, gain, d_own, d_others, d_normed, d_middle, cosine, sine, w_key, w_value, *rest):
+def keyval_back_kernel(
+    pieces, info, x, gain, d_own, d_others, d_normed, d_middle, cosine, sine, grad_router, grad_gain_moe,
+    w_key, w_value, *rest,
+):
     parts = rest[:pieces]
-    d_x, keep, send, grad_gain, weights, d_pre, sem = rest[pieces:]
+    d_x, keep, send, weights, d_pre, sem = rest[pieces:]
     load_dense(info, (w_key, w_value), parts, x.shape[1], weights.shape[1], weights, sem)
     hidden = x[...].astype(f32)
     scale = rms(hidden)
@@ -435,13 +519,20 @@
         d_pre[:, place : place + LANES] = tile.astype(bf16)
     wait_dense(weights, sem)
     total = d_normed[...] + dot(d_pre[...], weights[...], 1, 1)
-    grad_gain[...] = jnp.sum(total * normal, axis=0, keepdims=True)
+    grad_gain = jnp.sum(total * normal, axis=0, keepdims=True)
+    tall = jnp.concatenate(
+        [grad_router[...], jnp.zeros((LANES - EXPERTS, total.shape[1]), f32)], axis=0
+    )
+    row = lax.broadcasted_iota(jnp.int32, tall.shape, 0)
+    tall = jnp.where(row == EXPERTS, grad_gain_moe[...], jnp.where(row == EXPERTS + 1, grad_gain, tall))
     d_norm = total * gain[...]
     d_x[...] = (
         d_middle[...]
         + scale * (d_norm - normal * jnp.mean(d_norm * normal, axis=1, keepdims=True))
     ).astype(bf16)
-    write_pieces(info, dot(normed, d_pre[...], 0, 0), keep, send, ())
+    both = 2 * width
+    write_pieces(info, dot(normed, d_pre[...], 0, 0), keep, send, (slice(None), slice(0, both)))
+    write_pieces(info, tall.T, keep, send, (slice(None), slice(both, both + LANES)))
 
 
 def slot_rows(info, table, local, experts_here):
@@ -612,34 +703,51 @@
         grad_router[...] = router_total
 
 
-def expert_grads_kernel(info, rows, grad_rows, d_gate, d_up, activated, keep, send):
-    capacity, width = rows.shape[1], rows.shape[2]
-    mine = rows[...].reshape(rows.shape[0] * capacity, width)
-    incoming = grad_rows[...].reshape(rows.shape[0] * capacity, width)
-    pieces = 2 * keep.shape[0]
-    wide = width // pieces
-    narrow = activated.shape[2] // pieces
-    half = width // 2
-    write_pieces(info, dot(mine, d_gate[0], 0, 0), keep, send, (0, slice(0, wide)))
-    write_pieces(info, dot(mine, d_up[0], 0, 0), keep, send, (0, slice(wide, 2 * wide)))
-    down = dot(activated[0], incoming, 0, 0)
-    for side in range(2):
-        begin = 2 * wide + side * narrow
-        write_pieces(
-            info, down[:, side * half : (side + 1) * half], keep, send, (0, slice(begin, begin + narrow))
-        )
-
-
-def layer_forward(x, weights, tables, info, routes):
-    (gain_attn, gain_moe, router, owns, dense_parts, expert_parts) = weights
-    w_query, w_key, w_value, w_out, w_gate, w_up, w_down = owns
-    cosine, sine, query_docs, key_docs, usable, reach = tables
+def expert_grads_kernel(info, *refs):
+    *arrays, out = refs
+    ranks, capacity, width = arrays[0].shape
+    pairs = out.shape[0]
+    hidden = arrays[4].shape[2]
+    wide, narrow, half = width // (2 * pairs), hidden // (2 * pairs), width // 2
+    sides = [arrays[:5], arrays[5:]]
+    incoming = [grad_rows[...].reshape(ranks * capacity, width) for rows, grad_rows, *_ in sides]
+    for pair in range(pairs):
+        owner = 2 * pair + info[1] % 2
+        column = pl.multiple_of(owner * wide, wide)
+        gate = up = None
+        for rows, grad_rows, d_gate, d_up, activated in sides:
+            mine = rows[:, :, pl.ds(column, wide)].reshape(ranks * capacity, wide)
+            gate_term, up_term = dot(mine, d_gate[0], 0, 0), dot(mine, d_up[0], 0, 0)
+            gate = gate_term if gate is None else gate + gate_term
+            up = up_term if up is None else up + up_term
+        out[pair, 0, :wide] = gate.astype(bf16)
+        out[pair, 0, wide : 2 * wide] = up.astype(bf16)
+        if narrow % LANES == 0:
+            column = pl.multiple_of(owner * narrow, narrow)
+            down = sum(
+                dot(side[4][0, :, pl.ds(column, narrow)], rows, 0, 0) for side, rows in zip(sides, incoming)
+            ).astype(bf16)
+            out[pair, 0, 2 * wide : 2 * wide + narrow] = down[:, :half]
+            out[pair, 0, 2 * wide + narrow :] = down[:, half:]
+    if narrow % LANES:
+        down = sum(dot(side[4][0], rows, 0, 0) for side, rows in zip(sides, incoming)).astype(bf16)
+        for p in range(2 * pairs):
+
+            @pl.when(info[1] % 2 == p % 2)
+            def _():
+                part = down[p * narrow : (p + 1) * narrow]
+                out[p // 2, 0, 2 * wide : 2 * wide + narrow] = part[:, :half]
+                out[p // 2, 0, 2 * wide + narrow :] = part[:, half:]
+
+
+def layer_project(x, weights, tables, info, waits=()):
+    (gain_attn, gain_moe, router, owns, dense_parts) = weights
+    w_query, w_key, w_value, w_out = owns[:4]
+    cosine, sine = tables[:2]
     rows, width = x.shape
-    ranks = lax.axis_size("expert")
-    pieces = lax.axis_size("dp")
+    pieces = dp_size()
     kv_width = 2 * KV_HEADS * HEAD_DIM
-    keys = (reach + 1) * rows
-    query, keyval = call(
+    return call(
         functools.partial(project_kernel, pieces),
         (struct((rows, width), bf16), struct((rows, kv_width), bf16)),
         [SMEM] + [VMEM] * 4 + [ANY] * (3 + pieces),
@@ -648,12 +756,27 @@
         flops=2 * rows * width * (width + kv_width),
         bytes_accessed=2 * width * (width + kv_width),
         name="project",
+        waits=waits,
     )(info, x, gain_attn, cosine, sine, w_query, w_key, w_value, *dense_parts)
+
+
+def earlier_keys(keyval, tables):
     earlier, moving = [], keyval
-    for _ in range(reach):
+    for _ in range(tables[-1]):
         moving = shifted(moving, "expert", 1)
         earlier.append(moving)
-    mixed, log_total, middle, routed = call(
+    return earlier
+
+
+def layer_attend(x, query, keyval, earlier, weights, tables, info, waits=()):
+    (gain_attn, gain_moe, router, owns, dense_parts) = weights
+    w_out = owns[3]
+    cosine, sine, query_docs, key_docs, usable, reach = tables
+    rows, width = x.shape
+    pieces = dp_size()
+    kv_width = 2 * KV_HEADS * HEAD_DIM
+    keys = (reach + 1) * rows
+    return call(
         functools.partial(attend_kernel, pieces, reach),
         (
             struct((rows, width), bf16),
@@ -673,8 +796,19 @@
         flops=16 * rows * keys * width,
         bytes_accessed=2 * width * width,
         name="attend",
+        waits=waits,
     )(info, query, keyval, *earlier, query_docs, key_docs, x, gain_moe, w_out, *dense_parts)
-    ups, downs = line_gather(routed)
+
+
+def layer_experts(x, query, keyval, earlier, attended, line_blocks, weights, tables, info, routes, waits=()):
+    (gain_attn, gain_moe, router, owns, dense_parts, expert_parts) = weights
+    w_gate, w_up, w_down = owns[4:]
+    usable = tables[4]
+    mixed, log_total, middle, routed = attended
+    ups, downs = line_blocks
+    rows, width = x.shape
+    pieces = dp_size()
+    ranks = lax.axis_size("expert")
     experts_here, _, hidden = w_gate.shape
     capacity = rows * TOPK // EXPERTS
     slots = experts_here * capacity
@@ -705,23 +839,27 @@
         flops=6 * experts_here * ranks * capacity * width * hidden,
         bytes_accessed=6 * experts_here * width * hidden,
         name="experts",
+        waits=waits,
     )(
         info, routed, *ups, *downs, routes, usable, router, w_gate, w_up, w_down,
         *[piece for chunk in expert_parts for piece in chunk],
     )
-    result = (middle + line_reduce(sums)).astype(bf16)
     kept = (x, query, keyval, earlier, mixed, log_total, middle, everyone, expert_rows, gates, codes, gate_pre, up_pre)
-    return result, kept
-
-
-def layer_backward(grad, grad_line, kept, weights, tables, info):
+    return middle, sums, kept
+
+
+def layer_result(middle, sums, ties={}):
+    return (middle + line_reduce(sums, ties)).astype(bf16)
+
+
+def layer_backward(layer, grad, grad_line, kept, weights, tables, info, waits={}):
     (gain_attn, gain_moe, router, owns, dense_parts, expert_parts) = weights
     w_query, w_key, w_value, w_out, w_gate, w_up, w_down = owns
     cosine, sine, query_docs, key_docs, usable, reach = tables
     (x, query, keyval, earlier, mixed, log_total, middle, everyone, expert_rows, gates, codes, gate_pre, up_pre) = kept
     rows, width = x.shape
     ranks = lax.axis_size("expert")
-    pieces = lax.axis_size("dp")
+    pieces = dp_size()
     kv_width = 2 * KV_HEADS * HEAD_DIM
     keys = (reach + 1) * rows
     experts_here, _, hidden = w_gate.shape
@@ -756,33 +894,49 @@
         flops=6 * experts_here * ranks * capacity * width * hidden,
         bytes_accessed=6 * experts_here * width * hidden,
         name="experts_back",
+        waits=waits.get("experts_back", ()),
     )(
         info, grad, *ups, *downs, everyone, gates, codes, router, gate_pre, up_pre, w_gate, w_up, w_down,
         *[piece for chunk in expert_parts for piece in chunk],
     )
-    chunk_count = len(expert_parts)
-    per_chunk = experts_here // chunk_count
     wide, narrow = width // pieces, hidden // pieces
     piece_rows = 2 * wide + 2 * narrow
-    expert_sums = []
-    for c in range(chunk_count):
+    chunk_count = min(2 if layer == 1 else 4, experts_here)
+    per_chunk = experts_here // chunk_count
+    marks = []
+    if "reduce" in waits:
+        sums, *waits["reduce"] = tie(sums, *waits["reduce"])
+    d_routed = line_reduce(sums, marks=marks)
+    marks += marks[-1:] * 2
+    own_terms = (expert_rows, grad_rows, d_gate, d_up, activated)
+    near_terms = [swapped(term, "near", 1) for term in own_terms]
+    pairs = []
+
+    def gradients(*others):
+        c = len(pairs)
         place = functools.partial(lambda c, e: (c * per_chunk + e, 0, 0), c)
         row_place = functools.partial(lambda c, e: (0, c * per_chunk + e, 0), c)
-        keep, send = call(
-            expert_grads_kernel,
-            (struct((pieces // 2, per_chunk, piece_rows, hidden), bf16),) * 2,
-            [SMEM]
-            + [pl.BlockSpec((ranks, capacity, width), row_place)] * 2
-            + [pl.BlockSpec((1, ranks * capacity, hidden), place)] * 3,
-            (pl.BlockSpec((pieces // 2, 1, piece_rows, hidden), lambda e: (0, e, 0, 0)),) * 2,
-            [],
-            grid=(per_chunk,),
-            flops=6 * per_chunk * ranks * capacity * width * hidden,
-            bytes_accessed=6 * per_chunk * width * hidden,
-            name="expert_grads",
-        )(info, expert_rows, grad_rows, d_gate, d_up, activated)
-        expert_sums.append(dp_reduce(keep, send))
-    d_routed = line_reduce(sums)
+        in_specs = [pl.BlockSpec((ranks, capacity, width), row_place)] * 2 + [
+            pl.BlockSpec((1, ranks * capacity, hidden), place)
+        ] * 3
+        pairs.append(
+            call(
+                expert_grads_kernel,
+                struct((pieces // 2, per_chunk, piece_rows, hidden), bf16),
+                [SMEM] + in_specs * 2,
+                pl.BlockSpec((pieces // 2, 1, piece_rows, hidden), lambda e: (0, e, 0, 0)),
+                [],
+                grid=(per_chunk,),
+                flops=6 * per_chunk * ranks * capacity * width * hidden,
+                bytes_accessed=9 * per_chunk * width * hidden,
+                name="expert_grads",
+                waits=[*others, *pairs[-1:]],
+            )(info, *own_terms, *near_terms)
+        )
+
+    gradients(*marks[0], *waits.get("expert_grads", ()))
+    if layer == 0:
+        gradients(*marks[1])
     outs = call(
         functools.partial(attend_back_kernel, pieces, reach),
         (
@@ -807,13 +961,15 @@
         flops=40 * rows * keys * width,
         bytes_accessed=2 * width * width,
         name="attend_back",
+        waits=pairs[:1],
     )(
-        info, d_routed, grad, middle, gain_moe, mixed, query, log_total, keyval, *earlier,
+        info, d_routed, grad[:, :width], middle, gain_moe, mixed, query, log_total, keyval, *earlier,
         query_docs, key_docs, cosine, sine, w_out, *dense_parts,
     )
     d_middle, d_query, d_own = outs[:3]
     d_earlier = outs[3 : 3 + reach]
     out_keep, out_send, grad_gain_moe = outs[3 + reach :]
+    gradients(d_query)
     moving = d_earlier[reach - 1]
     for s in reversed(range(reach)):
         moving = shifted(moving, "expert", -1)
@@ -829,12 +985,16 @@
         flops=4 * rows * width * width,
         bytes_accessed=4 * width * width,
         name="query_back",
+        waits=pairs[-1:],
     )(info, x, gain_attn, d_query, w_query, *dense_parts)
-    d_x, kv_keep, kv_send, grad_gain_attn = call(
+    if layer == 0:
+        gradients(d_normed)
+    kv_struct = struct((pieces // 2, width // pieces, kv_width + LANES), bf16)
+    d_x, kv_keep, kv_send = call(
         functools.partial(keyval_back_kernel, pieces),
-        (struct((rows, width), bf16), piece_struct, piece_struct, struct((1, width), f32)),
-        [SMEM] + [VMEM] * 8 + [ANY] * (2 + pieces),
-        (VMEM,) * 4,
+        (struct((rows, width), bf16), kv_struct, kv_struct),
+        [SMEM] + [VMEM] * 10 + [ANY] * (2 + pieces),
+        (VMEM,) * 3,
         [
             pltpu.VMEM((width, kv_width), bf16),
             pltpu.VMEM((rows, kv_width), bf16),
@@ -843,16 +1003,20 @@
         flops=4 * rows * width * kv_width,
         bytes_accessed=4 * width * kv_width,
         name="keyval_back",
+        waits=pairs[-1:] if layer == 0 else (),
     )(
-        info, x, gain_attn, d_own, moving, d_normed, d_middle, cosine, sine, w_key, w_value, *dense_parts,
-    )
-    dense_sums = []
-    for keep, send in ((out_keep, out_send), (query_keep, query_send), (kv_keep, kv_send)):
-        mine = dp_reduce(keep, send)
-        dense_sums.append(line_reduce(mine.reshape(ranks, -1, width)))
-    small = jnp.concatenate([grad_router, grad_gain_moe, grad_gain_attn], axis=0).T
-    small = lax.psum_scatter(small, ("dp", "expert"), scatter_dimension=0, tiled=True)
-    return d_x, expert_sums, dense_sums, small
+        info, x, gain_attn, d_own, moving, d_normed, d_middle, cosine, sine, grad_router, grad_gain_moe,
+        w_key, w_value, *dense_parts,
+    )
+    dense = jnp.concatenate(
+        [
+            near_sum(keep, send)
+            for keep, send in ((out_keep, out_send), (query_keep, query_send), (kv_keep, kv_send))
+        ],
+        axis=2,
+    )
+    expert_sums = [lax.psum_scatter(pair, "far", scatter_dimension=0, tiled=True)[0] for pair in pairs]
+    return d_x, expert_sums, dense
 
 
 def doc_ids(lengths, positions):
@@ -866,9 +1030,9 @@
 ):
     rows, width = inputs.shape[2:]
     ranks = lax.axis_size("expert")
-    pieces = lax.axis_size("dp")
+    pieces = dp_size()
     section = lax.axis_index("section")
-    place = lax.axis_index("dp")
+    place = lax.axis_index("far") * 2 + lax.axis_index("near")
     line = lax.axis_index("expert")
     experts_here, _, hidden = w_gate.shape[1:]
     first = section == 0
@@ -884,46 +1048,41 @@
     lengths = mine(doc_lengths[:, 0])
 
     wide, narrow = width // pieces, hidden // pieces
-
-    def rows_of(matrix, axis, size):
-        return lax.dynamic_slice_in_dim(matrix, place * size, size, axis)
-
-    dense_piece = jnp.concatenate(
-        [rows_of(w[0], 0, wide) for w in (w_query, w_key, w_value, w_out)], axis=1
-    )
-    dense_parts = fetch_pieces(dense_piece)
+    where = jnp.stack([jnp.int32(0), place, line]).astype(jnp.int32)
+    dense_own = (w_query[0], w_key[0], w_value[0], w_out[0])
     small = jnp.concatenate([w_router[0].T.astype(f32), gain_attn, gain_moe], axis=0)
     other_small = swapped(small, "section", 1)
-    chunk_count = 4 if experts_here % 4 == 0 else 1
-    per_chunk = experts_here // chunk_count
-    expert_parts = []
-    for c in range(chunk_count):
-        span = slice(c * per_chunk, (c + 1) * per_chunk)
-        down = rows_of(w_down[0, span], 1, narrow)
-        piece = jnp.concatenate(
-            [
-                rows_of(w_gate[0, span], 1, wide),
-                rows_of(w_up[0, span], 1, wide),
-                down[:, :, : width // 2],
-                down[:, :, width // 2 :],
-            ],
-            axis=1,
-        )
-        expert_parts.append(fetch_pieces(piece))
-
-    owns = (w_query[0], w_key[0], w_value[0], w_out[0], w_gate[0], w_up[0], w_down[0])
     here = routes[0, :, 0]
     my_routes = mine(here)
     other_routes = swapped(other(here), "section", 1)
-    both = jnp.stack([jnp.where(first, my_routes, other_routes), jnp.where(first, other_routes, my_routes)])
-    both = lax.all_gather(both, "expert", axis=1, tiled=True).transpose(0, 2, 1)
-    layers, infos = [], []
-    for layer in range(2):
-        held = section == layer
-        table = jnp.where(held, small, other_small)
-        layers.append((table[EXPERTS : EXPERTS + 1], table[EXPERTS + 1 :], table[:EXPERTS].astype(bf16), owns, dense_parts, expert_parts))
-        infos.append(jnp.stack([held.astype(jnp.int32), place, line]).astype(jnp.int32))
-
+    dense_piece, other_small, other_routes = tie(pack_dense(where, dense_own, pieces), other_small, other_routes)
+    dense_first_hop = swapped(dense_piece, "section", 1)
+    both = jnp.concatenate(
+        [jnp.where(first, my_routes, other_routes), jnp.where(first, other_routes, my_routes)], axis=1
+    )
+    named = jnp.pad(both.astype(bf16), ((0, 0), (0, LANES - 2 * TOPK)))
+    top_named = jnp.concatenate([top, named], axis=1)
+    top_line = line_gather(top_named)
+    dense_first_hop, top_line[0][0], top_line[1][0] = tie(dense_first_hop, top_line[0][0], top_line[1][0])
+    cyclic = [top_named] + [
+        jnp.where(line >= s, top_line[0][s - 1], top_line[1][ranks - s - 1]) for s in range(1, ranks)
+    ]
+    cyclic = jnp.stack([block[:, width : width + 2 * TOPK] for block in cyclic[::-1]] * 2)
+    both = lax.dynamic_slice_in_dim(cyclic, ranks - 1 - line, ranks, 0).reshape(ranks * rows, 2 * TOPK)
+    both = both.T.astype(jnp.int32).reshape(2, TOPK, ranks * rows)
+    def with_line(piece, bit):
+        if bit == 1:
+            piece, top_line[0][-1], top_line[1][-1] = tie(piece, top_line[0][-1], top_line[1][-1])
+        return piece
+
+    dense_parts = spread_pieces(dense_first_hop, with_line)
+    sizes = [2, 2, 2, 1, 1] if experts_here == 8 else [1] * experts_here
+    packs = [
+        pack_experts(where, (w_gate[0], w_up[0], w_down[0]), pieces, sum(sizes[:c]), size)
+        for c, size in enumerate(sizes)
+    ]
+
+    owns = (w_query[0], w_key[0], w_value[0], w_out[0], w_gate[0], w_up[0], w_down[0])
     offset = line * rows
     reach = min((WINDOW - 1) // rows + 1, ranks - 1)
     positions = offset + jnp.arange(rows, dtype=jnp.int32)
@@ -939,30 +1098,106 @@
     sine = jnp.concatenate([-sine, sine, -sine, sine], axis=1)
     tables = (cosine, sine, query_docs, key_docs, usable, reach)
 
-    top_line = line_gather(top)
-    between, kept_first = layer_forward(x, layers[0], tables, infos[0], both[0])
-    final, kept_second = layer_forward(between, layers[1], tables, infos[1], both[1])
-    d_between, experts_second, dense_second, small_second = layer_backward(
-        top, top_line, kept_second, layers[1], tables, infos[1]
-    )
-    d_first, experts_first, dense_first, small_first = layer_backward(
-        d_between, line_gather(d_between), kept_first, layers[0], tables, infos[0]
-    )
-
-    def by_section(of_first, of_second):
+    weights = []
+    infos = []
+    for layer in range(2):
+        held = section == layer
+        table = jnp.where(held, small, other_small)
+        vectors = (table[EXPERTS : EXPERTS + 1], table[EXPERTS + 1 :], table[:EXPERTS].astype(bf16))
+        weights.append(vectors + (owns, dense_parts))
+        infos.append(jnp.stack([held.astype(jnp.int32), place, line]).astype(jnp.int32))
+
+    marks = []
+
+    def next_chunk(*mark):
+        chunk, = crossing[:1]
+        del crossing[0]
+        if mark:
+            chunk, seen = tie(chunk, *mark)
+            marks.append(seen)
+        expert_parts.append(spread_pieces(chunk))
+        if packs:
+            piece, _ = tie(packs.pop(0), chunk)
+            crossing.append(swapped(piece, "section", 1))
+
+    expert_parts = []
+    piece, dense_gone = tie(packs.pop(0), dense_first_hop)
+    crossing = [swapped(piece, "section", 1)]
+    if packs:
+        crossing.append(swapped(packs.pop(0), "section", 1))
+    query, keyval = layer_project(x, weights[0], tables, infos[0], [dense_gone])
+    next_chunk()
+    earlier = earlier_keys(keyval, tables)
+    next_chunk(earlier[-1])
+    attended = layer_attend(x, query, keyval, earlier, weights[0], tables, infos[0])
+    line_blocks = line_gather(attended[-1])
+    for block in line_blocks[0]:
+        if crossing:
+            next_chunk(block)
+    while crossing:
+        next_chunk()
+    layers = [weight + (expert_parts,) for weight in weights]
+    middle, sums, kept_first = layer_experts(
+        x, query, keyval, earlier, attended, line_blocks, layers[0], tables, infos[0], both[0], marks
+    )
+    between = layer_result(middle, sums)
+    query, keyval = layer_project(between, weights[1], tables, infos[1])
+    earlier = earlier_keys(keyval, tables)
+    attended = layer_attend(between, query, keyval, earlier, weights[1], tables, infos[1])
+    middle, sums, kept_second = layer_experts(
+        between, query, keyval, earlier, attended, line_gather(attended[-1]), layers[1], tables, infos[1], both[1]
+    )
+    d_between, experts_second, dense_second = layer_backward(
+        1, top_named, top_line, kept_second, layers[1], tables, infos[1]
+    )
+    between_line = line_gather(d_between)
+    half = experts_second[0].shape[0] // 2
+    def to_give(of_first, of_second):
+        return jnp.where(first, of_second, of_first)
+
+    dense_second = lax.psum_scatter(dense_second, "far", scatter_dimension=0, tiled=True)[0]
+    waits = {"experts_back": experts_second[:1], "reduce": experts_second[1:], "expert_grads": [dense_second]}
+    d_first, experts_first, dense_first = layer_backward(
+        0, d_between, between_line, kept_first, layers[0], tables, infos[0], waits
+    )
+    experts_second[1:] = waits["reduce"]
+    second = [part for of_second in experts_second for part in (of_second[:half], of_second[half:])]
+    sums, d_first, dense_first = tie(sums, d_first, dense_first)
+    got = [swapped(to_give(a, b), "section", 1) for a, b in zip(experts_first[:2], second)]
+    for bit in fetch_bits()[:-1]:
+        parts = dense_first.reshape((2, -1) + dense_first.shape[1:])
+        high = (place // bit) % 2
+        keep = lax.dynamic_index_in_dim(parts, high, 0, False)
+        send = lax.dynamic_index_in_dim(parts, 1 - high, 0, False)
+        dense_first = (keep.astype(f32) + dp_swapped(send, bit).astype(f32)).astype(bf16)
+    ties = {2: got, 3: [dense_first]}
+    final = layer_result(middle, sums, ties)
+    dense_first, got = ties[3][0], list(ties[2])
+    last = len(experts_first) - 1
+    got += [None] * (last - 1)
+    behind = 0
+    for c in range(2, last + 1):
+        experts_first[c], got[behind] = tie(experts_first[c], got[behind])
+        got[c] = swapped(to_give(experts_first[c], second[c]), "section", 1)
+        behind = c
+    dense = jnp.concatenate([dense_first.reshape(dense_second.shape), dense_second], axis=1)
+    ties = {2: got[2:3]}
+    dense = line_reduce(dense.reshape(ranks, -1, dense.shape[1]), ties).astype(bf16)
+    dense_first, dense_second = jnp.split(dense, 2, axis=1)
+    got[2], d_first, final = tie(*ties[2], d_first, final)
+
+    def by_section(of_first, of_second, got=None):
         held = jnp.where(first, of_first, of_second)
-        got = swapped(jnp.where(first, of_second, of_first), "section", 1)
+        if got is None:
+            got = swapped(jnp.where(first, of_second, of_first), "section", 1)
         return jnp.stack([jnp.where(first, held, got), jnp.where(first, got, held)])
 
-    def total(of_first, of_second):
-        got = to_owner(of_first, 0), to_owner(of_second, 1)
-        return jnp.where(
-            first, of_first.astype(f32) + got[0].astype(f32), of_second.astype(f32) + got[1].astype(f32)
-        )
+    def total(of_first, of_second, got):
+        return jnp.where(first, of_first, of_second).astype(f32) + got.astype(f32)
 
     outputs = by_section(between, final)
     input_grads = by_section(d_first, d_between)
-    chunks = [total(a, b) for a, b in zip(experts_first, experts_second)]
+    chunks = [total(*terms) for terms in zip(experts_first, second, got)]
     grad_gate = jnp.concatenate([c[:, :wide] for c in chunks], axis=0)
     grad_up = jnp.concatenate([c[:, wide : 2 * wide] for c in chunks], axis=0)
     grad_down = jnp.concatenate(
@@ -972,10 +1207,9 @@
         ],
         axis=0,
     )
-    grad_out, grad_query, grad_keyval = [
-        total(a.astype(bf16), b.astype(bf16)) for a, b in zip(dense_first, dense_second)
-    ]
-    vectors = total(small_first, small_second)
+    dense = total(dense_first, dense_second, swapped(to_give(dense_first, dense_second), "section", 1))
+    grad_out, grad_query, grad_keyval = dense[:, :width], dense[:, width : 2 * width], dense[:, 2 * width : 3 * width]
+    vectors = dense[:, 3 * width :]
     kv_half = KV_HEADS * HEAD_DIM
     return (
         outputs[None, :, None],
@@ -995,8 +1229,8 @@
 
 def solution(mesh):
     placed = (
-        P(None, "dp", "expert", None),
-        P(None, "dp", "expert", None),
+        P(None, ("far", "near"), "expert", None),
+        P(None, ("far", "near"), "expert", None),
         P("section", None),
         P("section", None, None),
         P("section", None, None),
@@ -1007,26 +1241,29 @@
         P("section", "expert", None, None),
         P("section", "expert", None, None),
         P("section", "expert", None, None),
-        P(None, "dp", None),
-        P("section", None, "dp", "expert", None),
-    )
+        P(None, ("far", "near"), None),
+        P("section", None, ("far", "near"), "expert", None),
+    )
+    sections, dp, ranks = mesh.devices.shape
+    devices = mesh.devices.reshape(sections, dp // 2, 2, ranks)
+    split = jax.sharding.Mesh(devices, ("section", "far", "near", "expert"))
     return jax.shard_map(
         per_device,
-        mesh=mesh,
+        mesh=split,
         in_specs=placed,
         out_specs=(
-            P("section", None, "dp", "expert", None),
-            P("section", None, "dp", "expert", None),
-            P("section", ("dp", "expert")),
-            P("section", ("dp", "expert"), None),
-            P("section", ("dp", "expert"), None),
-            P("section", ("dp", "expert"), None),
-            P("section", ("dp", "expert"), None),
-            P("section", ("dp", "expert")),
-            P("section", ("dp", "expert"), None),
-            P("section", "expert", "dp", None),
-            P("section", "expert", "dp", None),
-            P("section", "expert", "dp", None),
+            P("section", None, ("far", "near"), "expert", None),
+            P("section", None, ("far", "near"), "expert", None),
+            P("section", ("far", "near", "expert")),
+            P("section", ("far", "near", "expert"), None),
+            P("section", ("far", "near", "expert"), None),
+            P("section", ("far", "near", "expert"), None),
+            P("section", ("far", "near", "expert"), None),
+            P("section", ("far", "near", "expert")),
+            P("section", ("far", "near", "expert"), None),
+            P("section", "expert", ("far", "near"), None),
+            P("section", "expert", ("far", "near"), None),
+            P("section", "expert", ("far", "near"), None),
         ),
         check_vma=False,
     )

time: 1400 us -> 1090 us (0.78)
  waiting for transfers between devices: 623 us -> 486 us
  starting transfers between devices: 313 us -> 215 us
  other arithmetic: 111 us -> 61.9 us
  blocking collectives: 19.6 us -> 0 us
    ppermute x92 -> x62, waiting for transfers between devices: 142 us -> 280 us  [shifted(): lax.ppermute(value, axis, [(source, source + steps) for source in names])]
    ppermute x16 -> x0, waiting for transfers between devices: 107 us -> none  [to_owner(): return lax.ppermute(value, 'section', [(1 - layer, layer)])]
    unnamed x4 -> x7, waiting for transfers between devices: 103 us -> 0.63 us
    ppermute x52 -> x50, waiting for transfers between devices: 271 us -> 205 us  [swapped(): lax.ppermute(value, axis, [(source, source ^ bit) for source in range(cou...]
    ppermute x92 -> x62, starting transfers between devices: 240 us -> 177 us  [shifted(): lax.ppermute(value, axis, [(source, source + steps) for source in names])]
    ppermute x16 -> x0, starting transfers between devices: 35.4 us -> none  [to_owner(): return lax.ppermute(value, 'section', [(1 - layer, layer)])]
    convert_element_type x28 -> x13, other arithmetic: 38.7 us -> 13.8 us  [the longest x6 5.06 us: near_sum(): (keep.astype(f32) + swapped(send, 'near', 1).astype(f32)).astype(bf16)]
    all_gather x1 -> x0, blocking collectives: 19.6 us -> none  [per_device(): both = lax.all_gather(both, 'expert', axis=1, tiled=True).transpose(0, 2, 1)]
  transfers between devices with their start and end apart: 162 -> 119, of which waited for: 58 -> 61; matrix products, arithmetic and copies ran while one was open for 10% -> 7% of each run, Pallas kernels for 13% -> 14%
where the time goes in v2:
time: 1090 us; the launch traced here: 1080 us
  waiting for transfers between devices  486 us (45%)
  Pallas kernels  251 us (23%)
  starting transfers between devices  215 us (20%)
  other arithmetic  61.9 us (6%)
  local copies, waits for them, and re-layouts  47.8 us (4%)
  between operations  16.2 us (1%)
    ppermute x62, waiting for transfers between devices, shifted(): lax.ppermute(value, axis, [(source, source + steps) for source in names])  280 us
    pallas_call x20, Pallas kernels, call(): return lambda *args: run(*args, *waits)  234 us
    ppermute x50, waiting for transfers between devices, swapped(): lax.ppermute(value, axis, [(source, source ^ bit) for source in range(cou...  205 us
    ppermute x62, starting transfers between devices, shifted(): lax.ppermute(value, axis, [(source, source + steps) for source in names])  177 us
    ppermute x50, starting transfers between devices, swapped(): lax.ppermute(value, axis, [(source, source ^ bit) for source in range(cou...  37.8 us
    unnamed x197, local copies, waits for them, and re-layouts  23.3 us
  transfers between devices with their start and end apart: 119, of which 61 were waited for; matrix products, arithmetic and copies ran while one was open for 7% of the time, Pallas kernels for 14%

profile of v2, /device:TPU:0, one launch (start us, length us, event | category | flops | bytes accessed | tf_op | source)
XLA Modules:
  0.0 1078.8 jit_solution(2864852566280818841)
XLA Ops:
  24.7 9.6 collective-permute-done.3.refs_2_
  39.3 13.5 %collective-permute-done.2.refs_8_.refs_12_.refs_10_.refs_16_.refs_5_.refs_13_ = bf16[256,3072]{1,0:T(8,128)(2,1)S(1)} collective-permute-done((bf16[256,3072]{1,0:T(8,128)(2,1)}, bf16[256,3072]{1,0:T(8,128)(2,1)S(1)}, u32[]{:S(2)}, u32[]{:S(2)}) %collective-permute-start.2) | collective-permute-done | bytes 1572896 | tf_op jit(solution)/shard_map/ppermute | solution.py:34
  76.1 8.5 collective-permute-done.10.refs_7_
  89.3 9.1 collective-permute-done.20.refs_14_.refs_17_
  125.2 6.5 collective-permute-done.22.refs_16_.refs_19_
  136.6 12.8 %attend.2 = (bf16[256,1024]{1,0:T(8,128)(2,1)}, f32[256,128]{1,0:T(8,128)}, f32[256,1024]{1,0:T(8,128)}, bf16[256,1024]{1,0:T(8,128)(2,1)}) custom-call(s32[3]{0:T(128)} %add_add_fusion.refs_0_, bf16[256,1024]{1,0:T(8,128)(2,1)} %get-tuple-element.128.refs_1_.refs_6_, bf16[256,1024]{1,0:T(8,128)(2,1)} %get-tuple-element.129.refs_2_.refs_8_, ...), custom_call_target="tpu_custom_call" | custom-call | flops 3221225472 | bytes 2097152 | tf_op jit(solution)/shard_map/attend/pallas_call | solution.py:120
  158.9 27.2 %collective-permute-done.28.refs_22_.refs_25_ = bf16[2,768,512]{2,1,0:T(8,128)(2,1)} collective-permute-done((bf16[2,768,512]{2,1,0:T(8,128)(2,1)}, bf16[2,768,512]{2,1,0:T(8,128)(2,1)}, u32[]{:S(2)}, u32[]{:S(2)}) %collective-permute-start.28) | collective-permute-done | bytes 1572896 | tf_op jit(solution)/shard_map/ppermute | solution.py:34
  194.7 8.4 collective-permute-done.17.refs_5_
  218.9 8.4 collective-permute-done.36.refs_30_.refs_33_
  233.0 13.2 %collective-permute-done.19.refs_7_ = bf16[256,1024]{1,0:T(8,128)(2,1)} collective-permute-done((bf16[256,1024]{1,0:T(8,128)(2,1)}, bf16[256,1024]{1,0:T(8,128)(2,1)}, u32[]{:S(2)}, u32[]{:S(2)}) %collective-permute-start.19) | collective-permute-done | bytes 524320 | tf_op jit(solution)/shard_map/ppermute | solution.py:29
  246.7 20.0 %collective-permute-done.34.refs_28_.refs_31_ = bf16[1,768,512]{2,1,0:T(8,128)(2,1)} collective-permute-done((bf16[1,768,512]{2,1,0:T(8,128)(2,1)S(1)}, bf16[1,768,512]{2,1,0:T(8,128)(2,1)}, u32[]{:S(2)}, u32[]{:S(2)}) %collective-permute-start.34) | collective-permute-done | bytes 786464 | tf_op jit(solution)/shard_map/ppermute | solution.py:34
  269.8 11.6 %collective-permute-done.38.refs_32_.refs_35_ = bf16[1,768,512]{2,1,0:T(8,128)(2,1)} collective-permute-done((bf16[1,768,512]{2,1,0:T(8,128)(2,1)S(1)}, bf16[1,768,512]{2,1,0:T(8,128)(2,1)}, u32[]{:S(2)}, u32[]{:S(2)}) %collective-permute-start.38) | collective-permute-done | bytes 786464 | tf_op jit(solution)/shard_map/ppermute | solution.py:34
  284.8 22.4 %experts.2 = (bf16[4,256,1024]{2,1,0:T(8,128)(2,1)}, bf16[4,256,1024]{2,1,0:T(8,128)(2,1)}, bf16[4,512,1024]{2,1,0:T(8,128)(2,1)}, f32[4,32,256]{2,1,0:T(8,128)}...) custom-call(s32[3]{0:T(128)} %add_add_fusion.refs_0_, ...), custom_call_target="tpu_custom_call" | custom-call | flops 6442450944 | bytes 25165824 | tf_op jit(solution)/shard_map/experts/pallas_call | solution.py:120
  315.8 10.2 collective-permute-done.40
  335.1 8.6 collective-permute-done.41
  346.4 9.2 collective-permute-start.42
  378.6 8.7 collective-permute-done.46.refs_3_.refs_9_
  391.6 7.5 collective-permute-done.47.refs_4_.refs_10_
  400.0 12.6 %attend.3 = (bf16[256,1024]{1,0:T(8,128)(2,1)}, f32[256,128]{1,0:T(8,128)}, f32[256,1024]{1,0:T(8,128)}, bf16[256,1024]{1,0:T(8,128)(2,1)}) custom-call(s32[3]{0:T(128)} %add_add_fusion.2.refs_0_, bf16[256,1024]{1,0:T(8,128)(2,1)} %get-tuple-element.147.refs_1_.refs_6_, bf16[256,1024]{1,0:T(8,128)(2,1)} %get-tuple-element.148.refs_2_.refs_8_, ...), custom_call_target="tpu_custom_call" | custom-call | flops 3221225472 | bytes 2097152 | tf_op jit(solution)/shard_map/attend/pallas_call | solution.py:120
  418.3 7.0 collective-permute-done.48.refs_2_
  431.2 7.3 collective-permute-done.49.refs_3_
  455.5 23.4 %experts.3 = (bf16[4,256,1024]{2,1,0:T(8,128)(2,1)}, bf16[4,256,1024]{2,1,0:T(8,128)(2,1)}, bf16[4,512,1024]{2,1,0:T(8,128)(2,1)}, f32[4,32,256]{2,1,0:T(8,128)}...) custom-call(s32[3]{0:T(128)} %add_add_fusion.2.refs_0_, ...), custom_call_target="tpu_custom_call" | custom-call | flops 6442450944 | bytes 25165824 | tf_op jit(solution)/shard_map/experts/pallas_call | solution.py:120
  478.9 26.4 %experts_back.2 = (bf16[4,256,1024]{2,1,0:T(8,128)(2,1)}, f32[32,1024]{1,0:T(8,128)}, bf16[4,512,1024]{2,1,0:T(8,128)(2,1)}, bf16[8,256,512]{2,1,0:T(8,128)(2,1)...) custom-call(s32[3]{0:T(128)} %add_add_fusion.2.refs_0_, bf16[256,1152]{1,0:T(8,128)(2,1)} %copy-done.37, ...), custom_call_target="tpu_custom_call" | custom-call | flops 6442450944 | bytes 25165824 | tf_op jit(solution)/shard_map/experts_back/pallas_call | solution.py:120
  509.5 10.7 collective-permute-done.54.refs_11_
  529.1 9.6 expert_grads.6.refs_20_.refs_12_
  546.2 10.3 collective-permute-done.55
  557.0 6.7 collective-permute-start.56
  565.0 9.4 collective-permute-done.56
  579.8 16.5 %attend_back.2 = (f32[256,1024]{1,0:T(8,128)}, bf16[256,1024]{1,0:T(8,128)(2,1)}, f32[256,1024]{1,0:T(8,128)}, bf16[256,1024]{1,0:T(8,128)(2,1)}, bf16[256,1024]...) custom-call(s32[3]{0:T(128)} %add_add_fusion.2.refs_0_, ...), custom_call_target="tpu_custom_call" | custom-call | flops 8053063680 | bytes 2097152 | tf_op jit(solution)/shard_map/attend_back/pallas_call | solution.py:120
  596.3 9.6 expert_grads.7.refs_9_
  608.2 12.6 %collective-permute-done.65 = bf16[256,1024]{1,0:T(8,128)(2,1)S(1)} collective-permute-done((bf16[256,1024]{1,0:T(8,128)(2,1)S(1)}, bf16[256,1024]{1,0:T(8,128)(2,1)S(1)}, u32[]{:S(2)}, u32[]{:S(2)}) %collective-permute-start.65) | collective-permute-done | bytes 524320 | tf_op jit(solution)/shard_map/ppermute | solution.py:29
  634.9 8.1 keyval_back.2
  653.3 10.1 collective-permute-done.67.refs_2_
  669.2 9.4 collective-permute-done.68.refs_3_
  684.4 8.5 collective-permute-done.69.refs_4_
  697.9 27.1 %experts_back.3 = (bf16[4,256,1024]{2,1,0:T(8,128)(2,1)}, f32[32,1024]{1,0:T(8,128)}, bf16[4,512,1024]{2,1,0:T(8,128)(2,1)}, bf16[8,256,512]{2,1,0:T(8,128)(2,1)...) custom-call(s32[3]{0:T(128)} %add_add_fusion.refs_0_, ...), custom_call_target="tpu_custom_call" | custom-call | flops 6442450944 | bytes 25165824 | tf_op jit(solution)/shard_map/experts_back/pallas_call | solution.py:120
  729.9 10.8 %collective-permute-done.73.refs_11_ = bf16[256,1024]{1,0:T(8,128)(2,1)S(1)} collective-permute-done((bf16[256,1024]{1,0:T(8,128)(2,1)S(1)}, bf16[256,1024]{1,0:T(8,128)(2,1)S(1)}, u32[]{:S(2)}, u32[]{:S(2)}) %collective-permute-start.73) | collective-permute-done | bytes 524320 | tf_op jit(solution)/shard_map/ppermute | solution.py:29
  769.2 8.1 collective-permute-start.75
  778.8 9.0 collective-permute-done.75
  793.2 15.8 %attend_back.3 = (f32[256,1024]{1,0:T(8,128)}, bf16[256,1024]{1,0:T(8,128)(2,1)}, f32[256,1024]{1,0:T(8,128)}, bf16[256,1024]{1,0:T(8,128)(2,1)}, bf16[256,1024]...) custom-call(s32[3]{0:T(128)} %add_add_fusion.refs_0_, ...), custom_call_target="tpu_custom_call" | custom-call | flops 8053063680 | bytes 2097152 | tf_op jit(solution)/shard_map/attend_back/pallas_call | solution.py:120
  816.6 12.6 %collective-permute-done.87 = bf16[256,1024]{1,0:T(8,128)(2,1)S(1)} collective-permute-done((bf16[256,1024]{1,0:T(8,128)(2,1)S(1)}, bf16[256,1024]{1,0:T(8,128)(2,1)S(1)}, u32[]{:S(2)}, u32[]{:S(2)}) %collective-permute-start.87) | collective-permute-done | bytes 524320 | tf_op jit(solution)/shard_map/ppermute | solution.py:29
  843.3 7.8 keyval_back.3
  878.5 44.4 %collective-permute-done.98 = bf16[1,256,3200]{2,1,0:T(8,128)(2,1)} collective-permute-done((bf16[1,256,3200]{2,1,0:T(8,128)(2,1)}, bf16[1,256,3200]{2,1,0:T(8,128)(2,1)}, u32[]{:S(2)}, u32[]{:S(2)}) %collective-permute-start.98) | collective-permute-done | bytes 1638432 | tf_op jit(solution)/shard_map/ppermute | solution.py:34
  925.2 15.7 %collective-permute-done.95 = bf16[2,768,512]{2,1,0:T(8,128)(2,1)} collective-permute-done((bf16[2,768,512]{2,1,0:T(8,128)(2,1)}, bf16[2,768,512]{2,1,0:T(8,128)(2,1)}, u32[]{:S(2)}, u32[]{:S(2)}) %collective-permute-start.95) | collective-permute-done | bytes 1572896 | tf_op jit(solution)/shard_map/ppermute | solution.py:34
  959.5 6.3 collective-permute-start.102
  980.5 13.1 %collective-permute-done.99 = bf16[64,6400]{1,0:T(8,128)(2,1)S(1)} collective-permute-done((bf16[64,6400]{1,0:T(8,128)(2,1)S(1)}, bf16[64,6400]{1,0:T(8,128)(2,1)S(1)}, u32[]{:S(2)}, u32[]{:S(2)}) %collective-permute-start.99) | collective-permute-done | bytes 819232 | tf_op jit(solution)/shard_map/ppermute | solution.py:29
  1011.3 10.1 collective-permute-done.104
  1029.5 22.8 %collective-permute-done.111 = bf16[2,768,512]{2,1,0:T(8,128)(2,1)S(1)} collective-permute-done((bf16[2,768,512]{2,1,0:T(8,128)(2,1)S(1)}, bf16[2,768,512]{2,1,0:T(8,128)(2,1)S(1)}, u32[]{:S(2)}, u32[]{:S(2)}) %collective-permute-start.111) | collective-permute-done | bytes 1572896 | tf_op jit(solution)/shard_map/ppermute | solution.py:34
  (524 shorter events, 445.3 us)
Async XLA Ops:
  7.2 689.8 %reduce-scatter.8.cloned.1.call-start = ((), (), s32[]{:S(2)}) async-start(), calls=%async_computation.7 | async-start | bytes 9437184 | tf_op jit(solution)/shard_map/reduce_scatter | solution.py:1018
  16.7 36.1 %collective-permute-start.2 = (bf16[256,3072]{1,0:T(8,128)(2,1)}, bf16[256,3072]{1,0:T(8,128)(2,1)S(1)}, u32[]{:S(2)}, u32[]{:S(2)}) collective-permute-start(bf16[256,3072]{1,0:T(8,128)(2,1)} %pack_dense.1), channel_id=1, source_target_pairs={{0,16},{16,0},{1,17},{17,1},{2,18},{18,2},{3,19},{19,3},{4,20},{20... | collective-permute-start | bytes 4718600 | tf_op jit(solution)/shard_map/ppermute | solution.py:34
  52.8 35.0 %collective-permute-start.6 = (bf16[256,3072]{1,0:T(8,128)(2,1)S(1)}, bf16[256,3072]{1,0:T(8,128)(2,1)}, u32[]{:S(2)}, u32[]{:S(2)}) collective-permute-start(bf16[256,3072]{1,0:T(8,128)(2,1)S(1)} %collective-permute-done.2.refs_8_.refs_12_.refs_10_.refs_16_.refs_5_.refs_13_), channel_id=1, source_target_pairs={{0,8},{8,0},{1,9},{9,1},{2,10},{10,2},{3,11},{11,3},{4,12},{12,4},... | collective-permute-start | bytes 4718600 | tf_op jit(solution)/shard_map/ppermute | solution.py:34
  64.2 34.2 %collective-permute-start.20 = (bf16[2,768,512]{2,1,0:T(8,128)(2,1)}, bf16[2,768,512]{2,1,0:T(8,128)(2,1)}, u32[]{:S(2)}, u32[]{:S(2)}) collective-permute-start(bf16[2,768,512]{2,1,0:T(8,128)(2,1)} %pack_experts.5), channel_id=1, source_target_pairs={{0,16},{16,0},{1,17},{17,1},{2,18},{18,2},{3,19},{19,3},{4,20},{20... | collective-permute-start | bytes 4718600 | tf_op jit(solution)/shard_map/ppermute | solution.py:34
  76.0 27.7 %collective-permute-start.5 = (bf16[256,3072]{1,0:T(8,128)(2,1)S(1)}, bf16[256,3072]{1,0:T(8,128)(2,1)}, u32[]{:S(2)}, u32[]{:S(2)}) collective-permute-start(bf16[256,3072]{1,0:T(8,128)(2,1)S(1)} %collective-permute-done.2.refs_8_.refs_12_.refs_10_.refs_16_.refs_5_.refs_13_), channel_id=1, source_target_pairs={{0,4},{4,0},{1,5},{5,1},{2,6},{6,2},{3,7},{7,3},{8,12},{12,8},{9,1... | collective-permute-start | bytes 4718600 | tf_op jit(solution)/shard_map/ppermute | solution.py:34
  98.4 33.2 %collective-permute-start.22 = (bf16[2,768,512]{2,1,0:T(8,128)(2,1)}, bf16[2,768,512]{2,1,0:T(8,128)(2,1)}, u32[]{:S(2)}, u32[]{:S(2)}) collective-permute-start(bf16[2,768,512]{2,1,0:T(8,128)(2,1)} %collective-permute-done.20.refs_14_.refs_17_), channel_id=1, source_target_pairs={{0,8},{8,0},{1,9},{9,1},{2,10},{10,2},{3,11},{11,3},{4,12},{12,4},... | collective-permute-start | bytes 4718600 | tf_op jit(solution)/shard_map/ppermute | solution.py:34
  114.7 42.8 %collective-permute-start.24 = (bf16[2,768,512]{2,1,0:T(8,128)(2,1)}, bf16[2,768,512]{2,1,0:T(8,128)(2,1)S(1)}, u32[]{:S(2)}, u32[]{:S(2)}) collective-permute-start(bf16[2,768,512]{2,1,0:T(8,128)(2,1)} %pack_experts.6), channel_id=1, source_target_pairs={{0,16},{16,0},{1,17},{17,1},{2,18},{18,2},{3,19},{19,3},{4,20},{20... | collective-permute-start | bytes 4718600 | tf_op jit(solution)/shard_map/ppermute | solution.py:34
  119.2 66.9 %collective-permute-start.28 = (bf16[2,768,512]{2,1,0:T(8,128)(2,1)}, bf16[2,768,512]{2,1,0:T(8,128)(2,1)}, u32[]{:S(2)}, u32[]{:S(2)}) collective-permute-start(bf16[2,768,512]{2,1,0:T(8,128)(2,1)} %pack_experts.7), channel_id=1, source_target_pairs={{0,16},{16,0},{1,17},{17,1},{2,18},{18,2},{3,19},{19,3},{4,20},{20... | collective-permute-start | bytes 4718600 | tf_op jit(solution)/shard_map/ppermute | solution.py:34
  119.7 67.6 %collective-permute-start.21 = (bf16[2,768,512]{2,1,0:T(8,128)(2,1)}, bf16[2,768,512]{2,1,0:T(8,128)(2,1)}, u32[]{:S(2)}, u32[]{:S(2)}) collective-permute-start(bf16[2,768,512]{2,1,0:T(8,128)(2,1)} %collective-permute-done.20.refs_14_.refs_17_), channel_id=1, source_target_pairs={{0,4},{4,0},{1,5},{5,1},{2,6},{6,2},{3,7},{7,3},{8,12},{12,8},{9,1... | collective-permute-start | bytes 4718600 | tf_op jit(solution)/shard_map/ppermute | solution.py:34
  131.6 75.4 %collective-permute-start.23 = (bf16[2,768,512]{2,1,0:T(8,128)(2,1)}, bf16[2,768,512]{2,1,0:T(8,128)(2,1)}, u32[]{:S(2)}, u32[]{:S(2)}) collective-permute-start(bf16[2,768,512]{2,1,0:T(8,128)(2,1)} %collective-permute-done.22.refs_16_.refs_19_), channel_id=1, source_target_pairs={{0,4},{4,0},{1,5},{5,1},{2,6},{6,2},{3,7},{7,3},{8,12},{12,8},{9,1... | collective-permute-start | bytes 4718600 | tf_op jit(solution)/shard_map/ppermute | solution.py:34
  149.5 39.5 %collective-permute-start.14 = (bf16[256,1024]{1,0:T(8,128)(2,1)}, bf16[256,1024]{1,0:T(8,128)(2,1)}, u32[]{:S(2)}, u32[]{:S(2)}) collective-permute-start(bf16[256,1024]{1,0:T(8,128)(2,1)} %get-tuple-element.131.refs_1_), channel_id=1, source_target_pairs={{0,1},{1,2},{2,3},{4,5},{5,6},{6,7},{8,9},{9,10},{10,11},{12,13},{... | collective-permute-start | bytes 1572872 | tf_op jit(solution)/shard_map/ppermute | solution.py:29
  157.5 49.5 %collective-permute-start.32 = (bf16[1,768,512]{2,1,0:T(8,128)(2,1)}, bf16[1,768,512]{2,1,0:T(8,128)(2,1)S(1)}, u32[]{:S(2)}, u32[]{:S(2)}) collective-permute-start(bf16[1,768,512]{2,1,0:T(8,128)(2,1)} %pack_experts.8), channel_id=1, source_target_pairs={{0,16},{16,0},{1,17},{17,1},{2,18},{18,2},{3,19},{19,3},{4,20},{20... | collective-permute-start | bytes 2359304 | tf_op jit(solution)/shard_map/ppermute | solution.py:34
  187.4 41.4 %collective-permute-start.26 = (bf16[2,768,512]{2,1,0:T(8,128)(2,1)S(1)}, bf16[2,768,512]{2,1,0:T(8,128)(2,1)}, u32[]{:S(2)}, u32[]{:S(2)}) collective-permute-start(bf16[2,768,512]{2,1,0:T(8,128)(2,1)S(1)} %collective-permute-done.24.refs_18_.refs_21_), channel_id=1, source_target_pairs={{0,8},{8,0},{1,9},{9,1},{2,10},{10,2},{3,11},{11,3},{4,12},{12,4},... | collective-permute-start | bytes 4718600 | tf_op jit(solution)/shard_map/ppermute | solution.py:34
  189.0 19.7 %collective-permute-start.15 = (bf16[256,1024]{1,0:T(8,128)(2,1)}, bf16[256,1024]{1,0:T(8,128)(2,1)}, u32[]{:S(2)}, u32[]{:S(2)}) collective-permute-start(bf16[256,1024]{1,0:T(8,128)(2,1)} %collective-permute-done.14.refs_2_.refs_35_), channel_id=1, source_target_pairs={{0,1},{1,2},{2,3},{4,5},{5,6},{6,7},{8,9},{9,10},{10,11},{12,13},{... | collective-permute-start | bytes 1572872 | tf_op jit(solution)/shard_map/ppermute | solution.py:29
  207.1 25.4 %collective-permute-start.25 = (bf16[2,768,512]{2,1,0:T(8,128)(2,1)S(1)}, bf16[2,768,512]{2,1,0:T(8,128)(2,1)}, u32[]{:S(2)}, u32[]{:S(2)}) collective-permute-start(bf16[2,768,512]{2,1,0:T(8,128)(2,1)S(1)} %collective-permute-done.24.refs_18_.refs_21_), channel_id=1, source_target_pairs={{0,4},{4,0},{1,5},{5,1},{2,6},{6,2},{3,7},{7,3},{8,12},{12,8},{9,1... | collective-permute-start | bytes 4718600 | tf_op jit(solution)/shard_map/ppermute | solution.py:34
  207.1 20.2 %collective-permute-start.36 = (bf16[1,768,512]{2,1,0:T(8,128)(2,1)}, bf16[1,768,512]{2,1,0:T(8,128)(2,1)S(1)}, u32[]{:S(2)}, u32[]{:S(2)}) collective-permute-start(bf16[1,768,512]{2,1,0:T(8,128)(2,1)} %pack_experts.9), channel_id=1, source_target_pairs={{0,16},{16,0},{1,17},{17,1},{2,18},{18,2},{3,19},{19,3},{4,20},{20... | collective-permute-start | bytes 2359304 | tf_op jit(solution)/shard_map/ppermute | solution.py:34
  208.6 58.1 %collective-permute-start.30 = (bf16[2,768,512]{2,1,0:T(8,128)(2,1)}, bf16[2,768,512]{2,1,0:T(8,128)(2,1)}, u32[]{:S(2)}, u32[]{:S(2)}) collective-permute-start(bf16[2,768,512]{2,1,0:T(8,128)(2,1)} %collective-permute-done.28.refs_22_.refs_25_), channel_id=1, source_target_pairs={{0,8},{8,0},{1,9},{9,1},{2,10},{10,2},{3,11},{11,3},{4,12},{12,4},... | collective-permute-start | bytes 4718600 | tf_op jit(solution)/shard_map/ppermute | solution.py:34
  227.2 39.5 %collective-permute-start.34 = (bf16[1,768,512]{2,1,0:T(8,128)(2,1)S(1)}, bf16[1,768,512]{2,1,0:T(8,128)(2,1)}, u32[]{:S(2)}, u32[]{:S(2)}) collective-permute-start(bf16[1,768,512]{2,1,0:T(8,128)(2,1)S(1)} %collective-permute-done.32.refs_26_.refs_29_), channel_id=1, source_target_pairs={{0,8},{8,0},{1,9},{9,1},{2,10},{10,2},{3,11},{11,3},{4,12},{12,4},... | collective-permute-start | bytes 2359304 | tf_op jit(solution)/shard_map/ppermute | solution.py:34
  228.8 40.5 %collective-permute-start.29 = (bf16[2,768,512]{2,1,0:T(8,128)(2,1)}, bf16[2,768,512]{2,1,0:T(8,128)(2,1)}, u32[]{:S(2)}, u32[]{:S(2)}) collective-permute-start(bf16[2,768,512]{2,1,0:T(8,128)(2,1)} %collective-permute-done.28.refs_22_.refs_25_), channel_id=1, source_target_pairs={{0,4},{4,0},{1,5},{5,1},{2,6},{6,2},{3,7},{7,3},{8,12},{12,8},{9,1... | collective-permute-start | bytes 4718600 | tf_op jit(solution)/shard_map/ppermute | solution.py:34
  232.5 36.7 %collective-permute-start.33 = (bf16[1,768,512]{2,1,0:T(8,128)(2,1)S(1)}, bf16[1,768,512]{2,1,0:T(8,128)(2,1)}, u32[]{:S(2)}, u32[]{:S(2)}) collective-permute-start(bf16[1,768,512]{2,1,0:T(8,128)(2,1)S(1)} %collective-permute-done.32.refs_26_.refs_29_), channel_id=1, source_target_pairs={{0,4},{4,0},{1,5},{5,1},{2,6},{6,2},{3,7},{7,3},{8,12},{12,8},{9,1... | collective-permute-start | bytes 2359304 | tf_op jit(solution)/shard_map/ppermute | solution.py:34
  246.2 35.2 %collective-permute-start.38 = (bf16[1,768,512]{2,1,0:T(8,128)(2,1)S(1)}, bf16[1,768,512]{2,1,0:T(8,128)(2,1)}, u32[]{:S(2)}, u32[]{:S(2)}) collective-permute-start(bf16[1,768,512]{2,1,0:T(8,128)(2,1)S(1)} %collective-permute-done.36.refs_30_.refs_33_), channel_id=1, source_target_pairs={{0,8},{8,0},{1,9},{9,1},{2,10},{10,2},{3,11},{11,3},{4,12},{12,4},... | collective-permute-start | bytes 2359304 | tf_op jit(solution)/shard_map/ppermute | solution.py:34
  346.4 18.1 %collective-permute-start.42 = (bf16[256,1024]{1,0:T(8,128)(2,1)}, bf16[256,1024]{1,0:T(8,128)(2,1)}, u32[]{:S(2)}, u32[]{:S(2)}) collective-permute-start(bf16[256,1024]{1,0:T(8,128)(2,1)} %get-tuple-element.352), channel_id=1, source_target_pairs={{0,1},{1,2},{2,3},{4,5},{5,6},{6,7},{8,9},{9,10},{10,11},{12,13},{... | collective-permute-start | bytes 1572872 | tf_op jit(solution)/shard_map/ppermute | solution.py:29
  505.3 23.8 %collective-permute-start.61 = (bf16[4,512,1024]{2,1,0:T(8,128)(2,1)}, bf16[4,512,1024]{2,1,0:T(8,128)(2,1)}, u32[]{:S(2)}, u32[]{:S(2)}) collective-permute-start(bf16[4,512,1024]{2,1,0:T(8,128)(2,1)} %get-tuple-element.163.refs_2_), channel_id=1, source_target_pairs={{0,4},{4,0},{1,5},{5,1},{2,6},{6,2},{3,7},{7,3},{8,12},{12,8},{9,1... | collective-permute-start | bytes 12582920 | tf_op jit(solution)/shard_map/ppermute | solution.py:34
  505.4 23.7 %collective-permute-start.60 = (bf16[4,512,1024]{2,1,0:T(8,128)(2,1)S(1)}, bf16[4,512,1024]{2,1,0:T(8,128)(2,1)}, u32[]{:S(2)}, u32[]{:S(2)}) collective-permute-start(bf16[4,512,1024]{2,1,0:T(8,128)(2,1)S(1)} %copy-done.11), channel_id=1, source_target_pairs={{0,4},{4,0},{1,5},{5,1},{2,6},{6,2},{3,7},{7,3},{8,12},{12,8},{9,1... | collective-permute-start | bytes 12582920 | tf_op jit(solution)/shard_map/ppermute | solution.py:34
  538.7 186.3 %reduce-scatter.10.cloned.1.call-start = ((), (), s32[]{:S(2)}) async-start(), calls=%async_computation.8 | async-start | bytes 9437184 | tf_op jit(solution)/shard_map/reduce_scatter | solution.py:1018
  605.9 144.3 %reduce-scatter.12.cloned.1.call-start = ((), (), s32[]{:S(2)}) async-start(), calls=%async_computation.9 | async-start | bytes 4915200 | tf_op jit(solution)/shard_map/reduce_scatter | solution.py:1158
  622.4 20.7 %collective-permute-start.84 = (bf16[2,256,1024]{2,1,0:T(8,128)(2,1)S(1)}, bf16[2,256,1024]{2,1,0:T(8,128)(2,1)S(1)}, u32[]{:S(2)}, u32[]{:S(2)}) collective-permute-start(bf16[2,256,1024]{2,1,0:T(8,128)(2,1)S(1)} %copy-done.88), channel_id=1, source_target_pairs={{0,4},{4,0},{1,5},{5,1},{2,6},{6,2},{3,7},{7,3},{8,12},{12,8},{9,1... | collective-permute-start | bytes 3145736 | tf_op jit(solution)/shard_map/ppermute | solution.py:34
  648.3 217.2 %reduce-scatter.16.cloned.1.call-start = ((), (), s32[]{:S(2)}) async-start(), calls=%async_computation.11 | async-start | bytes 4718592 | tf_op jit(solution)/shard_map/reduce_scatter | solution.py:1018
  684.3 59.5 %collective-permute-start.79 = (bf16[4,512,1024]{2,1,0:T(8,128)(2,1)}, bf16[4,512,1024]{2,1,0:T(8,128)(2,1)}, u32[]{:S(2)}, u32[]{:S(2)}) collective-permute-start(bf16[4,512,1024]{2,1,0:T(8,128)(2,1)} %get-tuple-element.185.refs_1_), channel_id=1, source_target_pairs={{0,4},{4,0},{1,5},{5,1},{2,6},{6,2},{3,7},{7,3},{8,12},{12,8},{9,1... | collective-permute-start | bytes 12582920 | tf_op jit(solution)/shard_map/ppermute | solution.py:34
  724.9 25.4 %collective-permute-start.80 = (bf16[4,512,1024]{2,1,0:T(8,128)(2,1)}, bf16[4,512,1024]{2,1,0:T(8,128)(2,1)}, u32[]{:S(2)}, u32[]{:S(2)}) collective-permute-start(bf16[4,512,1024]{2,1,0:T(8,128)(2,1)} %get-tuple-element.186.refs_2_), channel_id=1, source_target_pairs={{0,4},{4,0},{1,5},{5,1},{2,6},{6,2},{3,7},{7,3},{8,12},{12,8},{9,1... | collective-permute-start | bytes 12582920 | tf_op jit(solution)/shard_map/ppermute | solution.py:34
  729.7 18.5 %collective-permute-start.81 = (bf16[8,256,512]{2,1,0:T(8,128)(2,1)S(1)}, bf16[8,256,512]{2,1,0:T(8,128)(2,1)S(1)}, u32[]{:S(2)}, u32[]{:S(2)}) collective-permute-start(bf16[8,256,512]{2,1,0:T(8,128)(2,1)S(1)} %copy-done.5), channel_id=1, source_target_pairs={{0,4},{4,0},{1,5},{5,1},{2,6},{6,2},{3,7},{7,3},{8,12},{12,8},{9,1... | collective-permute-start | bytes 6291464 | tf_op jit(solution)/shard_map/ppermute | solution.py:34
  767.0 98.4 %reduce-scatter.14.cloned.1.call-start = ((), (), s32[]{:S(2)}) async-start(), calls=%async_computation.10 | async-start | bytes 4718592 | tf_op jit(solution)/shard_map/reduce_scatter | solution.py:1018
  767.6 173.3 %reduce-scatter.20.cloned.1.call-start = ((), (), s32[]{:S(2)}) async-start(), calls=%async_computation.13 | async-start | bytes 4718592 | tf_op jit(solution)/shard_map/reduce_scatter | solution.py:1018
  769.2 18.6 %collective-permute-start.75 = (bf16[256,1024]{1,0:T(8,128)(2,1)S(1)}, bf16[256,1024]{1,0:T(8,128)(2,1)S(1)}, u32[]{:S(2)}, u32[]{:S(2)}) collective-permute-start(bf16[256,1024]{1,0:T(8,128)(2,1)S(1)} %get-tuple-element.340), channel_id=1, source_target_pairs={{0,1},{1,2},{2,3},{4,5},{5,6},{6,7},{8,9},{9,10},{10,11},{12,13},{... | collective-permute-start | bytes 1572872 | tf_op jit(solution)/shard_map/ppermute | solution.py:29
  814.4 180.7 %reduce-scatter.18.cloned.1.call-start = ((), (), s32[]{:S(2)}) async-start(), calls=%async_computation.12 | async-start | bytes 4718592 | tf_op jit(solution)/shard_map/reduce_scatter | solution.py:1018
  830.7 20.5 %collective-permute-start.89 = (bf16[2,256,1024]{2,1,0:T(8,128)(2,1)}, bf16[2,256,1024]{2,1,0:T(8,128)(2,1)S(1)}, u32[]{:S(2)}, u32[]{:S(2)}) collective-permute-start(bf16[2,256,1024]{2,1,0:T(8,128)(2,1)} %get-tuple-element.206), channel_id=1, source_target_pairs={{0,4},{4,0},{1,5},{5,1},{2,6},{6,2},{3,7},{7,3},{8,12},{12,8},{9,1... | collective-permute-start | bytes 3145736 | tf_op jit(solution)/shard_map/ppermute | solution.py:34
  835.3 18.5 %collective-permute-start.90 = (bf16[2,256,1024]{2,1,0:T(8,128)(2,1)}, bf16[2,256,1024]{2,1,0:T(8,128)(2,1)}, u32[]{:S(2)}, u32[]{:S(2)}) collective-permute-start(bf16[2,256,1024]{2,1,0:T(8,128)(2,1)} %get-tuple-element.208), channel_id=1, source_target_pairs={{0,4},{4,0},{1,5},{5,1},{2,6},{6,2},{3,7},{7,3},{8,12},{12,8},{9,1... | collective-permute-start | bytes 3145736 | tf_op jit(solution)/shard_map/ppermute | solution.py:34
  857.8 65.1 %collective-permute-start.98 = (bf16[1,256,3200]{2,1,0:T(8,128)(2,1)}, bf16[1,256,3200]{2,1,0:T(8,128)(2,1)}, u32[]{:S(2)}, u32[]{:S(2)}) collective-permute-start(bf16[1,256,3200]{2,1,0:T(8,128)(2,1)} %constant_dynamic-slice_fusion), channel_id=1, source_target_pairs={{0,8},{8,0},{1,9},{9,1},{2,10},{10,2},{3,11},{11,3},{4,12},{12,4},... | collective-permute-start | bytes 4915208 | tf_op jit(solution)/shard_map/ppermute | solution.py:34
  869.6 55.6 %collective-permute-start.94 = (bf16[2,768,512]{2,1,0:T(8,128)(2,1)}, bf16[2,768,512]{2,1,0:T(8,128)(2,1)}, u32[]{:S(2)}, u32[]{:S(2)}) collective-permute-start(bf16[2,768,512]{2,1,0:T(8,128)(2,1)} %get-tuple-element.333), channel_id=1, source_target_pairs={{0,16},{16,0},{1,17},{17,1},{2,18},{18,2},{3,19},{19,3},{4,20},{20... | collective-permute-start | bytes 4718600 | tf_op jit(solution)/shard_map/ppermute | solution.py:34
  872.2 68.8 %collective-permute-start.95 = (bf16[2,768,512]{2,1,0:T(8,128)(2,1)}, bf16[2,768,512]{2,1,0:T(8,128)(2,1)}, u32[]{:S(2)}, u32[]{:S(2)}) collective-permute-start(bf16[2,768,512]{2,1,0:T(8,128)(2,1)} %get-tuple-element.332), channel_id=1, source_target_pairs={{0,16},{16,0},{1,17},{17,1},{2,18},{18,2},{3,19},{19,3},{4,20},{20... | collective-permute-start | bytes 4718600 | tf_op jit(solution)/shard_map/ppermute | solution.py:34
  943.9 51.2 %collective-permute-start.101 = (bf16[2,768,512]{2,1,0:T(8,128)(2,1)}, bf16[2,768,512]{2,1,0:T(8,128)(2,1)}, u32[]{:S(2)}, u32[]{:S(2)}) collective-permute-start(bf16[2,768,512]{2,1,0:T(8,128)(2,1)} %broadcast_select_fusion.1), channel_id=1, source_target_pairs={{0,16},{16,0},{1,17},{17,1},{2,18},{18,2},{3,19},{19,3},{4,20},{20... | collective-permute-start | bytes 4718600 | tf_op jit(solution)/shard_map/ppermute | solution.py:34
  959.5 18.7 %collective-permute-start.102 = (bf16[256,1024]{1,0:T(8,128)(2,1)S(1)}, bf16[256,1024]{1,0:T(8,128)(2,1)S(1)}, u32[]{:S(2)}, u32[]{:S(2)}) collective-permute-start(bf16[256,1024]{1,0:T(8,128)(2,1)S(1)} %get-tuple-element.222), channel_id=1, source_target_pairs={{0,1},{1,2},{2,3},{4,5},{5,6},{6,7},{8,9},{9,10},{10,11},{12,13},{... | collective-permute-start | bytes 1572872 | tf_op jit(solution)/shard_map/ppermute | solution.py:29
  968.0 25.5 %collective-permute-start.99 = (bf16[64,6400]{1,0:T(8,128)(2,1)S(1)}, bf16[64,6400]{1,0:T(8,128)(2,1)S(1)}, u32[]{:S(2)}, u32[]{:S(2)}) collective-permute-start(bf16[64,6400]{1,0:T(8,128)(2,1)S(1)} %get-tuple-element.311), channel_id=1, source_target_pairs={{0,1},{4,5},{8,9},{12,13},{16,17},{20,21},{24,25},{28,29}} | collective-permute-start | bytes 2457608 | tf_op jit(solution)/shard_map/ppermute | solution.py:29
  997.1 24.2 %collective-permute-start.104 = (bf16[256,1024]{1,0:T(8,128)(2,1)S(1)}, bf16[256,1024]{1,0:T(8,128)(2,1)S(1)}, u32[]{:S(2)}, u32[]{:S(2)}) collective-permute-start(bf16[256,1024]{1,0:T(8,128)(2,1)S(1)} %broadcast_select_fusion.4), channel_id=1, source_target_pairs={{0,16},{16,0},{1,17},{17,1},{2,18},{18,2},{3,19},{19,3},{4,20},{20... | collective-permute-start | bytes 1572872 | tf_op jit(solution)/shard_map/ppermute | solution.py:34
  997.6 54.7 %collective-permute-start.111 = (bf16[2,768,512]{2,1,0:T(8,128)(2,1)S(1)}, bf16[2,768,512]{2,1,0:T(8,128)(2,1)S(1)}, u32[]{:S(2)}, u32[]{:S(2)}) collective-permute-start(bf16[2,768,512]{2,1,0:T(8,128)(2,1)S(1)} %broadcast_select_fusion), channel_id=1, source_target_pairs={{0,16},{16,0},{1,17},{17,1},{2,18},{18,2},{3,19},{19,3},{4,20},{20... | collective-permute-start | bytes 4718600 | tf_op jit(solution)/shard_map/ppermute | solution.py:34
  1000.9 21.6 %collective-permute-start.106 = (bf16[64,6400]{1,0:T(8,128)(2,1)S(1)}, bf16[64,6400]{1,0:T(8,128)(2,1)S(1)}, u32[]{:S(2)}, u32[]{:S(2)}) collective-permute-start(bf16[64,6400]{1,0:T(8,128)(2,1)S(1)} %copy-done.63), channel_id=1, source_target_pairs={{0,1},{1,2},{4,5},{5,6},{8,9},{9,10},{12,13},{13,14},{16,17},{17,1... | collective-permute-start | bytes 2457608 | tf_op jit(solution)/shard_map/ppermute | solution.py:29
  1022.9 36.7 %collective-permute-start.107 = (bf16[64,6400]{1,0:T(8,128)(2,1)S(1)}, bf16[64,6400]{1,0:T(8,128)(2,1)S(1)}, u32[]{:S(2)}, u32[]{:S(2)}) collective-permute-start(bf16[64,6400]{1,0:T(8,128)(2,1)S(1)} %get-tuple-element.306), channel_id=1, source_target_pairs={{0,1},{1,2},{2,3},{4,5},{5,6},{6,7},{8,9},{9,10},{10,11},{12,13},{... | collective-permute-start | bytes 2457608 | tf_op jit(solution)/shard_map/ppermute | solution.py:29
  1028.0 31.6 %collective-permute-start.109 = (bf16[64,6400]{1,0:T(8,128)(2,1)S(1)}, bf16[64,6400]{1,0:T(8,128)(2,1)S(1)}, u32[]{:S(2)}, u32[]{:S(2)}) collective-permute-start(bf16[64,6400]{1,0:T(8,128)(2,1)S(1)} %get-tuple-element.307), channel_id=1, source_target_pairs={{1,0},{2,1},{3,2},{5,4},{6,5},{7,6},{9,8},{10,9},{11,10},{13,12},{... | collective-permute-start | bytes 2457608 | tf_op jit(solution)/shard_map/ppermute | solution.py:29
  (166 other events, 2019.0 us)
Sparse Core Ops, SparseCore 0:
  538.9 77.3 reduce-scatter.7
  618.7 77.0 reduce-scatter.9
  698.6 44.7 reduce-scatter.11
  767.1 46.9 reduce-scatter.15
  816.8 43.3 reduce-scatter.13
  862.4 69.1 reduce-scatter.19
  933.8 42.9 reduce-scatter.17

commit v3 on v2

--- a/solution.py
+++ b/solution.py
@@ -553,8 +553,12 @@
     rest = rest[6:]
     chunks = [rest[c * pieces : (c + 1) * pieces] for c in range(chunk_count)]
     rest = rest[chunk_count * pieces :]
-    sums, everyone, rows, gates, codes, gate_out, up_out = rest[:7]
-    hits, results, gate_buf, up_buf, down_buf, sems, line_sem = rest[7:]
+    sums, everyone_out, rows_out, gates, codes, gate_out, up_out = rest[:7]
+    hits, results, gate_buf, up_buf, down_buf, everyone, rows, sems, line_sem, out_sems = rest[7:]
+    kept = [
+        pltpu.make_async_copy(everyone, everyone_out, out_sems.at[0]),
+        pltpu.make_async_copy(rows, rows_out, out_sems.at[1]),
+    ]
     expert, count = pl.program_id(0), pl.num_programs(0)
     buffers = (gate_buf, up_buf, down_buf)
     owns = (w_gate, w_up, w_down)
@@ -589,6 +593,8 @@
                 hit = slot_hits(slot_rows(info, code, e, experts_here), capacity)
                 hits[block, e * capacity : (e + 1) * capacity, :] = jnp.where(hit, 1.0, 0.0).astype(bf16)
             rows[block] = dot(hits[block], everyone[block]).astype(bf16)
+        for copy in kept:
+            copy.start()
 
     @pl.when(expert + 1 < count)
     def _():
@@ -596,14 +602,13 @@
 
     place = pl.multiple_of(expert * capacity, capacity)
     mine = jnp.concatenate([rows[block, pl.ds(place, capacity), :] for block in range(ranks)], axis=0)
-    wait_experts(slot, 0, buffers, sems)
+    for index in range(3):
+        wait_experts(slot, index, buffers, sems)
     gate_pre = dot(mine, gate_buf[slot])
-    wait_experts(slot, 1, buffers, sems)
     up_pre = dot(mine, up_buf[slot])
     gate_out[0] = gate_pre.astype(bf16)
     up_out[0] = up_pre.astype(bf16)
     activated = (gate_pre * jax.nn.sigmoid(gate_pre) * up_pre).astype(bf16)
-    wait_experts(slot, 2, buffers, sems)
     produced = dot(activated, down_buf[slot]).astype(bf16)
     for block in range(ranks):
         results[block, pl.ds(place, capacity), :] = produced[block * capacity : (block + 1) * capacity]
@@ -617,6 +622,8 @@
                 hit = hits[block, e * capacity : (e + 1) * capacity, :].astype(f32)
                 weighted.append((hit * weight).astype(bf16))
             sums[block] = dot(jnp.concatenate(weighted, axis=0), results[block], 0, 0).astype(bf16)
+        for copy in kept:
+            copy.wait()
 
 
 def experts_back_kernel(pieces, ranks, chunk_count, info, own, *rest):
@@ -626,8 +633,10 @@
     rest = rest[9:]
     chunks = [rest[c * pieces : (c + 1) * pieces] for c in range(chunk_count)]
     rest = rest[chunk_count * pieces :]
-    sums, grad_router, grad_rows, gate_out, up_out, active_out = rest[:6]
-    incoming, hits, columns, d_gates, d_rows, gate_buf, up_buf, down_buf, sems, line_sem = rest[6:]
+    sums, grad_router, rows_out, gate_out, up_out, active_out = rest[:6]
+    incoming, hits, columns, d_gates, d_rows, gate_buf, up_buf, down_buf = rest[6:14]
+    grad_rows, sems, line_sem, out_sem = rest[14:]
+    kept = pltpu.make_async_copy(grad_rows, rows_out, out_sem)
     expert, count = pl.program_id(0), pl.num_programs(0)
     buffers = (gate_buf, up_buf, down_buf)
     owns = (w_gate, w_up, w_down)
@@ -651,6 +660,7 @@
         wait_line(incoming, line_sem)
         for block in range(ranks):
             grad_rows[block] = dot(hits[block], incoming[block]).astype(bf16)
+        kept.start()
 
     @pl.when(expert + 1 < count)
     def _():
@@ -666,7 +676,8 @@
     sigma = jax.nn.sigmoid(gate)
     silu = gate * sigma
     activated = silu * up
-    wait_experts(slot, 2, buffers, sems)
+    for index in range(3):
+        wait_experts(slot, index, buffers, sems)
     unweighted = dot(mine, down_buf[slot], 1, 1)
     d_weight = jnp.sum(unweighted * activated, axis=1, keepdims=True)
     for block in range(ranks):
@@ -679,8 +690,6 @@
     d_up = (d_active * silu).astype(bf16)
     gate_out[0] = d_gate
     up_out[0] = d_up
-    wait_experts(slot, 0, buffers, sems)
-    wait_experts(slot, 1, buffers, sems)
     produced = (dot(d_gate, gate_buf[slot], 1, 1) + dot(d_up, up_buf[slot], 1, 1)).astype(bf16)
     for block in range(ranks):
         d_rows[block, pl.ds(place, capacity), :] = produced[block * capacity : (block + 1) * capacity]
@@ -701,6 +710,7 @@
             back = dot(hits[block], d_rows[block], 0, 0) + dot(d_logits, router[...], 0, 0)
             sums[block] = back.astype(bf16)
         grad_router[...] = router_total
+        kept.wait()
 
 
 def expert_grads_kernel(info, *refs):
@@ -824,7 +834,7 @@
             struct((experts_here, ranks * capacity, hidden), bf16),
         ),
         [SMEM] + [ANY] * (2 * ranks - 1) + [VMEM] * 3 + [ANY] * (3 + pieces * len(expert_parts)),
-        (VMEM,) * 5
+        (VMEM, ANY, ANY, VMEM, VMEM)
         + (pl.BlockSpec((1, ranks * capacity, hidden), lambda e: (e, 0, 0)),) * 2,
         [
             pltpu.VMEM((ranks, slots, rows), bf16),
@@ -832,8 +842,11 @@
             pltpu.VMEM((2, width, hidden), bf16),
             pltpu.VMEM((2, width, hidden), bf16),
             pltpu.VMEM((2, hidden, width), bf16),
+            pltpu.VMEM((ranks, rows, width), bf16),
+            pltpu.VMEM((ranks, slots, width), bf16),
             pltpu.SemaphoreType.DMA((2, 3)),
             pltpu.SemaphoreType.DMA,
+            pltpu.SemaphoreType.DMA((2,)),
         ],
         grid=(experts_here,),
         flops=6 * experts_here * ranks * capacity * width * hidden,
@@ -877,7 +890,7 @@
         + (struct((experts_here, ranks * capacity, hidden), bf16),) * 3,
         [SMEM] + [ANY] * (2 * ranks - 1) + [VMEM] * 4 + [per_expert] * 2
         + [ANY] * (3 + pieces * len(expert_parts)),
-        (VMEM,) * 3 + (per_expert,) * 3,
+        (VMEM, VMEM, ANY) + (per_expert,) * 3,
         [
             pltpu.VMEM((ranks, rows, width), bf16),
             pltpu.VMEM((ranks, slots, rows), bf16),
@@ -887,7 +900,9 @@
             pltpu.VMEM((2, width, hidden), bf16),
             pltpu.VMEM((2, width, hidden), bf16),
             pltpu.VMEM((2, hidden, width), bf16),
+            pltpu.VMEM((ranks, slots, width), bf16),
             pltpu.SemaphoreType.DMA((2, 3)),
+            pltpu.SemaphoreType.DMA,
             pltpu.SemaphoreType.DMA,
         ],
         grid=(experts_here,),
@@ -906,7 +921,11 @@
     marks = []
     if "reduce" in waits:
         sums, *waits["reduce"] = tie(sums, *waits["reduce"])
-    d_routed = line_reduce(sums, marks=marks)
+    if layer == 1:
+        d_routed = lax.psum_scatter(sums, "expert", scatter_dimension=0, tiled=True)
+        marks.append([])
+    else:
+        d_routed = line_reduce(sums, marks=marks)
     marks += marks[-1:] * 2
     own_terms = (expert_rows, grad_rows, d_gate, d_up, activated)
     near_terms = [swapped(term, "near", 1) for term in own_terms]
@@ -937,6 +956,9 @@
     gradients(*marks[0], *waits.get("expert_grads", ()))
     if layer == 0:
         gradients(*marks[1])
+    else:
+        pairs[0], d_routed = tie(pairs[0], d_routed)
+        d_routed = d_routed[0].astype(f32)
     outs = call(
         functools.partial(attend_back_kernel, pieces, reach),
         (
@@ -1170,9 +1192,11 @@
         keep = lax.dynamic_index_in_dim(parts, high, 0, False)
         send = lax.dynamic_index_in_dim(parts, 1 - high, 0, False)
         dense_first = (keep.astype(f32) + dp_swapped(send, bit).astype(f32)).astype(bf16)
-    ties = {2: got, 3: [dense_first]}
+    got_grad = swapped(to_give(d_first, d_between), "section", 1)
+    ties = {2: [dense_first, *got], 3: [got_grad]}
     final = layer_result(middle, sums, ties)
-    dense_first, got = ties[3][0], list(ties[2])
+    got_grad, (dense_first, *got) = ties[3][0], ties[2]
+    got_output = swapped(to_give(between, final), "section", 1)
     last = len(experts_first) - 1
     got += [None] * (last - 1)
     behind = 0
@@ -1181,22 +1205,20 @@
         got[c] = swapped(to_give(experts_first[c], second[c]), "section", 1)
         behind = c
     dense = jnp.concatenate([dense_first.reshape(dense_second.shape), dense_second], axis=1)
-    ties = {2: got[2:3]}
+    ties = {3: got[2:3]}
     dense = line_reduce(dense.reshape(ranks, -1, dense.shape[1]), ties).astype(bf16)
     dense_first, dense_second = jnp.split(dense, 2, axis=1)
-    got[2], d_first, final = tie(*ties[2], d_first, final)
-
-    def by_section(of_first, of_second, got=None):
+    got[2] = ties[3][0]
+
+    def by_section(of_first, of_second, got):
         held = jnp.where(first, of_first, of_second)
-        if got is None:
-            got = swapped(jnp.where(first, of_second, of_first), "section", 1)
         return jnp.stack([jnp.where(first, held, got), jnp.where(first, got, held)])
 
     def total(of_first, of_second, got):
         return jnp.where(first, of_first, of_second).astype(f32) + got.astype(f32)
 
-    outputs = by_section(between, final)
-    input_grads = by_section(d_first, d_between)
+    outputs = by_section(between, final, got_output)
+    input_grads = by_section(d_first, d_between, got_grad)
     chunks = [total(*terms) for terms in zip(experts_first, second, got)]
     grad_gate = jnp.concatenate([c[:, :wide] for c in chunks], axis=0)
     grad_up = jnp.concatenate([c[:, wide : 2 * wide] for c in chunks], axis=0)

time: 1090 us -> 1090 us (level)
    ppermute x62 -> x56, waiting for transfers between devices: 280 us -> 254 us  [shifted(): lax.ppermute(value, axis, [(source, source + steps) for source in names])]
    reduce_scatter x1, waiting for transfers between devices: 0.02 us -> 22.2 us  [per_device(): lax.psum_scatter(dense_second, 'far', scatter_dimension=0, tiled=True)[0]]
    reduce_scatter x0 -> x1, waiting for transfers between devices: none -> 10.9 us  [layer_backward(): d_routed = lax.psum_scatter(sums, 'expert', scatter_dimension=0, tiled=True)]
    ppermute x62 -> x56, starting transfers between devices: 177 us -> 171 us  [shifted(): lax.ppermute(value, axis, [(source, source + steps) for source in names])]
    unnamed x197 -> x191, local copies, waits for them, and re-layouts: 23.3 us -> 19.4 us
  transfers between devices with their start and end apart: 119 -> 114, of which waited for: 61 -> 57; matrix products, arithmetic and copies ran while one was open for 7% -> 7% of each run, Pallas kernels for 14% -> 14%
where the time goes in v3:
time: 1090 us; the launch traced here: 1080 us
  waiting for transfers between devices  495 us (45%)
  Pallas kernels  248 us (23%)
  starting transfers between devices  207 us (19%)
  other arithmetic  68 us (6%)
  local copies, waits for them, and re-layouts  42.4 us (4%)
  between operations  16.1 us (1%)
    ppermute x56, waiting for transfers between devices, shifted(): lax.ppermute(value, axis, [(source, source + steps) for source in names])  254 us
    pallas_call x20, Pallas kernels, call(): return lambda *args: run(*args, *waits)  231 us
    ppermute x50, waiting for transfers between devices, swapped(): lax.ppermute(value, axis, [(source, source ^ bit) for source in range(cou...  199 us
    ppermute x56, starting transfers between devices, shifted(): lax.ppermute(value, axis, [(source, source + steps) for source in names])  171 us
    ppermute x50, starting transfers between devices, swapped(): lax.ppermute(value, axis, [(source, source ^ bit) for source in range(cou...  35.2 us
    reduce_scatter x1, waiting for transfers between devices, per_device(): lax.psum_scatter(dense_second, 'far', scatter_dimension=0, tiled=True)[0]  22.2 us
  transfers between devices with their start and end apart: 114, of which 57 were waited for; matrix products, arithmetic and copies ran while one was open for 7% of the time, Pallas kernels for 14%

profile of v3, /device:TPU:0, one launch (start us, length us, event | category | flops | bytes accessed | tf_op | source)
XLA Modules:
  0.0 1076.4 jit_solution(13024143942917648697)
XLA Ops:
  24.7 9.6 collective-permute-done.3.refs_2_
  39.3 13.5 %collective-permute-done.2.refs_8_.refs_12_.refs_10_.refs_16_.refs_5_.refs_13_ = bf16[256,3072]{1,0:T(8,128)(2,1)S(1)} collective-permute-done((bf16[256,3072]{1,0:T(8,128)(2,1)}, bf16[256,3072]{1,0:T(8,128)(2,1)S(1)}, u32[]{:S(2)}, u32[]{:S(2)}) %collective-permute-start.2) | collective-permute-done | bytes 1572896 | tf_op jit(solution)/shard_map/ppermute | solution.py:34
  76.0 8.5 collective-permute-done.10.refs_7_
  89.3 9.2 collective-permute-done.20.refs_14_.refs_17_
  125.1 6.6 collective-permute-done.22.refs_16_.refs_19_
  136.5 12.8 %attend.2 = (bf16[256,1024]{1,0:T(8,128)(2,1)}, f32[256,128]{1,0:T(8,128)}, f32[256,1024]{1,0:T(8,128)}, bf16[256,1024]{1,0:T(8,128)(2,1)}) custom-call(s32[3]{0:T(128)} %add_add_fusion.refs_0_, bf16[256,1024]{1,0:T(8,128)(2,1)} %get-tuple-element.128.refs_1_.refs_6_, bf16[256,1024]{1,0:T(8,128)(2,1)} %get-tuple-element.129.refs_2_.refs_8_, ...), custom_call_target="tpu_custom_call" | custom-call | flops 3221225472 | bytes 2097152 | tf_op jit(solution)/shard_map/attend/pallas_call | solution.py:120
  158.7 27.3 %collective-permute-done.28.refs_22_.refs_25_ = bf16[2,768,512]{2,1,0:T(8,128)(2,1)} collective-permute-done((bf16[2,768,512]{2,1,0:T(8,128)(2,1)}, bf16[2,768,512]{2,1,0:T(8,128)(2,1)}, u32[]{:S(2)}, u32[]{:S(2)}) %collective-permute-start.28) | collective-permute-done | bytes 1572896 | tf_op jit(solution)/shard_map/ppermute | solution.py:34
  194.6 8.4 collective-permute-done.17.refs_5_
  218.8 8.4 collective-permute-done.36.refs_30_.refs_33_
  233.0 13.2 %collective-permute-done.19.refs_7_ = bf16[256,1024]{1,0:T(8,128)(2,1)} collective-permute-done((bf16[256,1024]{1,0:T(8,128)(2,1)}, bf16[256,1024]{1,0:T(8,128)(2,1)}, u32[]{:S(2)}, u32[]{:S(2)}) %collective-permute-start.19) | collective-permute-done | bytes 524320 | tf_op jit(solution)/shard_map/ppermute | solution.py:29
  246.6 20.0 %collective-permute-done.34.refs_28_.refs_31_ = bf16[1,768,512]{2,1,0:T(8,128)(2,1)} collective-permute-done((bf16[1,768,512]{2,1,0:T(8,128)(2,1)S(1)}, bf16[1,768,512]{2,1,0:T(8,128)(2,1)}, u32[]{:S(2)}, u32[]{:S(2)}) %collective-permute-start.34) | collective-permute-done | bytes 786464 | tf_op jit(solution)/shard_map/ppermute | solution.py:34
  269.7 11.6 %collective-permute-done.38.refs_32_.refs_35_ = bf16[1,768,512]{2,1,0:T(8,128)(2,1)} collective-permute-done((bf16[1,768,512]{2,1,0:T(8,128)(2,1)S(1)}, bf16[1,768,512]{2,1,0:T(8,128)(2,1)}, u32[]{:S(2)}, u32[]{:S(2)}) %collective-permute-start.38) | collective-permute-done | bytes 786464 | tf_op jit(solution)/shard_map/ppermute | solution.py:34
  284.7 22.8 %experts.2 = (bf16[4,256,1024]{2,1,0:T(8,128)(2,1)}, bf16[4,256,1024]{2,1,0:T(8,128)(2,1)}, bf16[4,512,1024]{2,1,0:T(8,128)(2,1)}, f32[4,32,256]{2,1,0:T(8,128)}...) custom-call(s32[3]{0:T(128)} %add_add_fusion.refs_0_, ...), custom_call_target="tpu_custom_call" | custom-call | flops 6442450944 | bytes 25165824 | tf_op jit(solution)/shard_map/experts/pallas_call | solution.py:120
  316.1 10.3 collective-permute-done.40
  335.4 8.7 collective-permute-done.41
  346.7 9.1 collective-permute-start.42
  378.8 8.8 collective-permute-done.46.refs_3_.refs_9_
  391.9 7.5 collective-permute-done.47.refs_4_.refs_10_
  400.3 12.6 %attend.3 = (bf16[256,1024]{1,0:T(8,128)(2,1)}, f32[256,128]{1,0:T(8,128)}, f32[256,1024]{1,0:T(8,128)}, bf16[256,1024]{1,0:T(8,128)(2,1)}) custom-call(s32[3]{0:T(128)} %add_add_fusion.2.refs_0_, bf16[256,1024]{1,0:T(8,128)(2,1)} %get-tuple-element.147.refs_1_.refs_6_, bf16[256,1024]{1,0:T(8,128)(2,1)} %get-tuple-element.148.refs_2_.refs_8_, ...), custom_call_target="tpu_custom_call" | custom-call | flops 3221225472 | bytes 2097152 | tf_op jit(solution)/shard_map/attend/pallas_call | solution.py:120
  418.6 6.9 collective-permute-done.48.refs_2_
  431.5 7.4 collective-permute-done.49.refs_3_
  455.7 22.5 %experts.3 = (bf16[4,256,1024]{2,1,0:T(8,128)(2,1)}, bf16[4,256,1024]{2,1,0:T(8,128)(2,1)}, bf16[4,512,1024]{2,1,0:T(8,128)(2,1)}, f32[4,32,256]{2,1,0:T(8,128)}...) custom-call(s32[3]{0:T(128)} %add_add_fusion.2.refs_0_, ...), custom_call_target="tpu_custom_call" | custom-call | flops 6442450944 | bytes 25165824 | tf_op jit(solution)/shard_map/experts/pallas_call | solution.py:120
  478.2 25.6 %experts_back.2 = (bf16[4,256,1024]{2,1,0:T(8,128)(2,1)}, f32[32,1024]{1,0:T(8,128)}, bf16[4,512,1024]{2,1,0:T(8,128)(2,1)}, bf16[8,256,512]{2,1,0:T(8,128)(2,1)...) custom-call(s32[3]{0:T(128)} %add_add_fusion.2.refs_0_, bf16[256,1152]{1,0:T(8,128)(2,1)} %copy-done.36, ...), custom_call_target="tpu_custom_call" | custom-call | flops 6442450944 | bytes 25165824 | tf_op jit(solution)/shard_map/experts_back/pallas_call | solution.py:120
  505.9 14.1 %collective-permute-done.56.refs_8_ = bf16[8,256,512]{2,1,0:T(8,128)(2,1)S(1)} collective-permute-done((bf16[8,256,512]{2,1,0:T(8,128)(2,1)S(1)}, bf16[8,256,512]{2,1,0:T(8,128)(2,1)S(1)}, u32[]{:S(2)}, u32[]{:S(2)}) %collective-permute-start.56) | collective-permute-done | bytes 2097184 | tf_op jit(solution)/shard_map/ppermute | solution.py:34
  526.4 9.7 expert_grads.6.refs_20_.refs_12_
  536.1 10.9 %reduce-scatter.9.cloned.1.call-done = bf16[1,256,1024]{2,1,0:T(8,128)(2,1)} async-done(((bf16[4,256,1024]{2,1,0:T(8,128)(2,1)}), bf16[1,256,1024]{2,1,0:T(8,128)(2,1)}) %reduce-scatter.9.cloned.1.call-update) | async-done | bytes 524304 | tf_op jit(solution)/shard_map/reduce_scatter | solution.py:925
  549.1 16.2 %attend_back.2 = (f32[256,1024]{1,0:T(8,128)}, bf16[256,1024]{1,0:T(8,128)(2,1)}, f32[256,1024]{1,0:T(8,128)}, bf16[256,1024]{1,0:T(8,128)(2,1)}, bf16[256,1024]...) custom-call(s32[3]{0:T(128)} %add_add_fusion.2.refs_0_, ...), custom_call_target="tpu_custom_call" | custom-call | flops 8053063680 | bytes 2097152 | tf_op jit(solution)/shard_map/attend_back/pallas_call | solution.py:120
  565.4 9.8 expert_grads.7.refs_9_
  577.6 14.1 %collective-permute-done.59 = bf16[256,1024]{1,0:T(8,128)(2,1)S(1)} collective-permute-done((bf16[256,1024]{1,0:T(8,128)(2,1)S(1)}, bf16[256,1024]{1,0:T(8,128)(2,1)S(1)}, u32[]{:S(2)}, u32[]{:S(2)}) %collective-permute-start.59) | collective-permute-done | bytes 524320 | tf_op jit(solution)/shard_map/ppermute | solution.py:29
  598.3 8.2 collective-permute-done.60.refs_4_
  607.3 8.0 keyval_back.2
  626.2 10.1 collective-permute-done.61.refs_2_
  642.0 9.3 collective-permute-done.62.refs_3_
  657.2 8.4 collective-permute-done.63.refs_4_
  670.5 26.1 %experts_back.3 = (bf16[4,256,1024]{2,1,0:T(8,128)(2,1)}, f32[32,1024]{1,0:T(8,128)}, bf16[4,512,1024]{2,1,0:T(8,128)(2,1)}, bf16[8,256,512]{2,1,0:T(8,128)(2,1)...) custom-call(s32[3]{0:T(128)} %add_add_fusion.refs_0_, ...), custom_call_target="tpu_custom_call" | custom-call | flops 6442450944 | bytes 25165824 | tf_op jit(solution)/shard_map/experts_back/pallas_call | solution.py:120
  696.7 8.5 reduce-scatter.13.cloned.1.call-done
  710.7 10.3 collective-permute-done.67.refs_11_
  730.5 22.2 %reduce-scatter.15.cloned.1.call-done = bf16[1,256,3200]{2,1,0:T(8,128)(2,1)} async-done(((bf16[2,256,3200]{2,1,0:T(8,128)(2,1)}), bf16[1,256,3200]{2,1,0:T(8,128)(2,1)}) %reduce-scatter.15.cloned.1.call-update) | async-done | bytes 1638416 | tf_op jit(solution)/shard_map/reduce_scatter | solution.py:1180
  772.2 9.7 collective-permute-done.69
  787.3 15.8 %attend_back.3 = (f32[256,1024]{1,0:T(8,128)}, bf16[256,1024]{1,0:T(8,128)(2,1)}, f32[256,1024]{1,0:T(8,128)}, bf16[256,1024]{1,0:T(8,128)(2,1)}, bf16[256,1024]...) custom-call(s32[3]{0:T(128)} %add_add_fusion.refs_0_, ...), custom_call_target="tpu_custom_call" | custom-call | flops 8053063680 | bytes 2097152 | tf_op jit(solution)/shard_map/attend_back/pallas_call | solution.py:120
  810.8 13.3 %collective-permute-done.81 = bf16[256,1024]{1,0:T(8,128)(2,1)S(1)} collective-permute-done((bf16[256,1024]{1,0:T(8,128)(2,1)S(1)}, bf16[256,1024]{1,0:T(8,128)(2,1)S(1)}, u32[]{:S(2)}, u32[]{:S(2)}) %collective-permute-start.81) | collective-permute-done | bytes 524320 | tf_op jit(solution)/shard_map/ppermute | solution.py:29
  838.8 7.8 keyval_back.3
  876.4 42.6 %collective-permute-done.88 = bf16[1,256,3200]{2,1,0:T(8,128)(2,1)} collective-permute-done((bf16[1,256,3200]{2,1,0:T(8,128)(2,1)}, bf16[1,256,3200]{2,1,0:T(8,128)(2,1)}, u32[]{:S(2)}, u32[]{:S(2)}) %collective-permute-start.88) | collective-permute-done | bytes 1638432 | tf_op jit(solution)/shard_map/ppermute | solution.py:34
  920.8 18.1 %collective-permute-done.90 = bf16[2,768,512]{2,1,0:T(8,128)(2,1)} collective-permute-done((bf16[2,768,512]{2,1,0:T(8,128)(2,1)}, bf16[2,768,512]{2,1,0:T(8,128)(2,1)}, u32[]{:S(2)}, u32[]{:S(2)}) %collective-permute-start.90) | collective-permute-done | bytes 1572896 | tf_op jit(solution)/shard_map/ppermute | solution.py:34
  969.3 18.5 %collective-permute-done.94 = bf16[256,1024]{1,0:T(8,128)(2,1)S(1)} collective-permute-done((bf16[256,1024]{1,0:T(8,128)(2,1)S(1)}, bf16[256,1024]{1,0:T(8,128)(2,1)S(1)}, u32[]{:S(2)}, u32[]{:S(2)}) %collective-permute-start.94) | collective-permute-done | bytes 524320 | tf_op jit(solution)/shard_map/ppermute | solution.py:29
  994.8 20.3 %collective-permute-start.98 = (bf16[64,6400]{1,0:T(8,128)(2,1)}, bf16[64,6400]{1,0:T(8,128)(2,1)}, u32[]{:S(2)}, u32[]{:S(2)}) collective-permute-start(bf16[64,6400]{1,0:T(8,128)(2,1)} %get-tuple-element.309), channel_id=1, source_target_pairs={{0,1},{1,2},{4,5},{5,6},{8,9},{9,10},{12,13},{13,14},{16,17},{17,1... | collective-permute-start | bytes 2457608 | tf_op jit(solution)/shard_map/ppermute | solution.py:29
  1021.3 7.5 collective-permute-done.98
  1036.1 14.5 %collective-permute-done.105 = bf16[2,768,512]{2,1,0:T(8,128)(2,1)S(1)} collective-permute-done((bf16[2,768,512]{2,1,0:T(8,128)(2,1)S(1)}, bf16[2,768,512]{2,1,0:T(8,128)(2,1)S(1)}, u32[]{:S(2)}, u32[]{:S(2)}) %collective-permute-start.105) | collective-permute-done | bytes 1572896 | tf_op jit(solution)/shard_map/ppermute | solution.py:34
  (506 shorter events, 415.0 us)
Async XLA Ops:
  7.2 539.8 %reduce-scatter.9.cloned.1.call-start = ((), (), s32[]{:S(2)}) async-start(), calls=%async_computation.8 | async-start | bytes 2621440 | tf_op jit(solution)/shard_map/reduce_scatter | solution.py:925
  16.7 36.1 %collective-permute-start.2 = (bf16[256,3072]{1,0:T(8,128)(2,1)}, bf16[256,3072]{1,0:T(8,128)(2,1)S(1)}, u32[]{:S(2)}, u32[]{:S(2)}) collective-permute-start(bf16[256,3072]{1,0:T(8,128)(2,1)} %pack_dense.1), channel_id=1, source_target_pairs={{0,16},{16,0},{1,17},{17,1},{2,18},{18,2},{3,19},{19,3},{4,20},{20... | collective-permute-start | bytes 4718600 | tf_op jit(solution)/shard_map/ppermute | solution.py:34
  52.8 35.0 %collective-permute-start.6 = (bf16[256,3072]{1,0:T(8,128)(2,1)S(1)}, bf16[256,3072]{1,0:T(8,128)(2,1)}, u32[]{:S(2)}, u32[]{:S(2)}) collective-permute-start(bf16[256,3072]{1,0:T(8,128)(2,1)S(1)} %collective-permute-done.2.refs_8_.refs_12_.refs_10_.refs_16_.refs_5_.refs_13_), channel_id=1, source_target_pairs={{0,8},{8,0},{1,9},{9,1},{2,10},{10,2},{3,11},{11,3},{4,12},{12,4},... | collective-permute-start | bytes 4718600 | tf_op jit(solution)/shard_map/ppermute | solution.py:34
  64.3 34.2 %collective-permute-start.20 = (bf16[2,768,512]{2,1,0:T(8,128)(2,1)}, bf16[2,768,512]{2,1,0:T(8,128)(2,1)}, u32[]{:S(2)}, u32[]{:S(2)}) collective-permute-start(bf16[2,768,512]{2,1,0:T(8,128)(2,1)} %pack_experts.5), channel_id=1, source_target_pairs={{0,16},{16,0},{1,17},{17,1},{2,18},{18,2},{3,19},{19,3},{4,20},{20... | collective-permute-start | bytes 4718600 | tf_op jit(solution)/shard_map/ppermute | solution.py:34
  76.0 27.7 %collective-permute-start.5 = (bf16[256,3072]{1,0:T(8,128)(2,1)S(1)}, bf16[256,3072]{1,0:T(8,128)(2,1)}, u32[]{:S(2)}, u32[]{:S(2)}) collective-permute-start(bf16[256,3072]{1,0:T(8,128)(2,1)S(1)} %collective-permute-done.2.refs_8_.refs_12_.refs_10_.refs_16_.refs_5_.refs_13_), channel_id=1, source_target_pairs={{0,4},{4,0},{1,5},{5,1},{2,6},{6,2},{3,7},{7,3},{8,12},{12,8},{9,1... | collective-permute-start | bytes 4718600 | tf_op jit(solution)/shard_map/ppermute | solution.py:34
  98.4 33.2 %collective-permute-start.22 = (bf16[2,768,512]{2,1,0:T(8,128)(2,1)}, bf16[2,768,512]{2,1,0:T(8,128)(2,1)}, u32[]{:S(2)}, u32[]{:S(2)}) collective-permute-start(bf16[2,768,512]{2,1,0:T(8,128)(2,1)} %collective-permute-done.20.refs_14_.refs_17_), channel_id=1, source_target_pairs={{0,8},{8,0},{1,9},{9,1},{2,10},{10,2},{3,11},{11,3},{4,12},{12,4},... | collective-permute-start | bytes 4718600 | tf_op jit(solution)/shard_map/ppermute | solution.py:34
  114.6 42.7 %collective-permute-start.24 = (bf16[2,768,512]{2,1,0:T(8,128)(2,1)}, bf16[2,768,512]{2,1,0:T(8,128)(2,1)S(1)}, u32[]{:S(2)}, u32[]{:S(2)}) collective-permute-start(bf16[2,768,512]{2,1,0:T(8,128)(2,1)} %pack_experts.6), channel_id=1, source_target_pairs={{0,16},{16,0},{1,17},{17,1},{2,18},{18,2},{3,19},{19,3},{4,20},{20... | collective-permute-start | bytes 4718600 | tf_op jit(solution)/shard_map/ppermute | solution.py:34
  119.1 66.9 %collective-permute-start.28 = (bf16[2,768,512]{2,1,0:T(8,128)(2,1)}, bf16[2,768,512]{2,1,0:T(8,128)(2,1)}, u32[]{:S(2)}, u32[]{:S(2)}) collective-permute-start(bf16[2,768,512]{2,1,0:T(8,128)(2,1)} %pack_experts.7), channel_id=1, source_target_pairs={{0,16},{16,0},{1,17},{17,1},{2,18},{18,2},{3,19},{19,3},{4,20},{20... | collective-permute-start | bytes 4718600 | tf_op jit(solution)/shard_map/ppermute | solution.py:34
  119.7 67.6 %collective-permute-start.21 = (bf16[2,768,512]{2,1,0:T(8,128)(2,1)}, bf16[2,768,512]{2,1,0:T(8,128)(2,1)}, u32[]{:S(2)}, u32[]{:S(2)}) collective-permute-start(bf16[2,768,512]{2,1,0:T(8,128)(2,1)} %collective-permute-done.20.refs_14_.refs_17_), channel_id=1, source_target_pairs={{0,4},{4,0},{1,5},{5,1},{2,6},{6,2},{3,7},{7,3},{8,12},{12,8},{9,1... | collective-permute-start | bytes 4718600 | tf_op jit(solution)/shard_map/ppermute | solution.py:34
  131.7 75.3 %collective-permute-start.23 = (bf16[2,768,512]{2,1,0:T(8,128)(2,1)}, bf16[2,768,512]{2,1,0:T(8,128)(2,1)}, u32[]{:S(2)}, u32[]{:S(2)}) collective-permute-start(bf16[2,768,512]{2,1,0:T(8,128)(2,1)} %collective-permute-done.22.refs_16_.refs_19_), channel_id=1, source_target_pairs={{0,4},{4,0},{1,5},{5,1},{2,6},{6,2},{3,7},{7,3},{8,12},{12,8},{9,1... | collective-permute-start | bytes 4718600 | tf_op jit(solution)/shard_map/ppermute | solution.py:34
  149.3 39.5 %collective-permute-start.14 = (bf16[256,1024]{1,0:T(8,128)(2,1)}, bf16[256,1024]{1,0:T(8,128)(2,1)}, u32[]{:S(2)}, u32[]{:S(2)}) collective-permute-start(bf16[256,1024]{1,0:T(8,128)(2,1)} %get-tuple-element.131.refs_1_), channel_id=1, source_target_pairs={{0,1},{1,2},{2,3},{4,5},{5,6},{6,7},{8,9},{9,10},{10,11},{12,13},{... | collective-permute-start | bytes 1572872 | tf_op jit(solution)/shard_map/ppermute | solution.py:29
  157.4 49.6 %collective-permute-start.32 = (bf16[1,768,512]{2,1,0:T(8,128)(2,1)}, bf16[1,768,512]{2,1,0:T(8,128)(2,1)S(1)}, u32[]{:S(2)}, u32[]{:S(2)}) collective-permute-start(bf16[1,768,512]{2,1,0:T(8,128)(2,1)} %pack_experts.8), channel_id=1, source_target_pairs={{0,16},{16,0},{1,17},{17,1},{2,18},{18,2},{3,19},{19,3},{4,20},{20... | collective-permute-start | bytes 2359304 | tf_op jit(solution)/shard_map/ppermute | solution.py:34
  187.3 41.4 %collective-permute-start.26 = (bf16[2,768,512]{2,1,0:T(8,128)(2,1)S(1)}, bf16[2,768,512]{2,1,0:T(8,128)(2,1)}, u32[]{:S(2)}, u32[]{:S(2)}) collective-permute-start(bf16[2,768,512]{2,1,0:T(8,128)(2,1)S(1)} %collective-permute-done.24.refs_18_.refs_21_), channel_id=1, source_target_pairs={{0,8},{8,0},{1,9},{9,1},{2,10},{10,2},{3,11},{11,3},{4,12},{12,4},... | collective-permute-start | bytes 4718600 | tf_op jit(solution)/shard_map/ppermute | solution.py:34
  207.0 25.5 %collective-permute-start.25 = (bf16[2,768,512]{2,1,0:T(8,128)(2,1)S(1)}, bf16[2,768,512]{2,1,0:T(8,128)(2,1)}, u32[]{:S(2)}, u32[]{:S(2)}) collective-permute-start(bf16[2,768,512]{2,1,0:T(8,128)(2,1)S(1)} %collective-permute-done.24.refs_18_.refs_21_), channel_id=1, source_target_pairs={{0,4},{4,0},{1,5},{5,1},{2,6},{6,2},{3,7},{7,3},{8,12},{12,8},{9,1... | collective-permute-start | bytes 4718600 | tf_op jit(solution)/shard_map/ppermute | solution.py:34
  208.6 58.1 %collective-permute-start.30 = (bf16[2,768,512]{2,1,0:T(8,128)(2,1)}, bf16[2,768,512]{2,1,0:T(8,128)(2,1)}, u32[]{:S(2)}, u32[]{:S(2)}) collective-permute-start(bf16[2,768,512]{2,1,0:T(8,128)(2,1)} %collective-permute-done.28.refs_22_.refs_25_), channel_id=1, source_target_pairs={{0,8},{8,0},{1,9},{9,1},{2,10},{10,2},{3,11},{11,3},{4,12},{12,4},... | collective-permute-start | bytes 4718600 | tf_op jit(solution)/shard_map/ppermute | solution.py:34
  227.2 39.5 %collective-permute-start.34 = (bf16[1,768,512]{2,1,0:T(8,128)(2,1)S(1)}, bf16[1,768,512]{2,1,0:T(8,128)(2,1)}, u32[]{:S(2)}, u32[]{:S(2)}) collective-permute-start(bf16[1,768,512]{2,1,0:T(8,128)(2,1)S(1)} %collective-permute-done.32.refs_26_.refs_29_), channel_id=1, source_target_pairs={{0,8},{8,0},{1,9},{9,1},{2,10},{10,2},{3,11},{11,3},{4,12},{12,4},... | collective-permute-start | bytes 2359304 | tf_op jit(solution)/shard_map/ppermute | solution.py:34
  228.7 40.5 %collective-permute-start.29 = (bf16[2,768,512]{2,1,0:T(8,128)(2,1)}, bf16[2,768,512]{2,1,0:T(8,128)(2,1)}, u32[]{:S(2)}, u32[]{:S(2)}) collective-permute-start(bf16[2,768,512]{2,1,0:T(8,128)(2,1)} %collective-permute-done.28.refs_22_.refs_25_), channel_id=1, source_target_pairs={{0,4},{4,0},{1,5},{5,1},{2,6},{6,2},{3,7},{7,3},{8,12},{12,8},{9,1... | collective-permute-start | bytes 4718600 | tf_op jit(solution)/shard_map/ppermute | solution.py:34
  232.4 36.7 %collective-permute-start.33 = (bf16[1,768,512]{2,1,0:T(8,128)(2,1)S(1)}, bf16[1,768,512]{2,1,0:T(8,128)(2,1)}, u32[]{:S(2)}, u32[]{:S(2)}) collective-permute-start(bf16[1,768,512]{2,1,0:T(8,128)(2,1)S(1)} %collective-permute-done.32.refs_26_.refs_29_), channel_id=1, source_target_pairs={{0,4},{4,0},{1,5},{5,1},{2,6},{6,2},{3,7},{7,3},{8,12},{12,8},{9,1... | collective-permute-start | bytes 2359304 | tf_op jit(solution)/shard_map/ppermute | solution.py:34
  246.1 35.2 %collective-permute-start.38 = (bf16[1,768,512]{2,1,0:T(8,128)(2,1)S(1)}, bf16[1,768,512]{2,1,0:T(8,128)(2,1)}, u32[]{:S(2)}, u32[]{:S(2)}) collective-permute-start(bf16[1,768,512]{2,1,0:T(8,128)(2,1)S(1)} %collective-permute-done.36.refs_30_.refs_33_), channel_id=1, source_target_pairs={{0,8},{8,0},{1,9},{9,1},{2,10},{10,2},{3,11},{11,3},{4,12},{12,4},... | collective-permute-start | bytes 2359304 | tf_op jit(solution)/shard_map/ppermute | solution.py:34
  503.8 22.6 %collective-permute-start.55 = (bf16[4,512,1024]{2,1,0:T(8,128)(2,1)}, bf16[4,512,1024]{2,1,0:T(8,128)(2,1)}, u32[]{:S(2)}, u32[]{:S(2)}) collective-permute-start(bf16[4,512,1024]{2,1,0:T(8,128)(2,1)} %get-tuple-element.160.refs_2_), channel_id=1, source_target_pairs={{0,4},{4,0},{1,5},{5,1},{2,6},{6,2},{3,7},{7,3},{8,12},{12,8},{9,1... | collective-permute-start | bytes 12582920 | tf_op jit(solution)/shard_map/ppermute | solution.py:34
  503.9 22.5 %collective-permute-start.54 = (bf16[4,512,1024]{2,1,0:T(8,128)(2,1)}, bf16[4,512,1024]{2,1,0:T(8,128)(2,1)}, u32[]{:S(2)}, u32[]{:S(2)}) collective-permute-start(bf16[4,512,1024]{2,1,0:T(8,128)(2,1)} %get-tuple-element.152.refs_1_), channel_id=1, source_target_pairs={{0,4},{4,0},{1,5},{5,1},{2,6},{6,2},{3,7},{7,3},{8,12},{12,8},{9,1... | collective-permute-start | bytes 12582920 | tf_op jit(solution)/shard_map/ppermute | solution.py:34
  504.4 165.3 %reduce-scatter.11.cloned.1.call-start = ((), (), s32[]{:S(2)}) async-start(), calls=%async_computation.9 | async-start | bytes 9437184 | tf_op jit(solution)/shard_map/reduce_scatter | solution.py:1040
  547.0 158.2 %reduce-scatter.13.cloned.1.call-start = ((), (), s32[]{:S(2)}) async-start(), calls=%async_computation.10 | async-start | bytes 9437184 | tf_op jit(solution)/shard_map/reduce_scatter | solution.py:1040
  575.2 177.5 %reduce-scatter.15.cloned.1.call-start = ((), (), s32[]{:S(2)}) async-start(), calls=%async_computation.11 | async-start | bytes 4915200 | tf_op jit(solution)/shard_map/reduce_scatter | solution.py:1180
  620.6 241.3 %reduce-scatter.19.cloned.1.call-start = ((), (), s32[]{:S(2)}) async-start(), calls=%async_computation.13 | async-start | bytes 4718592 | tf_op jit(solution)/shard_map/reduce_scatter | solution.py:1040
  657.1 67.0 %collective-permute-start.73 = (bf16[4,512,1024]{2,1,0:T(8,128)(2,1)}, bf16[4,512,1024]{2,1,0:T(8,128)(2,1)}, u32[]{:S(2)}, u32[]{:S(2)}) collective-permute-start(bf16[4,512,1024]{2,1,0:T(8,128)(2,1)} %get-tuple-element.187.refs_1_), channel_id=1, source_target_pairs={{0,4},{4,0},{1,5},{5,1},{2,6},{6,2},{3,7},{7,3},{8,12},{12,8},{9,1... | collective-permute-start | bytes 12582920 | tf_op jit(solution)/shard_map/ppermute | solution.py:34
  696.6 56.2 %collective-permute-start.74 = (bf16[4,512,1024]{2,1,0:T(8,128)(2,1)}, bf16[4,512,1024]{2,1,0:T(8,128)(2,1)}, u32[]{:S(2)}, u32[]{:S(2)}) collective-permute-start(bf16[4,512,1024]{2,1,0:T(8,128)(2,1)} %get-tuple-element.188.refs_2_), channel_id=1, source_target_pairs={{0,4},{4,0},{1,5},{5,1},{2,6},{6,2},{3,7},{7,3},{8,12},{12,8},{9,1... | collective-permute-start | bytes 12582920 | tf_op jit(solution)/shard_map/ppermute | solution.py:34
  721.0 31.8 %collective-permute-start.76 = (bf16[8,256,512]{2,1,0:T(8,128)(2,1)}, bf16[8,256,512]{2,1,0:T(8,128)(2,1)}, u32[]{:S(2)}, u32[]{:S(2)}) collective-permute-start(bf16[8,256,512]{2,1,0:T(8,128)(2,1)} %get-tuple-element.190.refs_4_), channel_id=1, source_target_pairs={{0,4},{4,0},{1,5},{5,1},{2,6},{6,2},{3,7},{7,3},{8,12},{12,8},{9,1... | collective-permute-start | bytes 6291464 | tf_op jit(solution)/shard_map/ppermute | solution.py:34
  721.0 31.7 %collective-permute-start.77 = (bf16[8,256,512]{2,1,0:T(8,128)(2,1)}, bf16[8,256,512]{2,1,0:T(8,128)(2,1)}, u32[]{:S(2)}, u32[]{:S(2)}) collective-permute-start(bf16[8,256,512]{2,1,0:T(8,128)(2,1)} %get-tuple-element.191.refs_5_), channel_id=1, source_target_pairs={{0,4},{4,0},{1,5},{5,1},{2,6},{6,2},{3,7},{7,3},{8,12},{12,8},{9,1... | collective-permute-start | bytes 6291464 | tf_op jit(solution)/shard_map/ppermute | solution.py:34
  724.1 34.0 %collective-permute-start.68 = (bf16[256,1024]{1,0:T(8,128)(2,1)}, bf16[256,1024]{1,0:T(8,128)(2,1)S(1)}, u32[]{:S(2)}, u32[]{:S(2)}) collective-permute-start(bf16[256,1024]{1,0:T(8,128)(2,1)} %get-tuple-element.342), channel_id=1, source_target_pairs={{0,1},{1,2},{4,5},{5,6},{8,9},{9,10},{12,13},{13,14},{16,17},{17,1... | collective-permute-start | bytes 1572872 | tf_op jit(solution)/shard_map/ppermute | solution.py:29
  729.8 28.3 %collective-permute-start.71 = (bf16[256,1024]{1,0:T(8,128)(2,1)}, bf16[256,1024]{1,0:T(8,128)(2,1)S(1)}, u32[]{:S(2)}, u32[]{:S(2)}) collective-permute-start(bf16[256,1024]{1,0:T(8,128)(2,1)} %get-tuple-element.343), channel_id=1, source_target_pairs={{2,1},{3,2},{6,5},{7,6},{10,9},{11,10},{14,13},{15,14},{18,17},{19... | collective-permute-start | bytes 1572872 | tf_op jit(solution)/shard_map/ppermute | solution.py:29
  765.1 96.8 %reduce-scatter.17.cloned.1.call-start = ((), (), s32[]{:S(2)}) async-start(), calls=%async_computation.12 | async-start | bytes 4718592 | tf_op jit(solution)/shard_map/reduce_scatter | solution.py:1040
  765.7 173.2 %reduce-scatter.23.cloned.1.call-start = ((), (), s32[]{:S(2)}) async-start(), calls=%async_computation.15 | async-start | bytes 4718592 | tf_op jit(solution)/shard_map/reduce_scatter | solution.py:1040
  808.5 207.7 %reduce-scatter.21.cloned.1.call-start = ((), (), s32[]{:S(2)}) async-start(), calls=%async_computation.14 | async-start | bytes 4718592 | tf_op jit(solution)/shard_map/reduce_scatter | solution.py:1040
  853.4 65.6 %collective-permute-start.88 = (bf16[1,256,3200]{2,1,0:T(8,128)(2,1)}, bf16[1,256,3200]{2,1,0:T(8,128)(2,1)}, u32[]{:S(2)}, u32[]{:S(2)}) collective-permute-start(bf16[1,256,3200]{2,1,0:T(8,128)(2,1)} %constant_dynamic-slice_fusion), channel_id=1, source_target_pairs={{0,8},{8,0},{1,9},{9,1},{2,10},{10,2},{3,11},{11,3},{4,12},{12,4},... | collective-permute-start | bytes 4915208 | tf_op jit(solution)/shard_map/ppermute | solution.py:34
  866.6 54.2 %collective-permute-start.89 = (bf16[2,768,512]{2,1,0:T(8,128)(2,1)}, bf16[2,768,512]{2,1,0:T(8,128)(2,1)}, u32[]{:S(2)}, u32[]{:S(2)}) collective-permute-start(bf16[2,768,512]{2,1,0:T(8,128)(2,1)} %get-tuple-element.333), channel_id=1, source_target_pairs={{0,16},{16,0},{1,17},{17,1},{2,18},{18,2},{3,19},{19,3},{4,20},{20... | collective-permute-start | bytes 4718600 | tf_op jit(solution)/shard_map/ppermute | solution.py:34
  869.7 69.2 %collective-permute-start.90 = (bf16[2,768,512]{2,1,0:T(8,128)(2,1)}, bf16[2,768,512]{2,1,0:T(8,128)(2,1)}, u32[]{:S(2)}, u32[]{:S(2)}) collective-permute-start(bf16[2,768,512]{2,1,0:T(8,128)(2,1)} %get-tuple-element.332), channel_id=1, source_target_pairs={{0,16},{16,0},{1,17},{17,1},{2,18},{18,2},{3,19},{19,3},{4,20},{20... | collective-permute-start | bytes 4718600 | tf_op jit(solution)/shard_map/ppermute | solution.py:34
  871.8 89.8 %collective-permute-start.93 = (bf16[256,1024]{1,0:T(8,128)(2,1)}, bf16[256,1024]{1,0:T(8,128)(2,1)S(1)}, u32[]{:S(2)}, u32[]{:S(2)}) collective-permute-start(bf16[256,1024]{1,0:T(8,128)(2,1)} %broadcast_select_fusion.5), channel_id=1, source_target_pairs={{0,16},{16,0},{1,17},{17,1},{2,18},{18,2},{3,19},{19,3},{4,20},{20... | collective-permute-start | bytes 1572872 | tf_op jit(solution)/shard_map/ppermute | solution.py:34
  941.8 74.4 %collective-permute-start.101 = (bf16[2,768,512]{2,1,0:T(8,128)(2,1)}, bf16[2,768,512]{2,1,0:T(8,128)(2,1)}, u32[]{:S(2)}, u32[]{:S(2)}) collective-permute-start(bf16[2,768,512]{2,1,0:T(8,128)(2,1)} %broadcast_select_fusion.1), channel_id=1, source_target_pairs={{0,16},{16,0},{1,17},{17,1},{2,18},{18,2},{3,19},{19,3},{4,20},{20... | collective-permute-start | bytes 4718600 | tf_op jit(solution)/shard_map/ppermute | solution.py:34
  956.7 36.6 %collective-permute-start.97 = (bf16[64,6400]{1,0:T(8,128)(2,1)S(1)}, bf16[64,6400]{1,0:T(8,128)(2,1)S(1)}, u32[]{:S(2)}, u32[]{:S(2)}) collective-permute-start(bf16[64,6400]{1,0:T(8,128)(2,1)S(1)} %get-tuple-element.311), channel_id=1, source_target_pairs={{0,1},{4,5},{8,9},{12,13},{16,17},{20,21},{24,25},{28,29}} | collective-permute-start | bytes 2457608 | tf_op jit(solution)/shard_map/ppermute | solution.py:29
  961.6 26.2 %collective-permute-start.94 = (bf16[256,1024]{1,0:T(8,128)(2,1)S(1)}, bf16[256,1024]{1,0:T(8,128)(2,1)S(1)}, u32[]{:S(2)}, u32[]{:S(2)}) collective-permute-start(bf16[256,1024]{1,0:T(8,128)(2,1)S(1)} %get-tuple-element.218), channel_id=1, source_target_pairs={{0,1},{1,2},{2,3},{4,5},{5,6},{6,7},{8,9},{9,10},{10,11},{12,13},{... | collective-permute-start | bytes 1572872 | tf_op jit(solution)/shard_map/ppermute | solution.py:29
  964.7 26.7 %collective-permute-start.95 = (bf16[256,1024]{1,0:T(8,128)(2,1)S(1)}, bf16[256,1024]{1,0:T(8,128)(2,1)S(1)}, u32[]{:S(2)}, u32[]{:S(2)}) collective-permute-start(bf16[256,1024]{1,0:T(8,128)(2,1)S(1)} %get-tuple-element.219), channel_id=1, source_target_pairs={{1,0},{2,1},{3,2},{5,4},{6,5},{7,6},{9,8},{10,9},{11,10},{13,12},{... | collective-permute-start | bytes 1572872 | tf_op jit(solution)/shard_map/ppermute | solution.py:29
  966.2 27.0 %collective-permute-start.100 = (bf16[64,6400]{1,0:T(8,128)(2,1)S(1)}, bf16[64,6400]{1,0:T(8,128)(2,1)S(1)}, u32[]{:S(2)}, u32[]{:S(2)}) collective-permute-start(bf16[64,6400]{1,0:T(8,128)(2,1)S(1)} %fusion.1), channel_id=1, source_target_pairs={{2,1},{3,2},{6,5},{7,6},{10,9},{11,10},{14,13},{15,14},{18,17},{19... | collective-permute-start | bytes 2457608 | tf_op jit(solution)/shard_map/ppermute | solution.py:29
  992.7 26.2 %collective-permute-start.96 = (bf16[256,1024]{1,0:T(8,128)(2,1)}, bf16[256,1024]{1,0:T(8,128)(2,1)}, u32[]{:S(2)}, u32[]{:S(2)}) collective-permute-start(bf16[256,1024]{1,0:T(8,128)(2,1)} %get-tuple-element.306), channel_id=1, source_target_pairs={{0,16},{16,0},{1,17},{17,1},{2,18},{18,2},{3,19},{19,3},{4,20},{20... | collective-permute-start | bytes 1572872 | tf_op jit(solution)/shard_map/ppermute | solution.py:34
  994.8 34.0 %collective-permute-start.98 = (bf16[64,6400]{1,0:T(8,128)(2,1)}, bf16[64,6400]{1,0:T(8,128)(2,1)}, u32[]{:S(2)}, u32[]{:S(2)}) collective-permute-start(bf16[64,6400]{1,0:T(8,128)(2,1)} %get-tuple-element.309), channel_id=1, source_target_pairs={{0,1},{1,2},{4,5},{5,6},{8,9},{9,10},{12,13},{13,14},{16,17},{17,1... | collective-permute-start | bytes 2457608 | tf_op jit(solution)/shard_map/ppermute | solution.py:29
  1017.8 32.8 %collective-permute-start.105 = (bf16[2,768,512]{2,1,0:T(8,128)(2,1)S(1)}, bf16[2,768,512]{2,1,0:T(8,128)(2,1)S(1)}, u32[]{:S(2)}, u32[]{:S(2)}) collective-permute-start(bf16[2,768,512]{2,1,0:T(8,128)(2,1)S(1)} %broadcast_select_fusion), channel_id=1, source_target_pairs={{0,16},{16,0},{1,17},{17,1},{2,18},{18,2},{3,19},{19,3},{4,20},{20... | collective-permute-start | bytes 4718600 | tf_op jit(solution)/shard_map/ppermute | solution.py:34
  1030.2 27.7 %collective-permute-start.102 = (bf16[64,6400]{1,0:T(8,128)(2,1)S(1)}, bf16[64,6400]{1,0:T(8,128)(2,1)S(1)}, u32[]{:S(2)}, u32[]{:S(2)}) collective-permute-start(bf16[64,6400]{1,0:T(8,128)(2,1)S(1)} %fusion.2), channel_id=1, source_target_pairs={{0,1},{1,2},{2,3},{4,5},{5,6},{6,7},{8,9},{9,10},{10,11},{12,13},{... | collective-permute-start | bytes 2457608 | tf_op jit(solution)/shard_map/ppermute | solution.py:29
  1034.6 23.3 %collective-permute-start.103 = (bf16[64,6400]{1,0:T(8,128)(2,1)S(1)}, bf16[64,6400]{1,0:T(8,128)(2,1)S(1)}, u32[]{:S(2)}, u32[]{:S(2)}) collective-permute-start(bf16[64,6400]{1,0:T(8,128)(2,1)S(1)} %copy-done.57), channel_id=1, source_target_pairs={{1,0},{2,1},{3,2},{5,4},{6,5},{7,6},{9,8},{10,9},{11,10},{13,12},{... | collective-permute-start | bytes 2457608 | tf_op jit(solution)/shard_map/ppermute | solution.py:29
  (158 other events, 2125.7 us)
Sparse Core Ops, SparseCore 0:
  504.5 42.4 reduce-scatter.8
  549.4 76.3 reduce-scatter.10
  628.1 77.0 reduce-scatter.12
  708.0 44.7 reduce-scatter.14
  765.2 43.3 reduce-scatter.18
  811.3 43.3 reduce-scatter.16
  856.9 70.1 reduce-scatter.22
  929.4 43.1 reduce-scatter.20

commit v4 on v3

--- a/solution.py
+++ b/solution.py
@@ -1153,7 +1153,7 @@
     next_chunk(earlier[-1])
     attended = layer_attend(x, query, keyval, earlier, weights[0], tables, infos[0])
     line_blocks = line_gather(attended[-1])
-    for block in line_blocks[0]:
+    for block in line_blocks[0][1:2] * 2 + line_blocks[0][2:3]:
         if crossing:
             next_chunk(block)
     while crossing:
@@ -1162,7 +1162,8 @@
     middle, sums, kept_first = layer_experts(
         x, query, keyval, earlier, attended, line_blocks, layers[0], tables, infos[0], both[0], marks
     )
-    between = layer_result(middle, sums)
+    between = lax.psum_scatter(sums, "expert", scatter_dimension=0, tiled=True)[0]
+    between = (middle + between.astype(f32)).astype(bf16)
     query, keyval = layer_project(between, weights[1], tables, infos[1])
     earlier = earlier_keys(keyval, tables)
     attended = layer_attend(between, query, keyval, earlier, weights[1], tables, infos[1])

time: 1090 us -> 1080 us (level)
  starting transfers between devices: 207 us -> 180 us
  waiting for transfers between devices: 495 us -> 518 us
    reduce_scatter x0 -> x1, waiting for transfers between devices: none -> 41.7 us  [per_device(): lax.psum_scatter(sums, 'expert', scatter_dimension=0, tiled=True)[0]]
    ppermute x56 -> x50, starting transfers between devices: 171 us -> 146 us  [shifted(): lax.ppermute(value, axis, [(source, source + steps) for source in names])]
    ppermute x56 -> x50, waiting for transfers between devices: 254 us -> 234 us  [shifted(): lax.ppermute(value, axis, [(source, source + steps) for source in names])]
  transfers between devices with their start and end apart: 114 -> 109, of which waited for: 57 -> 55; matrix products, arithmetic and copies ran while one was open for 7% -> 7% of each run, Pallas kernels for 14% -> 14%
where the time goes in v4:
time: 1080 us; the launch traced here: 1070 us
  waiting for transfers between devices  518 us (48%)
  Pallas kernels  249 us (23%)
  starting transfers between devices  180 us (17%)
  other arithmetic  63.4 us (6%)
  local copies, waits for them, and re-layouts  39.5 us (4%)
  between operations  15.8 us (1%)
    ppermute x50, waiting for transfers between devices, shifted(): lax.ppermute(value, axis, [(source, source + steps) for source in names])  234 us
    pallas_call x20, Pallas kernels, call(): return lambda *args: run(*args, *waits)  231 us
    ppermute x50, waiting for transfers between devices, swapped(): lax.ppermute(value, axis, [(source, source ^ bit) for source in range(cou...  198 us
    ppermute x50, starting transfers between devices, shifted(): lax.ppermute(value, axis, [(source, source + steps) for source in names])  146 us
    reduce_scatter x1, waiting for transfers between devices, per_device(): lax.psum_scatter(sums, 'expert', scatter_dimension=0, tiled=True)[0]  41.7 us
    ppermute x50, starting transfers between devices, swapped(): lax.ppermute(value, axis, [(source, source ^ bit) for source in range(cou...  33.6 us
    reduce_scatter x1, waiting for transfers between devices, per_device(): lax.psum_scatter(dense_second, 'far', scatter_dimension=0, tiled=True)[0]  23.4 us
  transfers between devices with their start and end apart: 109, of which 55 were waited for; matrix products, arithmetic and copies ran while one was open for 7% of the time, Pallas kernels for 14%

profile of v4, /device:TPU:0, one launch (start us, length us, event | category | flops | bytes accessed | tf_op | source)
XLA Modules:
  0.0 1065.7 jit_solution(5435259865781870612)
XLA Ops:
  24.6 9.6 collective-permute-done.3.refs_2_
  39.3 13.5 %collective-permute-done.2.refs_8_.refs_12_.refs_10_.refs_16_.refs_5_.refs_13_ = bf16[256,3072]{1,0:T(8,128)(2,1)S(1)} collective-permute-done((bf16[256,3072]{1,0:T(8,128)(2,1)}, bf16[256,3072]{1,0:T(8,128)(2,1)S(1)}, u32[]{:S(2)}, u32[]{:S(2)}) %collective-permute-start.2) | collective-permute-done | bytes 1572896 | tf_op jit(solution)/shard_map/ppermute | solution.py:34
  55.8 5.4 collective-permute-start.7
  76.0 8.5 collective-permute-done.10.refs_7_
  89.2 9.2 collective-permute-done.20.refs_14_.refs_17_
  125.1 6.5 collective-permute-done.22.refs_16_.refs_19_
  136.5 12.8 %attend.2 = (bf16[256,1024]{1,0:T(8,128)(2,1)}, f32[256,128]{1,0:T(8,128)}, f32[256,1024]{1,0:T(8,128)}, bf16[256,1024]{1,0:T(8,128)(2,1)}) custom-call(s32[3]{0:T(128)} %add_add_fusion.refs_0_, bf16[256,1024]{1,0:T(8,128)(2,1)} %get-tuple-element.128.refs_1_.refs_6_, bf16[256,1024]{1,0:T(8,128)(2,1)} %get-tuple-element.129.refs_2_.refs_8_, ...), custom_call_target="tpu_custom_call" | custom-call | flops 3221225472 | bytes 2097152 | tf_op jit(solution)/shard_map/attend/pallas_call | solution.py:120
  155.1 25.8 %collective-permute-done.28.refs_22_.refs_25_ = bf16[2,768,512]{2,1,0:T(8,128)(2,1)} collective-permute-done((bf16[2,768,512]{2,1,0:T(8,128)(2,1)}, bf16[2,768,512]{2,1,0:T(8,128)(2,1)}, u32[]{:S(2)}, u32[]{:S(2)}) %collective-permute-start.28) | collective-permute-done | bytes 1572896 | tf_op jit(solution)/shard_map/ppermute | solution.py:34
  206.7 10.8 %collective-permute-done.16.refs_4_.refs_37_ = bf16[256,1024]{1,0:T(8,128)(2,1)S(1)} collective-permute-done((bf16[256,1024]{1,0:T(8,128)(2,1)}, bf16[256,1024]{1,0:T(8,128)(2,1)S(1)}, u32[]{:S(2)}, u32[]{:S(2)}) %collective-permute-start.16) | collective-permute-done | bytes 524320 | tf_op jit(solution)/shard_map/ppermute | solution.py:29
  224.6 11.6 %collective-permute-done.19.refs_7_ = bf16[256,1024]{1,0:T(8,128)(2,1)} collective-permute-done((bf16[256,1024]{1,0:T(8,128)(2,1)}, bf16[256,1024]{1,0:T(8,128)(2,1)}, u32[]{:S(2)}, u32[]{:S(2)}) %collective-permute-start.19) | collective-permute-done | bytes 524320 | tf_op jit(solution)/shard_map/ppermute | solution.py:29
  236.2 29.8 %collective-permute-done.34.refs_28_.refs_31_ = bf16[1,768,512]{2,1,0:T(8,128)(2,1)} collective-permute-done((bf16[1,768,512]{2,1,0:T(8,128)(2,1)S(1)}, bf16[1,768,512]{2,1,0:T(8,128)(2,1)}, u32[]{:S(2)}, u32[]{:S(2)}) %collective-permute-start.34) | collective-permute-done | bytes 786464 | tf_op jit(solution)/shard_map/ppermute | solution.py:34
  270.2 9.6 collective-permute-done.38.refs_32_.refs_35_
  283.3 22.7 %experts.2 = (bf16[4,256,1024]{2,1,0:T(8,128)(2,1)}, bf16[4,256,1024]{2,1,0:T(8,128)(2,1)}, bf16[4,512,1024]{2,1,0:T(8,128)(2,1)}, f32[4,32,256]{2,1,0:T(8,128)}...) custom-call(s32[3]{0:T(128)} %add_add_fusion.refs_0_, ...), custom_call_target="tpu_custom_call" | custom-call | flops 6442450944 | bytes 25165824 | tf_op jit(solution)/shard_map/experts/pallas_call | solution.py:120
  308.2 41.7 %reduce-scatter.10.cloned.1.call-done = bf16[1,256,1024]{2,1,0:T(8,128)(2,1)} async-done(((bf16[4,256,1024]{2,1,0:T(8,128)(2,1)}), bf16[1,256,1024]{2,1,0:T(8,128)(2,1)}) %reduce-scatter.10.cloned.1.call-update) | async-done | bytes 524304 | tf_op jit(solution)/shard_map/reduce_scatter | solution.py:1165
  351.8 5.4 project.3
  358.6 11.6 %collective-permute-done.40.refs_3_.refs_9_ = bf16[256,1024]{1,0:T(8,128)(2,1)S(1)} collective-permute-done((bf16[256,1024]{1,0:T(8,128)(2,1)}, bf16[256,1024]{1,0:T(8,128)(2,1)S(1)}, u32[]{:S(2)}, u32[]{:S(2)}) %collective-permute-start.40) | collective-permute-done | bytes 524320 | tf_op jit(solution)/shard_map/ppermute | solution.py:29
  374.9 10.3 collective-permute-done.41.refs_4_.refs_10_
  386.1 12.6 %attend.3 = (bf16[256,1024]{1,0:T(8,128)(2,1)}, f32[256,128]{1,0:T(8,128)}, f32[256,1024]{1,0:T(8,128)}, bf16[256,1024]{1,0:T(8,128)(2,1)}) custom-call(s32[3]{0:T(128)} %add_add_fusion.2.refs_0_, bf16[256,1024]{1,0:T(8,128)(2,1)} %get-tuple-element.147.refs_1_.refs_6_, bf16[256,1024]{1,0:T(8,128)(2,1)} %get-tuple-element.148.refs_2_.refs_8_, ...), custom_call_target="tpu_custom_call" | custom-call | flops 3221225472 | bytes 2097152 | tf_op jit(solution)/shard_map/attend/pallas_call | solution.py:120
  404.4 8.4 collective-permute-done.42.refs_2_
  418.8 6.9 collective-permute-done.43.refs_3_
  443.3 22.5 %experts.3 = (bf16[4,256,1024]{2,1,0:T(8,128)(2,1)}, bf16[4,256,1024]{2,1,0:T(8,128)(2,1)}, bf16[4,512,1024]{2,1,0:T(8,128)(2,1)}, f32[4,32,256]{2,1,0:T(8,128)}...) custom-call(s32[3]{0:T(128)} %add_add_fusion.2.refs_0_, ...), custom_call_target="tpu_custom_call" | custom-call | flops 6442450944 | bytes 25165824 | tf_op jit(solution)/shard_map/experts/pallas_call | solution.py:120
  465.7 25.6 %experts_back.2 = (bf16[4,256,1024]{2,1,0:T(8,128)(2,1)}, f32[32,1024]{1,0:T(8,128)}, bf16[4,512,1024]{2,1,0:T(8,128)(2,1)}, bf16[8,256,512]{2,1,0:T(8,128)(2,1)...) custom-call(s32[3]{0:T(128)} %add_add_fusion.2.refs_0_, bf16[256,1152]{1,0:T(8,128)(2,1)} %copy-done.35, ...), custom_call_target="tpu_custom_call" | custom-call | flops 6442450944 | bytes 25165824 | tf_op jit(solution)/shard_map/experts_back/pallas_call | solution.py:120
  493.5 14.1 %collective-permute-done.50.refs_8_ = bf16[8,256,512]{2,1,0:T(8,128)(2,1)S(1)} collective-permute-done((bf16[8,256,512]{2,1,0:T(8,128)(2,1)S(1)}, bf16[8,256,512]{2,1,0:T(8,128)(2,1)S(1)}, u32[]{:S(2)}, u32[]{:S(2)}) %collective-permute-start.50) | collective-permute-done | bytes 2097184 | tf_op jit(solution)/shard_map/ppermute | solution.py:34
  507.8 6.1 collective-permute-done.52.refs_10_
  514.0 9.6 expert_grads.6.refs_20_.refs_12_
  523.6 12.3 %reduce-scatter.12.cloned.1.call-done = bf16[1,256,1024]{2,1,0:T(8,128)(2,1)} async-done(((bf16[4,256,1024]{2,1,0:T(8,128)(2,1)}), bf16[1,256,1024]{2,1,0:T(8,128)(2,1)}) %reduce-scatter.12.cloned.1.call-update) | async-done | bytes 524304 | tf_op jit(solution)/shard_map/reduce_scatter | solution.py:925
  538.0 16.3 %attend_back.2 = (f32[256,1024]{1,0:T(8,128)}, bf16[256,1024]{1,0:T(8,128)(2,1)}, f32[256,1024]{1,0:T(8,128)}, bf16[256,1024]{1,0:T(8,128)(2,1)}, bf16[256,1024]...) custom-call(s32[3]{0:T(128)} %add_add_fusion.2.refs_0_, ...), custom_call_target="tpu_custom_call" | custom-call | flops 8053063680 | bytes 2097152 | tf_op jit(solution)/shard_map/attend_back/pallas_call | solution.py:120
  554.2 9.9 expert_grads.7.refs_9_
  566.5 14.1 %collective-permute-done.53 = bf16[256,1024]{1,0:T(8,128)(2,1)S(1)} collective-permute-done((bf16[256,1024]{1,0:T(8,128)(2,1)S(1)}, bf16[256,1024]{1,0:T(8,128)(2,1)S(1)}, u32[]{:S(2)}, u32[]{:S(2)}) %collective-permute-start.53) | collective-permute-done | bytes 524320 | tf_op jit(solution)/shard_map/ppermute | solution.py:29
  587.2 8.2 collective-permute-done.54.refs_4_
  596.2 8.0 keyval_back.2
  615.2 10.1 collective-permute-done.55.refs_2_
  631.1 9.4 collective-permute-done.56.refs_3_
  646.3 8.5 collective-permute-done.57.refs_4_
  659.7 25.9 %experts_back.3 = (bf16[4,256,1024]{2,1,0:T(8,128)(2,1)}, f32[32,1024]{1,0:T(8,128)}, bf16[4,512,1024]{2,1,0:T(8,128)(2,1)}, bf16[8,256,512]{2,1,0:T(8,128)(2,1)...) custom-call(s32[3]{0:T(128)} %add_add_fusion.refs_0_, ...), custom_call_target="tpu_custom_call" | custom-call | flops 6442450944 | bytes 25165824 | tf_op jit(solution)/shard_map/experts_back/pallas_call | solution.py:120
  685.8 8.1 reduce-scatter.16.cloned.1.call-done
  699.4 10.3 collective-permute-done.61.refs_11_
  718.0 23.4 %reduce-scatter.18.cloned.1.call-done = bf16[1,256,3200]{2,1,0:T(8,128)(2,1)} async-done(((bf16[2,256,3200]{2,1,0:T(8,128)(2,1)}), bf16[1,256,3200]{2,1,0:T(8,128)(2,1)}) %reduce-scatter.18.cloned.1.call-update) | async-done | bytes 1638416 | tf_op jit(solution)/shard_map/reduce_scatter | solution.py:1181
  761.8 10.0 collective-permute-done.63
  777.1 15.9 %attend_back.3 = (f32[256,1024]{1,0:T(8,128)}, bf16[256,1024]{1,0:T(8,128)(2,1)}, f32[256,1024]{1,0:T(8,128)}, bf16[256,1024]{1,0:T(8,128)(2,1)}, bf16[256,1024]...) custom-call(s32[3]{0:T(128)} %add_add_fusion.refs_0_, ...), custom_call_target="tpu_custom_call" | custom-call | flops 8053063680 | bytes 2097152 | tf_op jit(solution)/shard_map/attend_back/pallas_call | solution.py:120
  800.7 13.1 %collective-permute-done.75 = bf16[256,1024]{1,0:T(8,128)(2,1)S(1)} collective-permute-done((bf16[256,1024]{1,0:T(8,128)(2,1)S(1)}, bf16[256,1024]{1,0:T(8,128)(2,1)S(1)}, u32[]{:S(2)}, u32[]{:S(2)}) %collective-permute-start.75) | collective-permute-done | bytes 524320 | tf_op jit(solution)/shard_map/ppermute | solution.py:29
  828.4 7.8 keyval_back.3
  866.1 43.4 %collective-permute-done.82 = bf16[1,256,3200]{2,1,0:T(8,128)(2,1)} collective-permute-done((bf16[1,256,3200]{2,1,0:T(8,128)(2,1)}, bf16[1,256,3200]{2,1,0:T(8,128)(2,1)}, u32[]{:S(2)}, u32[]{:S(2)}) %collective-permute-start.82) | collective-permute-done | bytes 1638432 | tf_op jit(solution)/shard_map/ppermute | solution.py:34
  911.4 16.8 %collective-permute-done.84 = bf16[2,768,512]{2,1,0:T(8,128)(2,1)} collective-permute-done((bf16[2,768,512]{2,1,0:T(8,128)(2,1)}, bf16[2,768,512]{2,1,0:T(8,128)(2,1)}, u32[]{:S(2)}, u32[]{:S(2)}) %collective-permute-start.84) | collective-permute-done | bytes 1572896 | tf_op jit(solution)/shard_map/ppermute | solution.py:34
  959.5 18.3 %collective-permute-done.88 = bf16[256,1024]{1,0:T(8,128)(2,1)S(1)} collective-permute-done((bf16[256,1024]{1,0:T(8,128)(2,1)S(1)}, bf16[256,1024]{1,0:T(8,128)(2,1)S(1)}, u32[]{:S(2)}, u32[]{:S(2)}) %collective-permute-start.88) | collective-permute-done | bytes 524320 | tf_op jit(solution)/shard_map/ppermute | solution.py:29
  984.5 20.2 %collective-permute-start.92 = (bf16[64,6400]{1,0:T(8,128)(2,1)}, bf16[64,6400]{1,0:T(8,128)(2,1)}, u32[]{:S(2)}, u32[]{:S(2)}) collective-permute-start(bf16[64,6400]{1,0:T(8,128)(2,1)} %get-tuple-element.309), channel_id=1, source_target_pairs={{0,1},{1,2},{4,5},{5,6},{8,9},{9,10},{12,13},{13,14},{16,17},{17,1... | collective-permute-start | bytes 2457608 | tf_op jit(solution)/shard_map/ppermute | solution.py:29
  1010.8 7.6 collective-permute-done.92
  1025.7 14.4 %collective-permute-done.99 = bf16[2,768,512]{2,1,0:T(8,128)(2,1)S(1)} collective-permute-done((bf16[2,768,512]{2,1,0:T(8,128)(2,1)S(1)}, bf16[2,768,512]{2,1,0:T(8,128)(2,1)S(1)}, u32[]{:S(2)}, u32[]{:S(2)}) %collective-permute-start.99) | collective-permute-done | bytes 1572896 | tf_op jit(solution)/shard_map/ppermute | solution.py:34
  (494 shorter events, 366.9 us)
Async XLA Ops:
  7.2 342.7 %reduce-scatter.10.cloned.1.call-start = ((), (), s32[]{:S(2)}) async-start(), calls=%async_computation.9 | async-start | bytes 2621440 | tf_op jit(solution)/shard_map/reduce_scatter | solution.py:1165
  16.6 36.1 %collective-permute-start.2 = (bf16[256,3072]{1,0:T(8,128)(2,1)}, bf16[256,3072]{1,0:T(8,128)(2,1)S(1)}, u32[]{:S(2)}, u32[]{:S(2)}) collective-permute-start(bf16[256,3072]{1,0:T(8,128)(2,1)} %pack_dense.1), channel_id=1, source_target_pairs={{0,16},{16,0},{1,17},{17,1},{2,18},{18,2},{3,19},{19,3},{4,20},{20... | collective-permute-start | bytes 4718600 | tf_op jit(solution)/shard_map/ppermute | solution.py:34
  52.8 35.0 %collective-permute-start.6 = (bf16[256,3072]{1,0:T(8,128)(2,1)S(1)}, bf16[256,3072]{1,0:T(8,128)(2,1)}, u32[]{:S(2)}, u32[]{:S(2)}) collective-permute-start(bf16[256,3072]{1,0:T(8,128)(2,1)S(1)} %collective-permute-done.2.refs_8_.refs_12_.refs_10_.refs_16_.refs_5_.refs_13_), channel_id=1, source_target_pairs={{0,8},{8,0},{1,9},{9,1},{2,10},{10,2},{3,11},{11,3},{4,12},{12,4},... | collective-permute-start | bytes 4718600 | tf_op jit(solution)/shard_map/ppermute | solution.py:34
  64.2 34.2 %collective-permute-start.20 = (bf16[2,768,512]{2,1,0:T(8,128)(2,1)}, bf16[2,768,512]{2,1,0:T(8,128)(2,1)}, u32[]{:S(2)}, u32[]{:S(2)}) collective-permute-start(bf16[2,768,512]{2,1,0:T(8,128)(2,1)} %pack_experts.5), channel_id=1, source_target_pairs={{0,16},{16,0},{1,17},{17,1},{2,18},{18,2},{3,19},{19,3},{4,20},{20... | collective-permute-start | bytes 4718600 | tf_op jit(solution)/shard_map/ppermute | solution.py:34
  75.9 27.7 %collective-permute-start.5 = (bf16[256,3072]{1,0:T(8,128)(2,1)S(1)}, bf16[256,3072]{1,0:T(8,128)(2,1)}, u32[]{:S(2)}, u32[]{:S(2)}) collective-permute-start(bf16[256,3072]{1,0:T(8,128)(2,1)S(1)} %collective-permute-done.2.refs_8_.refs_12_.refs_10_.refs_16_.refs_5_.refs_13_), channel_id=1, source_target_pairs={{0,4},{4,0},{1,5},{5,1},{2,6},{6,2},{3,7},{7,3},{8,12},{12,8},{9,1... | collective-permute-start | bytes 4718600 | tf_op jit(solution)/shard_map/ppermute | solution.py:34
  98.4 33.2 %collective-permute-start.22 = (bf16[2,768,512]{2,1,0:T(8,128)(2,1)}, bf16[2,768,512]{2,1,0:T(8,128)(2,1)}, u32[]{:S(2)}, u32[]{:S(2)}) collective-permute-start(bf16[2,768,512]{2,1,0:T(8,128)(2,1)} %collective-permute-done.20.refs_14_.refs_17_), channel_id=1, source_target_pairs={{0,8},{8,0},{1,9},{9,1},{2,10},{10,2},{3,11},{11,3},{4,12},{12,4},... | collective-permute-start | bytes 4718600 | tf_op jit(solution)/shard_map/ppermute | solution.py:34
  114.6 39.2 %collective-permute-start.24 = (bf16[2,768,512]{2,1,0:T(8,128)(2,1)}, bf16[2,768,512]{2,1,0:T(8,128)(2,1)S(1)}, u32[]{:S(2)}, u32[]{:S(2)}) collective-permute-start(bf16[2,768,512]{2,1,0:T(8,128)(2,1)} %pack_experts.6), channel_id=1, source_target_pairs={{0,16},{16,0},{1,17},{17,1},{2,18},{18,2},{3,19},{19,3},{4,20},{20... | collective-permute-start | bytes 4718600 | tf_op jit(solution)/shard_map/ppermute | solution.py:34
  119.1 61.9 %collective-permute-start.28 = (bf16[2,768,512]{2,1,0:T(8,128)(2,1)}, bf16[2,768,512]{2,1,0:T(8,128)(2,1)}, u32[]{:S(2)}, u32[]{:S(2)}) collective-permute-start(bf16[2,768,512]{2,1,0:T(8,128)(2,1)} %pack_experts.7), channel_id=1, source_target_pairs={{0,16},{16,0},{1,17},{17,1},{2,18},{18,2},{3,19},{19,3},{4,20},{20... | collective-permute-start | bytes 4718600 | tf_op jit(solution)/shard_map/ppermute | solution.py:34
  119.6 65.6 %collective-permute-start.21 = (bf16[2,768,512]{2,1,0:T(8,128)(2,1)}, bf16[2,768,512]{2,1,0:T(8,128)(2,1)}, u32[]{:S(2)}, u32[]{:S(2)}) collective-permute-start(bf16[2,768,512]{2,1,0:T(8,128)(2,1)} %collective-permute-done.20.refs_14_.refs_17_), channel_id=1, source_target_pairs={{0,4},{4,0},{1,5},{5,1},{2,6},{6,2},{3,7},{7,3},{8,12},{12,8},{9,1... | collective-permute-start | bytes 4718600 | tf_op jit(solution)/shard_map/ppermute | solution.py:34
  131.6 66.9 %collective-permute-start.23 = (bf16[2,768,512]{2,1,0:T(8,128)(2,1)}, bf16[2,768,512]{2,1,0:T(8,128)(2,1)}, u32[]{:S(2)}, u32[]{:S(2)}) collective-permute-start(bf16[2,768,512]{2,1,0:T(8,128)(2,1)} %collective-permute-done.22.refs_16_.refs_19_), channel_id=1, source_target_pairs={{0,4},{4,0},{1,5},{5,1},{2,6},{6,2},{3,7},{7,3},{8,12},{12,8},{9,1... | collective-permute-start | bytes 4718600 | tf_op jit(solution)/shard_map/ppermute | solution.py:34
  149.4 37.3 %collective-permute-start.14 = (bf16[256,1024]{1,0:T(8,128)(2,1)}, bf16[256,1024]{1,0:T(8,128)(2,1)S(1)}, u32[]{:S(2)}, u32[]{:S(2)}) collective-permute-start(bf16[256,1024]{1,0:T(8,128)(2,1)} %get-tuple-element.131.refs_1_), channel_id=1, source_target_pairs={{0,1},{1,2},{2,3},{4,5},{5,6},{6,7},{8,9},{9,10},{10,11},{12,13},{... | collective-permute-start | bytes 1572872 | tf_op jit(solution)/shard_map/ppermute | solution.py:29
  153.8 37.2 %collective-permute-start.17 = (bf16[256,1024]{1,0:T(8,128)(2,1)}, bf16[256,1024]{1,0:T(8,128)(2,1)}, u32[]{:S(2)}, u32[]{:S(2)}) collective-permute-start(bf16[256,1024]{1,0:T(8,128)(2,1)} %get-tuple-element.131.refs_1_), channel_id=1, source_target_pairs={{1,0},{2,1},{3,2},{5,4},{6,5},{7,6},{9,8},{10,9},{11,10},{13,12},{... | collective-permute-start | bytes 1572872 | tf_op jit(solution)/shard_map/ppermute | solution.py:29
  181.0 38.0 %collective-permute-start.26 = (bf16[2,768,512]{2,1,0:T(8,128)(2,1)S(1)}, bf16[2,768,512]{2,1,0:T(8,128)(2,1)}, u32[]{:S(2)}, u32[]{:S(2)}) collective-permute-start(bf16[2,768,512]{2,1,0:T(8,128)(2,1)S(1)} %collective-permute-done.24.refs_18_.refs_21_), channel_id=1, source_target_pairs={{0,8},{8,0},{1,9},{9,1},{2,10},{10,2},{3,11},{11,3},{4,12},{12,4},... | collective-permute-start | bytes 4718600 | tf_op jit(solution)/shard_map/ppermute | solution.py:34
  197.7 26.9 %collective-permute-start.25 = (bf16[2,768,512]{2,1,0:T(8,128)(2,1)S(1)}, bf16[2,768,512]{2,1,0:T(8,128)(2,1)}, u32[]{:S(2)}, u32[]{:S(2)}) collective-permute-start(bf16[2,768,512]{2,1,0:T(8,128)(2,1)S(1)} %collective-permute-done.24.refs_18_.refs_21_), channel_id=1, source_target_pairs={{0,4},{4,0},{1,5},{5,1},{2,6},{6,2},{3,7},{7,3},{8,12},{12,8},{9,1... | collective-permute-start | bytes 4718600 | tf_op jit(solution)/shard_map/ppermute | solution.py:34
  198.4 69.1 %collective-permute-start.30 = (bf16[2,768,512]{2,1,0:T(8,128)(2,1)}, bf16[2,768,512]{2,1,0:T(8,128)(2,1)}, u32[]{:S(2)}, u32[]{:S(2)}) collective-permute-start(bf16[2,768,512]{2,1,0:T(8,128)(2,1)} %collective-permute-done.28.refs_22_.refs_25_), channel_id=1, source_target_pairs={{0,8},{8,0},{1,9},{9,1},{2,10},{10,2},{3,11},{11,3},{4,12},{12,4},... | collective-permute-start | bytes 4718600 | tf_op jit(solution)/shard_map/ppermute | solution.py:34
  217.5 48.6 %collective-permute-start.34 = (bf16[1,768,512]{2,1,0:T(8,128)(2,1)S(1)}, bf16[1,768,512]{2,1,0:T(8,128)(2,1)}, u32[]{:S(2)}, u32[]{:S(2)}) collective-permute-start(bf16[1,768,512]{2,1,0:T(8,128)(2,1)S(1)} %collective-permute-done.32.refs_26_.refs_29_), channel_id=1, source_target_pairs={{0,8},{8,0},{1,9},{9,1},{2,10},{10,2},{3,11},{11,3},{4,12},{12,4},... | collective-permute-start | bytes 2359304 | tf_op jit(solution)/shard_map/ppermute | solution.py:34
  219.0 51.2 %collective-permute-start.29 = (bf16[2,768,512]{2,1,0:T(8,128)(2,1)}, bf16[2,768,512]{2,1,0:T(8,128)(2,1)}, u32[]{:S(2)}, u32[]{:S(2)}) collective-permute-start(bf16[2,768,512]{2,1,0:T(8,128)(2,1)} %collective-permute-done.28.refs_22_.refs_25_), channel_id=1, source_target_pairs={{0,4},{4,0},{1,5},{5,1},{2,6},{6,2},{3,7},{7,3},{8,12},{12,8},{9,1... | collective-permute-start | bytes 4718600 | tf_op jit(solution)/shard_map/ppermute | solution.py:34
  224.6 45.0 %collective-permute-start.33 = (bf16[1,768,512]{2,1,0:T(8,128)(2,1)S(1)}, bf16[1,768,512]{2,1,0:T(8,128)(2,1)}, u32[]{:S(2)}, u32[]{:S(2)}) collective-permute-start(bf16[1,768,512]{2,1,0:T(8,128)(2,1)S(1)} %collective-permute-done.32.refs_26_.refs_29_), channel_id=1, source_target_pairs={{0,4},{4,0},{1,5},{5,1},{2,6},{6,2},{3,7},{7,3},{8,12},{12,8},{9,1... | collective-permute-start | bytes 2359304 | tf_op jit(solution)/shard_map/ppermute | solution.py:34
  236.2 44.4 %collective-permute-start.27 = (bf16[2,768,512]{2,1,0:T(8,128)(2,1)}, bf16[2,768,512]{2,1,0:T(8,128)(2,1)S(1)}, u32[]{:S(2)}, u32[]{:S(2)}) collective-permute-start(bf16[2,768,512]{2,1,0:T(8,128)(2,1)} %collective-permute-done.26.refs_20_.refs_23_), channel_id=1, source_target_pairs={{0,4},{4,0},{1,5},{5,1},{2,6},{6,2},{3,7},{7,3},{8,12},{12,8},{9,1... | collective-permute-start | bytes 4718600 | tf_op jit(solution)/shard_map/ppermute | solution.py:34
  306.1 229.8 %reduce-scatter.12.cloned.1.call-start = ((), (), s32[]{:S(2)}) async-start(), calls=%async_computation.10 | async-start | bytes 2621440 | tf_op jit(solution)/shard_map/reduce_scatter | solution.py:925
  491.4 22.6 %collective-permute-start.49 = (bf16[4,512,1024]{2,1,0:T(8,128)(2,1)}, bf16[4,512,1024]{2,1,0:T(8,128)(2,1)}, u32[]{:S(2)}, u32[]{:S(2)}) collective-permute-start(bf16[4,512,1024]{2,1,0:T(8,128)(2,1)} %get-tuple-element.160.refs_2_), channel_id=1, source_target_pairs={{0,4},{4,0},{1,5},{5,1},{2,6},{6,2},{3,7},{7,3},{8,12},{12,8},{9,1... | collective-permute-start | bytes 12582920 | tf_op jit(solution)/shard_map/ppermute | solution.py:34
  492.0 167.0 %reduce-scatter.14.cloned.1.call-start = ((), (), s32[]{:S(2)}) async-start(), calls=%async_computation.11 | async-start | bytes 9437184 | tf_op jit(solution)/shard_map/reduce_scatter | solution.py:1040
  535.9 158.0 %reduce-scatter.16.cloned.1.call-start = ((), (), s32[]{:S(2)}) async-start(), calls=%async_computation.12 | async-start | bytes 9437184 | tf_op jit(solution)/shard_map/reduce_scatter | solution.py:1040
  564.2 177.2 %reduce-scatter.18.cloned.1.call-start = ((), (), s32[]{:S(2)}) async-start(), calls=%async_computation.13 | async-start | bytes 4915200 | tf_op jit(solution)/shard_map/reduce_scatter | solution.py:1181
  609.6 242.0 %reduce-scatter.22.cloned.1.call-start = ((), (), s32[]{:S(2)}) async-start(), calls=%async_computation.15 | async-start | bytes 4718592 | tf_op jit(solution)/shard_map/reduce_scatter | solution.py:1040
  646.2 66.7 %collective-permute-start.67 = (bf16[4,512,1024]{2,1,0:T(8,128)(2,1)}, bf16[4,512,1024]{2,1,0:T(8,128)(2,1)}, u32[]{:S(2)}, u32[]{:S(2)}) collective-permute-start(bf16[4,512,1024]{2,1,0:T(8,128)(2,1)} %get-tuple-element.187.refs_1_), channel_id=1, source_target_pairs={{0,4},{4,0},{1,5},{5,1},{2,6},{6,2},{3,7},{7,3},{8,12},{12,8},{9,1... | collective-permute-start | bytes 12582920 | tf_op jit(solution)/shard_map/ppermute | solution.py:34
  685.7 55.7 %collective-permute-start.68 = (bf16[4,512,1024]{2,1,0:T(8,128)(2,1)}, bf16[4,512,1024]{2,1,0:T(8,128)(2,1)}, u32[]{:S(2)}, u32[]{:S(2)}) collective-permute-start(bf16[4,512,1024]{2,1,0:T(8,128)(2,1)} %get-tuple-element.188.refs_2_), channel_id=1, source_target_pairs={{0,4},{4,0},{1,5},{5,1},{2,6},{6,2},{3,7},{7,3},{8,12},{12,8},{9,1... | collective-permute-start | bytes 12582920 | tf_op jit(solution)/shard_map/ppermute | solution.py:34
  709.7 31.7 %collective-permute-start.70 = (bf16[8,256,512]{2,1,0:T(8,128)(2,1)}, bf16[8,256,512]{2,1,0:T(8,128)(2,1)}, u32[]{:S(2)}, u32[]{:S(2)}) collective-permute-start(bf16[8,256,512]{2,1,0:T(8,128)(2,1)} %get-tuple-element.190.refs_4_), channel_id=1, source_target_pairs={{0,4},{4,0},{1,5},{5,1},{2,6},{6,2},{3,7},{7,3},{8,12},{12,8},{9,1... | collective-permute-start | bytes 6291464 | tf_op jit(solution)/shard_map/ppermute | solution.py:34
  709.8 31.6 %collective-permute-start.71 = (bf16[8,256,512]{2,1,0:T(8,128)(2,1)}, bf16[8,256,512]{2,1,0:T(8,128)(2,1)}, u32[]{:S(2)}, u32[]{:S(2)}) collective-permute-start(bf16[8,256,512]{2,1,0:T(8,128)(2,1)} %get-tuple-element.191.refs_5_), channel_id=1, source_target_pairs={{0,4},{4,0},{1,5},{5,1},{2,6},{6,2},{3,7},{7,3},{8,12},{12,8},{9,1... | collective-permute-start | bytes 6291464 | tf_op jit(solution)/shard_map/ppermute | solution.py:34
  712.9 33.9 %collective-permute-start.62 = (bf16[256,1024]{1,0:T(8,128)(2,1)}, bf16[256,1024]{1,0:T(8,128)(2,1)S(1)}, u32[]{:S(2)}, u32[]{:S(2)}) collective-permute-start(bf16[256,1024]{1,0:T(8,128)(2,1)} %get-tuple-element.342), channel_id=1, source_target_pairs={{0,1},{1,2},{4,5},{5,6},{8,9},{9,10},{12,13},{13,14},{16,17},{17,1... | collective-permute-start | bytes 1572872 | tf_op jit(solution)/shard_map/ppermute | solution.py:29
  717.3 29.5 %collective-permute-start.65 = (bf16[256,1024]{1,0:T(8,128)(2,1)}, bf16[256,1024]{1,0:T(8,128)(2,1)S(1)}, u32[]{:S(2)}, u32[]{:S(2)}) collective-permute-start(bf16[256,1024]{1,0:T(8,128)(2,1)} %get-tuple-element.343), channel_id=1, source_target_pairs={{2,1},{3,2},{6,5},{7,6},{10,9},{11,10},{14,13},{15,14},{18,17},{19... | collective-permute-start | bytes 1572872 | tf_op jit(solution)/shard_map/ppermute | solution.py:29
  753.7 97.8 %reduce-scatter.20.cloned.1.call-start = ((), (), s32[]{:S(2)}) async-start(), calls=%async_computation.14 | async-start | bytes 4718592 | tf_op jit(solution)/shard_map/reduce_scatter | solution.py:1040
  754.4 173.7 %reduce-scatter.26.cloned.1.call-start = ((), (), s32[]{:S(2)}) async-start(), calls=%async_computation.17 | async-start | bytes 4718592 | tf_op jit(solution)/shard_map/reduce_scatter | solution.py:1040
  798.4 207.3 %reduce-scatter.24.cloned.1.call-start = ((), (), s32[]{:S(2)}) async-start(), calls=%async_computation.16 | async-start | bytes 4718592 | tf_op jit(solution)/shard_map/reduce_scatter | solution.py:1040
  843.0 66.5 %collective-permute-start.82 = (bf16[1,256,3200]{2,1,0:T(8,128)(2,1)}, bf16[1,256,3200]{2,1,0:T(8,128)(2,1)}, u32[]{:S(2)}, u32[]{:S(2)}) collective-permute-start(bf16[1,256,3200]{2,1,0:T(8,128)(2,1)} %constant_dynamic-slice_fusion), channel_id=1, source_target_pairs={{0,8},{8,0},{1,9},{9,1},{2,10},{10,2},{3,11},{11,3},{4,12},{12,4},... | collective-permute-start | bytes 4915208 | tf_op jit(solution)/shard_map/ppermute | solution.py:34
  856.0 55.4 %collective-permute-start.83 = (bf16[2,768,512]{2,1,0:T(8,128)(2,1)}, bf16[2,768,512]{2,1,0:T(8,128)(2,1)}, u32[]{:S(2)}, u32[]{:S(2)}) collective-permute-start(bf16[2,768,512]{2,1,0:T(8,128)(2,1)} %get-tuple-element.333), channel_id=1, source_target_pairs={{0,16},{16,0},{1,17},{17,1},{2,18},{18,2},{3,19},{19,3},{4,20},{20... | collective-permute-start | bytes 4718600 | tf_op jit(solution)/shard_map/ppermute | solution.py:34
  858.9 69.2 %collective-permute-start.84 = (bf16[2,768,512]{2,1,0:T(8,128)(2,1)}, bf16[2,768,512]{2,1,0:T(8,128)(2,1)}, u32[]{:S(2)}, u32[]{:S(2)}) collective-permute-start(bf16[2,768,512]{2,1,0:T(8,128)(2,1)} %get-tuple-element.332), channel_id=1, source_target_pairs={{0,16},{16,0},{1,17},{17,1},{2,18},{18,2},{3,19},{19,3},{4,20},{20... | collective-permute-start | bytes 4718600 | tf_op jit(solution)/shard_map/ppermute | solution.py:34
  861.4 89.7 %collective-permute-start.87 = (bf16[256,1024]{1,0:T(8,128)(2,1)}, bf16[256,1024]{1,0:T(8,128)(2,1)S(1)}, u32[]{:S(2)}, u32[]{:S(2)}) collective-permute-start(bf16[256,1024]{1,0:T(8,128)(2,1)} %broadcast_select_fusion.5), channel_id=1, source_target_pairs={{0,16},{16,0},{1,17},{17,1},{2,18},{18,2},{3,19},{19,3},{4,20},{20... | collective-permute-start | bytes 1572872 | tf_op jit(solution)/shard_map/ppermute | solution.py:34
  931.0 74.7 %collective-permute-start.95 = (bf16[2,768,512]{2,1,0:T(8,128)(2,1)}, bf16[2,768,512]{2,1,0:T(8,128)(2,1)}, u32[]{:S(2)}, u32[]{:S(2)}) collective-permute-start(bf16[2,768,512]{2,1,0:T(8,128)(2,1)} %broadcast_select_fusion.1), channel_id=1, source_target_pairs={{0,16},{16,0},{1,17},{17,1},{2,18},{18,2},{3,19},{19,3},{4,20},{20... | collective-permute-start | bytes 4718600 | tf_op jit(solution)/shard_map/ppermute | solution.py:34
  946.2 36.7 %collective-permute-start.91 = (bf16[64,6400]{1,0:T(8,128)(2,1)S(1)}, bf16[64,6400]{1,0:T(8,128)(2,1)S(1)}, u32[]{:S(2)}, u32[]{:S(2)}) collective-permute-start(bf16[64,6400]{1,0:T(8,128)(2,1)S(1)} %get-tuple-element.311), channel_id=1, source_target_pairs={{0,1},{4,5},{8,9},{12,13},{16,17},{20,21},{24,25},{28,29}} | collective-permute-start | bytes 2457608 | tf_op jit(solution)/shard_map/ppermute | solution.py:29
  951.1 26.7 %collective-permute-start.88 = (bf16[256,1024]{1,0:T(8,128)(2,1)S(1)}, bf16[256,1024]{1,0:T(8,128)(2,1)S(1)}, u32[]{:S(2)}, u32[]{:S(2)}) collective-permute-start(bf16[256,1024]{1,0:T(8,128)(2,1)S(1)} %get-tuple-element.218), channel_id=1, source_target_pairs={{0,1},{1,2},{2,3},{4,5},{5,6},{6,7},{8,9},{9,10},{10,11},{12,13},{... | collective-permute-start | bytes 1572872 | tf_op jit(solution)/shard_map/ppermute | solution.py:29
  954.8 26.2 %collective-permute-start.89 = (bf16[256,1024]{1,0:T(8,128)(2,1)S(1)}, bf16[256,1024]{1,0:T(8,128)(2,1)S(1)}, u32[]{:S(2)}, u32[]{:S(2)}) collective-permute-start(bf16[256,1024]{1,0:T(8,128)(2,1)S(1)} %get-tuple-element.219), channel_id=1, source_target_pairs={{1,0},{2,1},{3,2},{5,4},{6,5},{7,6},{9,8},{10,9},{11,10},{13,12},{... | collective-permute-start | bytes 1572872 | tf_op jit(solution)/shard_map/ppermute | solution.py:29
  956.4 26.5 %collective-permute-start.94 = (bf16[64,6400]{1,0:T(8,128)(2,1)S(1)}, bf16[64,6400]{1,0:T(8,128)(2,1)S(1)}, u32[]{:S(2)}, u32[]{:S(2)}) collective-permute-start(bf16[64,6400]{1,0:T(8,128)(2,1)S(1)} %fusion.1), channel_id=1, source_target_pairs={{2,1},{3,2},{6,5},{7,6},{10,9},{11,10},{14,13},{15,14},{18,17},{19... | collective-permute-start | bytes 2457608 | tf_op jit(solution)/shard_map/ppermute | solution.py:29
  982.3 26.1 %collective-permute-start.90 = (bf16[256,1024]{1,0:T(8,128)(2,1)}, bf16[256,1024]{1,0:T(8,128)(2,1)}, u32[]{:S(2)}, u32[]{:S(2)}) collective-permute-start(bf16[256,1024]{1,0:T(8,128)(2,1)} %get-tuple-element.306), channel_id=1, source_target_pairs={{0,16},{16,0},{1,17},{17,1},{2,18},{18,2},{3,19},{19,3},{4,20},{20... | collective-permute-start | bytes 1572872 | tf_op jit(solution)/shard_map/ppermute | solution.py:34
  984.5 34.0 %collective-permute-start.92 = (bf16[64,6400]{1,0:T(8,128)(2,1)}, bf16[64,6400]{1,0:T(8,128)(2,1)}, u32[]{:S(2)}, u32[]{:S(2)}) collective-permute-start(bf16[64,6400]{1,0:T(8,128)(2,1)} %get-tuple-element.309), channel_id=1, source_target_pairs={{0,1},{1,2},{4,5},{5,6},{8,9},{9,10},{12,13},{13,14},{16,17},{17,1... | collective-permute-start | bytes 2457608 | tf_op jit(solution)/shard_map/ppermute | solution.py:29
  1007.3 32.8 %collective-permute-start.99 = (bf16[2,768,512]{2,1,0:T(8,128)(2,1)S(1)}, bf16[2,768,512]{2,1,0:T(8,128)(2,1)S(1)}, u32[]{:S(2)}, u32[]{:S(2)}) collective-permute-start(bf16[2,768,512]{2,1,0:T(8,128)(2,1)S(1)} %broadcast_select_fusion), channel_id=1, source_target_pairs={{0,16},{16,0},{1,17},{17,1},{2,18},{18,2},{3,19},{19,3},{4,20},{20... | collective-permute-start | bytes 4718600 | tf_op jit(solution)/shard_map/ppermute | solution.py:34
  1019.8 27.7 %collective-permute-start.96 = (bf16[64,6400]{1,0:T(8,128)(2,1)S(1)}, bf16[64,6400]{1,0:T(8,128)(2,1)S(1)}, u32[]{:S(2)}, u32[]{:S(2)}) collective-permute-start(bf16[64,6400]{1,0:T(8,128)(2,1)S(1)} %fusion.2), channel_id=1, source_target_pairs={{0,1},{1,2},{2,3},{4,5},{5,6},{6,7},{8,9},{9,10},{10,11},{12,13},{... | collective-permute-start | bytes 2457608 | tf_op jit(solution)/shard_map/ppermute | solution.py:29
  1024.2 23.2 %collective-permute-start.97 = (bf16[64,6400]{1,0:T(8,128)(2,1)S(1)}, bf16[64,6400]{1,0:T(8,128)(2,1)S(1)}, u32[]{:S(2)}, u32[]{:S(2)}) collective-permute-start(bf16[64,6400]{1,0:T(8,128)(2,1)S(1)} %copy-done.57), channel_id=1, source_target_pairs={{1,0},{2,1},{3,2},{5,4},{6,5},{7,6},{9,8},{10,9},{11,10},{13,12},{... | collective-permute-start | bytes 2457608 | tf_op jit(solution)/shard_map/ppermute | solution.py:29
  (153 other events, 2026.9 us)
Sparse Core Ops, SparseCore 0:
  306.2 43.6 reduce-scatter.9
  492.1 43.7 reduce-scatter.11
  538.2 76.3 reduce-scatter.13
  616.8 77.0 reduce-scatter.15
  696.6 44.7 reduce-scatter.17
  753.8 43.3 reduce-scatter.21
  800.0 43.3 reduce-scatter.19
  845.7 71.0 reduce-scatter.25
  919.0 43.3 reduce-scatter.23
